TPU v7x, 32 devices: a whole 2x2x4 slice. The times are simulated.
32 devices in a mesh: dp: 8 (over z, x), chan: 4 (over y, core).
Axes of the slice: x: 2, y: 2, z: 4, core: 2. Of those that a mesh axis runs over, the one named last changes fastest.
Arguments:
- input_a: bfloat16 [256, 25088], P('dp'), may hold values from -24 to 24, as said below
- input_b: bfloat16 [256, 9216], P('dp'), may hold values from -24 to 24, as said below
- boxes_a: int32 [128, 4], P('dp'), may hold values from 0 to 7, as said below
- boxes_b: int32 [256, 4], P('dp'), may hold values from 0 to 3, as said below
- weight_first: bfloat16 [9, 256, 512], P(None, None, 'chan'), may hold values from -0.125 to 0.125
- weight_second: bfloat16 [9, 512, 512], P(None, None, 'chan'), may hold values from -0.09375 to 0.09375
- weight_short: bfloat16 [256, 512], P(None, 'chan'), may hold values from -0.375 to 0.375
- gain_first: float32 [512], P('chan'), may hold values from 0.5 to 1.5
- shift_first: float32 [512], P('chan'), may hold values from -0.5 to 0.5
- gain_second: float32 [512], P('chan'), may hold values from 0.5 to 1.5
- shift_second: float32 [512], P('chan'), may hold values from -0.5 to 0.5
- gain_short: float32 [512], P('chan'), may hold values from 0.5 to 1.5
- shift_short: float32 [512], P('chan'), may hold values from -0.5 to 0.5
- upstream_a: bfloat16 [512, 6272], P('chan', 'dp'), may hold values from -6 to 6
- upstream_b: bfloat16 [512, 2304], P('chan', 'dp'), may hold values from -6 to 6
Outputs:
- out_a: bfloat16 [512, 6272], P('chan', 'dp')
- out_b: bfloat16 [512, 2304], P('chan', 'dp')
- grad_input_a: bfloat16 [256, 8, 4, 784], P('dp', None, 'chan')
- grad_input_b: bfloat16 [256, 8, 4, 288], P('dp', None, 'chan')
- grad_first: float32 [9, 256, 512], P(None, 'dp', 'chan')
- grad_second: float32 [9, 512, 512], P(None, 'dp', 'chan')
- grad_short: float32 [256, 512], P('dp', 'chan')
- grad_gain_first: float32 [512], P('chan')
- grad_shift_first: float32 [512], P('chan')
- grad_gain_second: float32 [512], P('chan')
- grad_shift_second: float32 [512], P('chan')
- grad_gain_short: float32 [512], P('chan')
- grad_shift_short: float32 [512], P('chan')
Inputs may be any that keep to these rules, and one draw needn't show every extreme that they name: `input_a`: entries of order one. `input_b`: entries of order one. `boxes_a`: each row is (first row, first column, height, width) of a box inside the output grid of side 14/2, height and width at least 1. `boxes_b`: each row is (first row, first column, height, width) of a box inside the output grid of side 6/2, height and width at least 1.
All inputs are finite; a program needn't handle non-finite values.
Results may differ from a plain program's by a relative error of at most 0.017.
Values may be sent and summed in bfloat16 or wider, within the bound.
A program may use at most 320 MiB of HBM per device.

v0:
```python
import jax
import jax.numpy as jnp
from jax import lax
from jax.sharding import PartitionSpec as P

SA = 14
SB = 6


epsilon = 1e-05


def box_mask(box_rows, extent):
    positions = jnp.arange(extent, dtype=jnp.int32)[None, :]
    row_inside = (positions >= box_rows[:, 0:1]) & (positions < box_rows[:, 0:1] + box_rows[:, 2:3])
    col_inside = (positions >= box_rows[:, 1:2]) & (positions < box_rows[:, 1:2] + box_rows[:, 3:4])
    return (row_inside[:, :, None] & col_inside[:, None, :]).astype(jnp.float32)


def taps_strided(feature, image_count, extent):
    channels = feature.shape[0]
    output_side = extent // 2
    padded = jnp.pad(
        feature.reshape(channels, image_count, extent, extent), ((0, 0), (0, 0), (1, 1), (1, 1))
    )
    pieces = [
        padded[:, :, tap_row : tap_row + extent : 2, tap_col : tap_col + extent : 2]
        for tap_row in range(3)
        for tap_col in range(3)
    ]
    return jnp.stack(pieces, axis=0).reshape(9 * channels, image_count * output_side * output_side)


def taps_plain(feature, image_count, extent):
    channels = feature.shape[0]
    padded = jnp.pad(
        feature.reshape(channels, image_count, extent, extent), ((0, 0), (0, 0), (1, 1), (1, 1))
    )
    pieces = [
        padded[:, :, tap_row : tap_row + extent, tap_col : tap_col + extent]
        for tap_row in range(3)
        for tap_col in range(3)
    ]
    return jnp.stack(pieces, axis=0).reshape(9 * channels, image_count * extent * extent)


def untaps_plain(columns, channels, image_count, extent):
    pieces = columns.reshape(9, channels, image_count, extent, extent)
    running = jnp.zeros((channels, image_count, extent + 2, extent + 2), jnp.float32)
    for tap_row in range(3):
        for tap_col in range(3):
            running = running + jnp.pad(
                pieces[3 * tap_row + tap_col],
                ((0, 0), (0, 0), (tap_row, 2 - tap_row), (tap_col, 2 - tap_col)),
            )
    return running[:, :, 1:-1, 1:-1].reshape(channels, image_count * extent * extent)


def untaps_strided(columns, shortcut, channels, image_count, extent):
    output_side = extent // 2
    pieces = columns.reshape(9, channels, image_count, output_side, output_side)
    parity_sums = {}
    for tap_row in range(3):
        for tap_col in range(3):
            block_row = tap_row // 2
            block_col = tap_col // 2
            placed = jnp.pad(
                pieces[3 * tap_row + tap_col],
                ((0, 0), (0, 0), (block_row, 1 - block_row), (block_col, 1 - block_col)),
            )
            parity = (tap_row % 2, tap_col % 2)
            parity_sums[parity] = (
                placed if parity not in parity_sums else parity_sums[parity] + placed
            )
    direct = jnp.pad(
        shortcut.reshape(channels, image_count, output_side, output_side),
        ((0, 0), (0, 0), (0, 1), (0, 1)),
    )
    parity_sums[1, 1] = parity_sums[1, 1] + direct
    rows_even = jnp.stack([parity_sums[0, 0], parity_sums[0, 1]], axis=-1)
    rows_odd = jnp.stack([parity_sums[1, 0], parity_sums[1, 1]], axis=-1)
    padded = jnp.stack([rows_even, rows_odd], axis=3).reshape(
        channels, image_count, extent + 2, extent + 2
    )
    return padded[:, :, 1:-1, 1:-1].reshape(channels, image_count * extent * extent)


def contract_first(weights, columns):
    return lax.dot_general(
        weights, columns, (((0,), (0,)), ((), ())), preferred_element_type=jnp.float32
    )


def weight_product(columns, gradient):
    return lax.dot_general(
        columns, gradient, (((1,), (1,)), ((), ())), preferred_element_type=jnp.float32
    )


def swish_slope(values):
    logistic = jax.nn.sigmoid(values)
    return logistic * (1.0 + values * (1.0 - logistic))


def moments(values, valid_list):
    running = 0.0
    squares = 0.0
    for tensor, valid in zip(values, valid_list):
        widened = tensor.astype(jnp.float32)
        running = running + jnp.sum(widened * valid, axis=1)
        squares = squares + jnp.sum(widened * widened * valid, axis=1)
    return (running, squares)


def standardize(values, running, squares, population):
    mean_value = running / population
    variance = squares / population - mean_value * mean_value
    scaling = lax.rsqrt(variance + epsilon)
    return (
        [
            (tensor.astype(jnp.float32) - mean_value[:, None]) * scaling[:, None]
            for tensor in values
        ],
        scaling,
    )


def norm_back(gradient, normed, valid, scaling, gain_values, shift_sum, gain_sum, population):
    return (gain_values * scaling)[:, None] * (
        gradient - valid * (shift_sum[:, None] + normed * gain_sum[:, None]) / population
    )


def body(
    input_a,
    input_b,
    boxes_a,
    boxes_b,
    weight_first,
    weight_second,
    weight_short,
    gain_first,
    shift_first,
    gain_second,
    shift_second,
    gain_short,
    shift_short,
    upstream_a,
    upstream_b,
):
    image_groups = lax.axis_size("dp")
    in_local = input_a.shape[0]
    chan_in = weight_first.shape[1]
    chan_part = weight_first.shape[2]
    chan_full = weight_second.shape[1]
    image_counts = (boxes_a.shape[0], boxes_b.shape[0])
    extents = (SA, SB)
    whole_a, whole_b = (
        lax.all_to_all(
            input_a.reshape(in_local, image_groups, -1),
            "dp",
            split_axis=1,
            concat_axis=0,
            tiled=True,
        ),
        lax.all_to_all(
            input_b.reshape(in_local, image_groups, -1),
            "dp",
            split_axis=1,
            concat_axis=0,
            tiled=True,
        ),
    )
    features = (whole_a.reshape(chan_in, -1), whole_b.reshape(chan_in, -1))
    valid_list = (
        box_mask(boxes_a, SA // 2).reshape(1, -1),
        box_mask(boxes_b, SB // 2).reshape(1, -1),
    )
    first_mat = weight_first.reshape(9 * chan_in, chan_part)
    second_mat = weight_second.reshape(9 * chan_full, chan_part)
    first_cols = []
    sampled = []
    first_z = []
    short_z = []
    for feature, image_count, extent in zip(features, image_counts, extents):
        columns = taps_strided(feature, image_count, extent)
        picked = feature.reshape(chan_in, image_count, extent, extent)[:, :, ::2, ::2].reshape(
            chan_in, -1
        )
        first_cols.append(columns)
        sampled.append(picked)
        first_z.append(contract_first(first_mat, columns).astype(jnp.bfloat16))
        short_z.append(contract_first(weight_short, picked).astype(jnp.bfloat16))
    sum_first, square_first = moments(first_z, valid_list)
    sum_short, square_short = moments(short_z, valid_list)
    population = jnp.sum(valid_list[0]) + jnp.sum(valid_list[1])
    sum_first, square_first, sum_short, square_short, population = lax.psum(
        (sum_first, square_first, sum_short, square_short, population), "dp"
    )
    normed_first, scaling_first = standardize(first_z, sum_first, square_first, population)
    normed_short, scaling_short = standardize(short_z, sum_short, square_short, population)
    before_first = [normed * gain_first[:, None] + shift_first[:, None] for normed in normed_first]
    outgoing_a = (jax.nn.silu(before_first[0]) * valid_list[0]).astype(jnp.bfloat16)
    outgoing_b = (jax.nn.silu(before_first[1]) * valid_list[1]).astype(jnp.bfloat16)
    gathered_a, gathered_b = (
        lax.all_gather(outgoing_a, "chan", axis=0, tiled=True),
        lax.all_gather(outgoing_b, "chan", axis=0, tiled=True),
    )
    second_cols = []
    second_z = []
    for gathered, image_count, extent in zip((gathered_a, gathered_b), image_counts, extents):
        columns = taps_plain(gathered, image_count, extent // 2)
        second_cols.append(columns)
        second_z.append(contract_first(second_mat, columns).astype(jnp.bfloat16))
    sum_second, square_second = moments(second_z, valid_list)
    sum_second, square_second = lax.psum((sum_second, square_second), "dp")
    normed_second, scaling_second = standardize(second_z, sum_second, square_second, population)
    summed_pre = [
        main_part * gain_second[:, None]
        + shift_second[:, None]
        + side_part * gain_short[:, None]
        + shift_short[:, None]
        for main_part, side_part in zip(normed_second, normed_short)
    ]
    outputs = [
        (jax.nn.silu(tensor) * valid).astype(jnp.bfloat16)
        for tensor, valid in zip(summed_pre, valid_list)
    ]
    tail_grads = [
        upstream.astype(jnp.float32) * valid * swish_slope(tensor)
        for upstream, valid, tensor in zip((upstream_a, upstream_b), valid_list, summed_pre)
    ]
    shift_tail = sum((jnp.sum(gradient, axis=1) for gradient in tail_grads))
    gain_tail = sum(
        (jnp.sum(gradient * normed, axis=1) for gradient, normed in zip(tail_grads, normed_second))
    )
    gain_side = sum(
        (jnp.sum(gradient * normed, axis=1) for gradient, normed in zip(tail_grads, normed_short))
    )
    shift_tail, gain_tail, gain_side = lax.psum((shift_tail, gain_tail, gain_side), "dp")
    grad_second_local = 0.0
    partial_hidden = []
    short_dz = []
    for index_group in range(2):
        valid = valid_list[index_group]
        dz_second = norm_back(
            tail_grads[index_group],
            normed_second[index_group],
            valid,
            scaling_second,
            gain_second,
            shift_tail,
            gain_tail,
            population,
        ).astype(jnp.bfloat16)
        dz_short = norm_back(
            tail_grads[index_group],
            normed_short[index_group],
            valid,
            scaling_short,
            gain_short,
            shift_tail,
            gain_side,
            population,
        ).astype(jnp.bfloat16)
        short_dz.append(dz_short)
        grad_second_local = grad_second_local + weight_product(second_cols[index_group], dz_second)
        back_cols = jnp.dot(second_mat, dz_second, preferred_element_type=jnp.float32)
        partial_hidden.append(
            untaps_plain(back_cols, chan_full, image_counts[index_group], extents[index_group] // 2)
        )
    hidden_a, hidden_b = (
        lax.psum_scatter(
            partial_hidden[0].astype(jnp.bfloat16), "chan", scatter_dimension=0, tiled=True
        ).astype(jnp.float32),
        lax.psum_scatter(
            partial_hidden[1].astype(jnp.bfloat16), "chan", scatter_dimension=0, tiled=True
        ).astype(jnp.float32),
    )
    head_grads = [
        hidden * valid * swish_slope(tensor)
        for hidden, valid, tensor in zip((hidden_a, hidden_b), valid_list, before_first)
    ]
    shift_head = sum((jnp.sum(gradient, axis=1) for gradient in head_grads))
    gain_head = sum(
        (jnp.sum(gradient * normed, axis=1) for gradient, normed in zip(head_grads, normed_first))
    )
    shift_head, gain_head = lax.psum((shift_head, gain_head), "dp")
    grad_first_local = 0.0
    grad_short_local = 0.0
    partial_inputs = []
    for index_group in range(2):
        valid = valid_list[index_group]
        dz_first = norm_back(
            head_grads[index_group],
            normed_first[index_group],
            valid,
            scaling_first,
            gain_first,
            shift_head,
            gain_head,
            population,
        ).astype(jnp.bfloat16)
        grad_first_local = grad_first_local + weight_product(first_cols[index_group], dz_first)
        grad_short_local = grad_short_local + weight_product(
            sampled[index_group], short_dz[index_group]
        )
        back_cols = jnp.dot(first_mat, dz_first, preferred_element_type=jnp.float32)
        back_short = jnp.dot(
            weight_short, short_dz[index_group], preferred_element_type=jnp.float32
        )
        flat_input = untaps_strided(
            back_cols, back_short, chan_in, image_counts[index_group], extents[index_group]
        )
        partial_inputs.append(flat_input.reshape(chan_in, 1, lax.axis_size("chan"), -1))
    arrived_a, arrived_b = (
        lax.all_to_all(
            partial_inputs[0].astype(jnp.bfloat16), "dp", split_axis=0, concat_axis=1, tiled=True
        ).astype(jnp.float32),
        lax.all_to_all(
            partial_inputs[1].astype(jnp.bfloat16), "dp", split_axis=0, concat_axis=1, tiled=True
        ).astype(jnp.float32),
    )
    summed_a, summed_b = (
        lax.psum_scatter(
            arrived_a.astype(jnp.bfloat16), "chan", scatter_dimension=2, tiled=True
        ).astype(jnp.float32),
        lax.psum_scatter(
            arrived_b.astype(jnp.bfloat16), "chan", scatter_dimension=2, tiled=True
        ).astype(jnp.float32),
    )
    grad_input_a = summed_a.astype(jnp.bfloat16)
    grad_input_b = summed_b.astype(jnp.bfloat16)
    grad_first_local = grad_first_local.reshape(9, chan_in, chan_part)
    grad_second_local = grad_second_local.reshape(9, chan_full, chan_part)
    total_first, total_second, total_short = lax.psum(
        (grad_first_local, grad_second_local, grad_short_local), "dp"
    )
    position = lax.axis_index("dp")
    rows_first = chan_in // image_groups
    rows_second = chan_full // image_groups
    grad_first = lax.dynamic_slice_in_dim(total_first, position * rows_first, rows_first, 1)
    grad_second = lax.dynamic_slice_in_dim(total_second, position * rows_second, rows_second, 1)
    grad_short = lax.dynamic_slice_in_dim(total_short, position * rows_first, rows_first, 0)
    return (
        outputs[0],
        outputs[1],
        grad_input_a,
        grad_input_b,
        grad_first,
        grad_second,
        grad_short,
        gain_head,
        shift_head,
        gain_tail,
        shift_tail,
        gain_side,
        shift_tail,
    )


def solution(mesh):
    placed = (
        P("dp", None),
        P("dp", None),
        P("dp", None),
        P("dp", None),
        P(None, None, "chan"),
        P(None, None, "chan"),
        P(None, "chan"),
        P("chan"),
        P("chan"),
        P("chan"),
        P("chan"),
        P("chan"),
        P("chan"),
        P("chan", "dp"),
        P("chan", "dp"),
    )
    return jax.shard_map(
        body,
        mesh=mesh,
        in_specs=placed,
        out_specs=(
            P("chan", "dp"),
            P("chan", "dp"),
            P("dp", None, "chan", None),
            P("dp", None, "chan", None),
            P(None, "dp", "chan"),
            P(None, "dp", "chan"),
            P("dp", "chan"),
            P("chan"),
            P("chan"),
            P("chan"),
            P("chan"),
            P("chan"),
            P("chan"),
        ),
        check_vma=False,
    )
```

profile of v0, /device:TPU:0, one launch (start us, length us, event | category | flops | bytes accessed | tf_op | source)
XLA Modules:
  0.0 1120.1 jit_solution(4593858028207861608)
XLA Ops:
  20.9 11.5 %all-to-all-done.1 = bf16[32,8,1152]{2,0,1:T(8,128)(2,1)S(1)} async-done(((bf16[32,8,1152]{2,0,1:T(8,128)(2,1)}), bf16[32,8,1152]{2,0,1:T(8,128)(2,1)S(1)}, u32[]{:S(2)}, u32[]{:S(2)}) %all-to-all-start.1) | async-done | bytes 589856 | tf_op jit(solution)/shard_map/all_to_all | solution.py:166
  45.9 41.9 %slice.347 = bf16[256,32,3,3]{0,3,2,1:T(4,128)(2,1)} slice(bf16[256,32,6,6]{0,3,2,1:T(8,128)(2,1)} %reshape_reshape.5), slice={[0:256:1], [0:32:1], [0:6:2], [0:6:2]} | slice | bytes 294912 | tf_op jit(solution)/shard_map/slice | solution.py:187
  102.7 28.5 %slice.318 = bf16[256,32,3,3]{0,3,2,1:T(4,128)(2,1)} slice(bf16[256,32,8,8]{0,3,2,1:T(8,128)(2,1)S(1)} %pad.157), slice={[0:256:1], [0:32:1], [0:6:2], [2:8:2]} | slice | bytes 294912 | tf_op jit(solution)/shard_map/slice | solution.py:27
  131.1 28.4 %slice.317 = bf16[256,32,3,3]{0,3,2,1:T(4,128)(2,1)} slice(bf16[256,32,8,8]{0,3,2,1:T(8,128)(2,1)S(1)} %pad.157), slice={[0:256:1], [0:32:1], [0:6:2], [1:7:2]} | slice | bytes 294912 | tf_op jit(solution)/shard_map/slice | solution.py:27
  159.6 28.4 %slice.316 = bf16[256,32,3,3]{0,3,2,1:T(4,128)(2,1)} slice(bf16[256,32,8,8]{0,3,2,1:T(8,128)(2,1)S(1)} %pad.157), slice={[0:256:1], [0:32:1], [0:6:2], [0:6:2]} | slice | bytes 294912 | tf_op jit(solution)/shard_map/slice | solution.py:27
  215.9 34.0 %slice.310 = bf16[256,16,7,7]{0,3,2,1:T(8,128)(2,1)} slice(bf16[256,16,16,16]{0,3,2,1:T(8,128)(2,1)S(1)} %pad.156), slice={[0:256:1], [0:16:1], [2:16:2], [2:16:2]} | slice | bytes 802816 | tf_op jit(solution)/shard_map/slice | solution.py:27
  249.9 33.9 %slice.309 = bf16[256,16,7,7]{0,3,2,1:T(8,128)(2,1)} slice(bf16[256,16,16,16]{0,3,2,1:T(8,128)(2,1)S(1)} %pad.156), slice={[0:256:1], [0:16:1], [2:16:2], [1:15:2]} | slice | bytes 802816 | tf_op jit(solution)/shard_map/slice | solution.py:27
  283.8 33.9 %slice.308 = bf16[256,16,7,7]{0,3,2,1:T(8,128)(2,1)} slice(bf16[256,16,16,16]{0,3,2,1:T(8,128)(2,1)S(1)} %pad.156), slice={[0:256:1], [0:16:1], [2:16:2], [0:14:2]} | slice | bytes 802816 | tf_op jit(solution)/shard_map/slice | solution.py:27
  317.7 34.0 %slice.307 = bf16[256,16,7,7]{0,3,2,1:T(8,128)(2,1)} slice(bf16[256,16,16,16]{0,3,2,1:T(8,128)(2,1)S(1)} %pad.156), slice={[0:256:1], [0:16:1], [1:15:2], [2:16:2]} | slice | bytes 802816 | tf_op jit(solution)/shard_map/slice | solution.py:27
  351.7 33.9 %slice.306 = bf16[256,16,7,7]{0,3,2,1:T(8,128)(2,1)} slice(bf16[256,16,16,16]{0,3,2,1:T(8,128)(2,1)S(1)} %pad.156), slice={[0:256:1], [0:16:1], [1:15:2], [1:15:2]} | slice | bytes 802816 | tf_op jit(solution)/shard_map/slice | solution.py:27
  385.6 33.9 %slice.305 = bf16[256,16,7,7]{0,3,2,1:T(8,128)(2,1)} slice(bf16[256,16,16,16]{0,3,2,1:T(8,128)(2,1)S(1)} %pad.156), slice={[0:256:1], [0:16:1], [1:15:2], [0:14:2]} | slice | bytes 802816 | tf_op jit(solution)/shard_map/slice | solution.py:27
  419.5 34.0 %slice.304 = bf16[256,16,7,7]{0,3,2,1:T(8,128)(2,1)} slice(bf16[256,16,16,16]{0,3,2,1:T(8,128)(2,1)S(1)} %pad.156), slice={[0:256:1], [0:16:1], [0:14:2], [2:16:2]} | slice | bytes 802816 | tf_op jit(solution)/shard_map/slice | solution.py:27
  453.4 33.9 %slice.303 = bf16[256,16,7,7]{0,3,2,1:T(8,128)(2,1)} slice(bf16[256,16,16,16]{0,3,2,1:T(8,128)(2,1)S(1)} %pad.156), slice={[0:256:1], [0:16:1], [0:14:2], [1:15:2]} | slice | bytes 802816 | tf_op jit(solution)/shard_map/slice | solution.py:27
  487.4 34.2 %slice.302 = bf16[256,16,7,7]{0,3,2,1:T(8,128)(2,1)} slice(bf16[256,16,16,16]{0,3,2,1:T(8,128)(2,1)S(1)} %pad.156), slice={[0:256:1], [0:16:1], [0:14:2], [0:14:2]} | slice | bytes 802816 | tf_op jit(solution)/shard_map/slice | solution.py:27
  534.8 41.1 %slice.346 = bf16[256,16,7,7]{0,3,2,1:T(8,128)(2,1)S(1)} slice(bf16[256,16,14,14]{0,3,2,1:T(8,128)(2,1)} %reshape_reshape.4), slice={[0:256:1], [0:16:1], [0:14:2], [0:14:2]} | slice | bytes 802816 | tf_op jit(solution)/shard_map/slice | solution.py:187
  575.9 22.2 %all-reduce.45 = (f32[]{:T(128)}, f32[128]{0:T(128)S(1)}, f32[128]{0:T(128)S(1)}) all-reduce(f32[]{:T(128)S(6)} %add.421, f32[128]{0:T(128)S(1)} %add.420, f32[128]{0:T(128)S(1)} %add.422), channel_id=1, replica_groups=mesh['dp'=8,'chan'=4] {'dp'}, use_global_device_ids=true, to_apply=%region_5.6 | all-reduce | flops 257 | bytes 2056 | tf_op jit(solution)/shard_map/psum | solution.py:197
  641.2 16.0 %copy.87 = bf16[98,8,9,512]{3,1,2,0:T(8,128)(2,1)} copy(bf16[98,8,9,512]{3,2,1,0:T(8,128)(2,1)} %bitcast.454) | data formatting | bytes 14450688
  665.2 17.3 %all-reduce.44 = (f32[128]{0:T(128)S(1)}, f32[128]{0:T(128)S(1)}, f32[128]{0:T(128)S(1)}, f32[128]{0:T(128)S(1)}) all-reduce(f32[128]{0:T(128)S(1)} %add.435, f32[128]{0:T(128)S(1)} %add.436, f32[128]{0:T(128)S(1)} %add.430, f32[128]{0:T(128)S(1)} %add.431), channel_id=1, replica_groups=mesh['dp'=8,'chan'=4] {'dp'}, use_global_device_ids=true, to_apply=%region_17.18 | all-reduce | flops 512 | bytes 4096 | tf_op jit(solution)/shard_map/psum | solution.py:197
  687.4 19.1 %all-reduce.43 = (f32[128]{0:T(128)S(1)}, f32[128]{0:T(128)S(1)}) all-reduce(f32[128]{0:T(128)S(1)} %add.450, f32[128]{0:T(128)S(1)} %add.452), channel_id=1, replica_groups=mesh['dp'=8,'chan'=4] {'dp'}, use_global_device_ids=true, to_apply=%region_23.24 | all-reduce | flops 256 | bytes 2048 | tf_op jit(solution)/shard_map/psum | solution.py:240
  790.6 12.5 %reduce-scatter.13.cloned.1.call-done = bf16[128,784]{1,0:T(8,128)(2,1)} async-done(((bf16[512,784]{1,0:T(8,128)(2,1)}), bf16[128,784]{1,0:T(8,128)(2,1)}) %reduce-scatter.13.cloned.1.call-update) | async-done | bytes 200720
  804.5 21.5 %all-reduce.42 = (f32[128]{0:T(128)S(1)}, f32[128]{0:T(128)S(1)}, f32[128]{0:T(128)S(1)}) all-reduce(f32[128]{0:T(128)S(1)} %add.483, f32[128]{0:T(128)S(1)} %add.476, f32[128]{0:T(128)S(1)} %add.474), channel_id=1, replica_groups=mesh['dp'=8,'chan'=4] {'dp'}, use_global_device_ids=true, to_apply=%region_37.38 | all-reduce | flops 384 | bytes 3072 | tf_op jit(solution)/shard_map/psum | solution.py:240
  905.4 80.2 %all_to_all.66 = bf16[256,1,4,784]{3,2,1,0:T(4,128)(2,1)S(1)} all-to-all(bf16[256,1,4,784]{3,2,1,0:T(4,128)(2,1)S(1)} %copy.71), channel_id=1, replica_groups=mesh['dp'=8,'chan'=4] {'dp'}, dimensions={0} | all-to-all | bytes 3211264 | tf_op jit(solution)/shard_map/all_to_all | solution.py:317
  988.9 90.8 %all-reduce.49.cloned.1.call-done = (f32[9,256,128]{2,1,0:T(8,128)}, f32[9,512,128]{2,1,0:T(8,128)}, f32[256,128]{0,1:T(8,128)}) async-done(((f32[9,256,128]{2,1,0:T(8,128)}, f32[9,512,128]{2,1,0:T(8,128)}, f32[256,128]{0,1:T(8,128)}), (f32[9,256,128]{2,1,0:T(8,128)}, f32[9,512,128]{2,1,0:T(8,128)}, f32[256,128]{0,1:T(8,128)})) %all-reduce.49.cloned.1.call-update) | async-done | bytes 3670032 | tf_op jit(solution)/shard_map/psum | solution.py:336
  1084.6 26.3 %reduce-scatter.9.cloned.1.call-done = bf16[32,8,1,784]{3,0,1,2:T(8,128)(2,1)} async-done(((bf16[32,8,4,784]{3,0,1,2:T(8,128)(2,1)}), bf16[32,8,1,784]{3,0,1,2:T(8,128)(2,1)}) %reduce-scatter.9.cloned.1.call-update) | async-done | bytes 401424 | tf_op jit(solution)/shard_map/reduce_scatter | solution.py:325
  (406 shorter events, 311.4 us)
Async XLA Ops:
  7.2 650.1 %copy-start = (bf16[9,512,128]{2,1,0:T(8,128)(2,1)S(1)}, bf16[9,512,128]{2,1,0:T(8,128)(2,1)}, u32[]{:S(2)}) copy-start(bf16[9,512,128]{2,1,0:T(8,128)(2,1)} %param.20) | copy-start | bytes 3538948
  9.2 23.1 %all-to-all-start.1 = ((bf16[32,8,1152]{2,0,1:T(8,128)(2,1)}), bf16[32,8,1152]{2,0,1:T(8,128)(2,1)S(1)}, u32[]{:S(2)}, u32[]{:S(2)}) async-start(bf16[32,8,1152]{2,0,1:T(8,128)(2,1)} %bitcast.449), calls=%async_computation.1 | async-start | bytes 1179648 | tf_op jit(solution)/shard_map/all_to_all | solution.py:166
  16.9 178.7 %copy-start.56 = (f32[288]{0:T(512)}, f32[288]{0:T(512)S(1)}, u32[]{:S(2)}) copy-start(f32[288]{0:T(512)S(1)} %reshape.431) | copy-start | bytes 3460
  32.4 164.8 %all-to-all-start = ((bf16[32,8,3136]{2,0,1:T(8,128)(2,1)}), bf16[32,8,3136]{2,0,1:T(8,128)(2,1)}, u32[]{:S(2)}, u32[]{:S(2)}) async-start(bf16[32,8,3136]{2,0,1:T(8,128)(2,1)} %copy.61), calls=%async_computation | async-start | bytes 3276800 | tf_op jit(solution)/shard_map/all_to_all | solution.py:159
  36.7 752.6 %reduce-scatter.15.cloned.1.call-start = ((), (), s32[]{:S(2)}) async-start(), calls=%async_computation.11 | async-start | bytes 491520
  197.1 402.1 %copy-start.41 = (f32[288,128]{1,0:T(8,128)}, f32[288,128]{1,0:T(8,128)S(1)}, u32[]{:S(2)}) copy-start(f32[288,128]{1,0:T(8,128)S(1)} %get-tuple-element.168) | copy-start | bytes 442372
  532.9 65.1 %copy-start.71 = (f32[128]{0:T(128)S(1)}, f32[128]{0:T(128)}, u32[]{:S(2)}) copy-start(f32[128]{0:T(128)} %param.22) | copy-start | bytes 1540
  532.9 66.3 %copy-start.49 = (bf16[256,288]{0,1:T(8,128)(2,1)S(1)}, bf16[256,288]{0,1:T(8,128)(2,1)}, u32[]{:S(2)}) copy-start(bf16[256,288]{0,1:T(8,128)(2,1)} %reshape.423) | copy-start | bytes 442372
  533.0 66.3 %copy-start.51 = (bf16[256,128]{1,0:T(8,128)(2,1)S(1)}, bf16[256,128]{1,0:T(8,128)(2,1)}, u32[]{:S(2)}) copy-start(bf16[256,128]{1,0:T(8,128)(2,1)} %param.21) | copy-start | bytes 196612
  533.0 66.3 %copy-start.57 = (f32[288]{0:T(512)S(1)}, f32[288]{0:T(512)}, u32[]{:S(2)}) copy-start(f32[288]{0:T(512)} %copy-done.56) | copy-start | bytes 3460
  533.0 66.3 %copy-start.79 = (f32[128]{0:T(128)S(1)}, f32[128]{0:T(128)}, u32[]{:S(2)}) copy-start(f32[128]{0:T(128)} %param.23) | copy-start | bytes 1540
  534.7 72.6 %copy-start.34 = (f32[784,128]{1,0:T(8,128)}, f32[784,128]{1,0:T(8,128)S(1)}, u32[]{:S(2)}) copy-start(f32[784,128]{1,0:T(8,128)S(1)} %get-tuple-element.167) | copy-start | bytes 1204228
  665.1 42.2 %copy-start.58 = (f32[288]{0:T(512)S(1)}, f32[288]{0:T(512)}, u32[]{:S(2)}) copy-start(f32[288]{0:T(512)} %copy-done.56) | copy-start | bytes 3460
  733.6 69.4 %reduce-scatter.13.cloned.1.call-start = ((), (), s32[]{:S(2)}) async-start(), calls=%async_computation.10 | async-start | bytes 1146880
  786.6 39.4 %copy-start.44 = (f32[128,288]{0,1:T(8,128)S(1)}, f32[128,288]{0,1:T(8,128)}, u32[]{:S(2)}) copy-start(f32[128,288]{0,1:T(8,128)} %copy-done.43) | copy-start | bytes 442372
  786.6 39.4 %copy-start.48 = (f32[128,288]{0,1:T(8,128)S(1)}, f32[128,288]{0,1:T(8,128)}, u32[]{:S(2)}) copy-start(f32[128,288]{0,1:T(8,128)} %get-tuple-element.170) | copy-start | bytes 442372
  786.6 39.4 %copy-start.65 = (f32[128]{0:T(128)S(1)}, f32[128]{0:T(128)}, u32[]{:S(2)}) copy-start(f32[128]{0:T(128)} %copy-done.64) | copy-start | bytes 1540
  786.6 39.4 %copy-start.67 = (f32[128]{0:T(128)S(1)}, f32[128]{0:T(128)}, u32[]{:S(2)}) copy-start(f32[128]{0:T(128)} %copy-done.66) | copy-start | bytes 1540
  851.1 20.2 %all-to-all-start.3 = ((bf16[256,1,4,288]{3,2,1,0:T(4,128)(2,1)}), bf16[256,1,4,288]{3,2,1,0:T(4,128)(2,1)S(1)}, u32[]{:S(2)}, u32[]{:S(2)}) async-start(bf16[256,1,4,288]{3,2,1,0:T(4,128)(2,1)} %copy.75), calls=%async_computation.4 | async-start | bytes 1572864 | tf_op jit(solution)/shard_map/all_to_all | solution.py:320
  854.6 132.6 %reduce-scatter.11.cloned.1.call-start = ((), (), s32[]{:S(2)}) async-start(), calls=%async_computation.9 | async-start | bytes 983040 | tf_op jit(solution)/shard_map/reduce_scatter | solution.py:328
  872.3 207.3 %all-reduce.49.cloned.1.call-start = ((), (), s32[]{:S(2)}) async-start(), calls=%async_computation.12 | async-start | bytes 7340032 | tf_op jit(solution)/shard_map/psum | solution.py:336
  880.7 230.2 %reduce-scatter.9.cloned.1.call-start = ((), (), s32[]{:S(2)}) async-start(), calls=%async_computation.8 | async-start | bytes 2293760 | tf_op jit(solution)/shard_map/reduce_scatter | solution.py:325
  985.7 127.7 %copy-start.1 = (bf16[9,512,128]{2,1,0:T(8,128)(2,1)S(1)}, bf16[9,512,128]{2,1,0:T(8,128)(2,1)}, u32[]{:S(2)}) copy-start(bf16[9,512,128]{2,1,0:T(8,128)(2,1)} %param.20) | copy-start | bytes 3538948
  987.2 125.7 %copy-start.70 = (f32[128]{0:T(128)S(1)}, f32[128]{0:T(128)}, u32[]{:S(2)}) copy-start(f32[128]{0:T(128)} %copy-done.68) | copy-start | bytes 1540
  (78 other events, 677.0 us)
Sparse Core Ops, SparseCore 0:
  733.7 17.9 reduce-scatter.14
  781.7 21.2 reduce-scatter.12
  872.4 21.3 reduce-scatter.10
  898.2 181.4 all-reduce.48
  1082.1 28.7 reduce-scatter.8
where the time goes:
time: 1140 us; the launch traced here: 1120 us
  local copies, waits for them, and re-layouts  695 us (61%)
  blocking collectives  176 us (15%)
  waiting for transfers between devices  151 us (13%)
  matrix products  36.3 us (3%)
  other arithmetic  29.2 us (3%)
  between operations  17.1 us (2%)
  starting transfers between devices  15.5 us (1%)
    slice x18, local copies, waits for them, and re-layouts, taps_strided(): padded[:, :, tap_row:tap_row + extent:2, tap_col:tap_col + extent:2]  405 us
    psum x1, waiting for transfers between devices, body(): lax.psum((grad_first_local, grad_second_local, grad_short_local), 'dp')  90.8 us
    slice x2, local copies, waits for them, and re-layouts, body(): feature.reshape(chan_in, image_count, extent, extent)[:, :, ::2, ::2]  83 us
    all_to_all x1, blocking collectives, body(): lax.all_to_all(partial_inputs[0].astype(jnp.bfloat16), 'dp', split_axis=0...  80.2 us
    unnamed x232, local copies, waits for them, and re-layouts  51 us
    psum x2, blocking collectives, body(): lax.psum((shift_tail, gain_tail, gain_side), 'dp')  40.6 us
    psum x2, blocking collectives, body(): lax.psum((sum_first, square_first, sum_short, square_short, population),...  39.5 us
    squeeze x18, local copies, waits for them, and re-layouts, untaps_plain(): pieces[3 * tap_row + tap_col]  37.8 us
  transfers between devices with their start and end apart: 8, of which 5 were waited for; matrix products, arithmetic and copies ran while one was open for 23% of the time, Pallas kernels for 0%

commit v1 on v0

--- a/solution.py
+++ b/solution.py
@@ -1,6 +1,9 @@
 import jax
 import jax.numpy as jnp
 from jax import lax
+import numpy as np
+from jax.experimental import pallas as pl
+from jax.experimental.pallas import tpu as pltpu
 from jax.sharding import PartitionSpec as P
 
 SA = 14
@@ -131,7 +134,7 @@
     )
 
 
-def body(
+def plain_body(
     input_a,
     input_b,
     boxes_a,
@@ -359,6 +362,679 @@
     )
 
 
+MESH = pl.DeviceIdType.MESH
+TAPS = tuple((a, b) for a in range(3) for b in range(3))
+PLANE_TAPS = (
+    ((1, 1),),
+    ((1, 0), (1, 2)),
+    ((0, 1), (2, 1)),
+    ((0, 0), (0, 2), (2, 0), (2, 2)),
+)
+ORDER = [tap for taps in PLANE_TAPS for tap in taps]
+LANES = 128
+
+
+def quarter_order(images, side, row_offset, lanes):
+    half = side // 2
+    matrix = np.zeros((half * half * 4 * images, lanes), np.float32)
+    for image in range(images):
+        for row in range(side):
+            for col in range(side):
+                plane = 2 * (row % 2) + col % 2
+                cell = (row // 2) * half + col // 2
+                target = (cell * 4 + plane) * images + image
+                matrix[target, row_offset + (image * side + row) * side + col] = 1.0
+    return matrix
+
+
+class Links:
+    def __init__(self, send_sems, recv_sems):
+        self.send_sems, self.recv_sems = send_sems, recv_sems
+        self.sends = self.slots = 0
+        self.open = []
+
+    def slot(self, count=1):
+        first = self.slots
+        self.slots += count
+        return first
+
+    def send(self, source, target, slot, where):
+        copy = pltpu.make_async_remote_copy(
+            source, target, self.send_sems.at[self.sends], self.recv_sems.at[slot],
+            device_id=where, device_id_type=MESH,
+        )
+        self.sends += 1
+        copy.start()
+        self.open.append(copy)
+
+    def arrived(self, target, slot, where):
+        pltpu.make_async_remote_copy(
+            target, target, self.send_sems.at[0], self.recv_sems.at[slot],
+            device_id=where, device_id_type=MESH,
+        ).wait_recv()
+
+    def drain(self):
+        for copy in self.open:
+            copy.wait_send()
+
+
+def mm(a, b, ca, cb):
+    return lax.dot_general(a, b, (((ca,), (cb,)), ((), ())), preferred_element_type=jnp.float32)
+
+
+def lanes_cat(parts):
+    return jnp.concatenate(parts, axis=1) if len(parts) > 1 else parts[0]
+
+
+def sigma(v):
+    return 0.5 * jnp.tanh(0.5 * v) + 0.5
+
+
+def make_fused(n_dp, in_local, images, sides, chan_in, chan_part, stop):
+    halves = tuple(side // 2 for side in sides)
+    sizes = tuple(h * h * n for h, n in zip(halves, images))
+    rows = sum(sizes)
+    quarter = tuple(n // 4 for n in images)
+    qlanes = tuple(q * side * side for q, side in zip(quarter, sides))
+    slab_lanes = -(-sum(qlanes) // LANES) * LANES
+    b_tile = qlanes[0] // LANES * LANES
+    b_skip = qlanes[0] - b_tile
+    chan_full = 4 * chan_part
+    out_rows = chan_full // n_dp
+    starts = (0, sizes[0])
+    chunks = [
+        (g, r, starts[g] + r * halves[g] * images[g], halves[g] * images[g])
+        for g in range(2)
+        for r in range(halves[g])
+    ]
+    win = [-(-(qlanes[g] + LANES - 1) // LANES) * LANES for g in range(2)]
+    win = [-(-qlanes[0] // LANES) * LANES, -(-qlanes[1] // LANES) * LANES]
+
+    def kernel(xa, xb, bxa, bxb, w1, w2, ws, g1, b1, g2, b2, gs, bs, ua, ub, pa, pb,
+               oa, ob, gr, gw1, gw2, vecs,
+               xs, xr, zg, zpa, zpb, valid, z1, zs, a1a, a1b, slots, up, outr, gv, dza, dzb, dzsr,
+               dd, hp, hr1, hs, hr2, gu, d1a, d1b, wg2, wr2, wx2, wz2, wg1, wr1, wx1, wz1,
+               gp, gr1, gsum, gr2, gt, ssem, rsem):
+        i, k = lax.axis_index("dp"), lax.axis_index("chan")
+        k1 = k + 1 - 2 * (k % 2)
+        k2 = (k + 2) % 4
+        k3 = (k1 + 2) % 4
+        ix = i % 2
+        mate = i + 1 - 2 * ix
+        net = Links(ssem, rsem)
+        zp, a1, dz, d1 = (zpa, zpb), (a1a, a1b), (dza, dzb), (d1a, d1b)
+        f32, bf16 = jnp.float32, jnp.bfloat16
+
+        def flat(value):
+            return value.reshape(-1, value.shape[-1])
+
+        barrier = pltpu.get_barrier_semaphore()
+        for d in range(1, n_dp):
+            pl.semaphore_signal(barrier, inc=1, device_id=((i + d) % n_dp, k), device_id_type=MESH)
+        pl.semaphore_signal(barrier, inc=1, device_id=(i, k1), device_id_type=MESH)
+        pl.semaphore_signal(barrier, inc=1, device_id=(i, k2), device_id_type=MESH)
+
+        lane = lax.broadcasted_iota(jnp.int32, (in_local, LANES), 1)
+        for d in range(n_dp):
+            j = (i + d) % n_dp
+            begin = 4 * qlanes[0] * j + qlanes[0] * k
+            tile = begin // LANES
+            part_a = xa[:, pl.ds(pl.multiple_of(tile * LANES, LANES), win[0])].astype(f32)
+            part_a = pltpu.roll(part_a, (win[0] - (begin - tile * LANES)) % win[0], 1)
+            begin = 4 * qlanes[1] * j + qlanes[1] * k
+            tile = begin // LANES
+            part_b = xb[:, pl.ds(pl.multiple_of(tile * LANES, LANES), win[1])].astype(f32)
+            part_b = jnp.concatenate([part_b, jnp.zeros((in_local, LANES), f32)], axis=1)
+            wide = win[1] + LANES
+            part_b = pltpu.roll(part_b, (wide + b_skip - (begin - tile * LANES)) % wide, 1)
+            seam = jnp.where(lane < b_skip, part_a[:, b_tile : b_tile + LANES], part_b[:, :LANES])
+            slab = jnp.concatenate(
+                [part_a[:, :b_tile], seam, part_b[:, LANES : slab_lanes - b_tile]], axis=1
+            ).astype(bf16)
+            if d == 0:
+                xr[i] = slab
+            else:
+                xs[j] = slab
+        pl.semaphore_wait(barrier, n_dp + 1)
+        base = net.slot(n_dp)
+        for d in range(1, n_dp):
+            j = (i + d) % n_dp
+            net.send(xs.at[j], xr.at[i], base + i, (j, k))
+
+        for buf in (zpa, zpb, a1a, a1b, dza, dzb, d1a, d1b):
+            side = buf.shape[1] if len(buf.shape) == 5 else buf.shape[0]
+            lead = (slice(None),) if len(buf.shape) == 5 else ()
+            for edge in (0, side - 1):
+                for index in (lead + (edge,), lead + (slice(None), edge)):
+                    region = buf.at[index]
+                    region[...] = jnp.zeros(region.shape, buf.dtype)
+        population = jnp.zeros((8, LANES), f32)
+        for g, box in enumerate((bxa, bxb)):
+            n, half = images[g], halves[g]
+            diag = lax.broadcasted_iota(jnp.int32, (n, n), 0) == lax.broadcasted_iota(jnp.int32, (n, n), 1)
+            cols = [
+                jnp.sum(jnp.where(diag, box[q : q + 1, :].astype(f32), 0.0), axis=1, keepdims=True)
+                for q in range(4)
+            ]
+            inside = [
+                [((p >= cols[q]) & (p < cols[q] + cols[q + 2])).astype(f32) for p in range(half)]
+                for q in range(2)
+            ]
+            for r in range(half):
+                for s in range(half):
+                    cell = jnp.broadcast_to(inside[0][r] * inside[1][s], (n, LANES))
+                    begin = starts[g] + (r * half + s) * n
+                    valid[begin : begin + n, :] = cell
+                    population = population + jnp.sum(cell.reshape(n // 8, 8, LANES), axis=0)
+        population = jnp.sum(population, axis=0, keepdims=True)
+        for g, source in enumerate((ua, ub)):
+            n, cells = images[g], halves[g] ** 2
+            gu[starts[g] : starts[g] + sizes[g], :] = source[...].astype(f32)
+            for cell in range(cells):
+                up[starts[g] + cell * n : starts[g] + (cell + 1) * n, :] = gu[
+                    pl.ds(starts[g] + cell, n, stride=cells), :
+                ]
+
+        for d in range(1, n_dp):
+            j = (i + d) % n_dp
+            net.arrived(xr.at[j], base + j, (j, k))
+        if stop == 0:
+            return finish(net, locals())
+        xall = jnp.concatenate([xr[q] for q in range(n_dp)], axis=0)
+        zg[k, : sizes[0], :] = mm(pa[...], xall[:, : pa.shape[1]], 1, 1).astype(bf16)
+        zg[k, sizes[0] :, :] = mm(pb[...], xall[:, b_tile:], 1, 1).astype(bf16)
+        slot = net.slot(4)
+        net.send(zg.at[k], zg.at[k], slot + k, (i, k2))
+        net.send(zg.at[k], zg.at[k], slot + k, (i, k1))
+        net.arrived(zg.at[k2], slot + k2, (i, k2))
+        net.send(zg.at[k2], zg.at[k2], slot + k2, (i, k1))
+        net.arrived(zg.at[k1], slot + k1, (i, k1))
+        net.arrived(zg.at[k3], slot + k3, (i, k1))
+        if stop == 1:
+            return finish(net, locals())
+
+        def planes_of(quarters, g):
+            step = quarter[g]
+            if step % 8 == 0:
+                return [
+                    jnp.concatenate([v[:, step * p : step * (p + 1)] for v in quarters], axis=1)
+                    for p in range(4)
+                ]
+            low = lax.broadcasted_iota(jnp.int32, (1, 8, 1), 1) < 4
+            halves_ = [[v[:, 8 * h : 8 * h + 8] for v in quarters] for h in range(2)]
+            turned = [[pltpu.roll(v, 4, 1) for v in side] for side in halves_]
+            result = []
+            for p in range(4):
+                h, odd = p // 2, p % 2
+                v, t = halves_[h], turned[h]
+                if odd == 0:
+                    parts = [jnp.where(low, v[0], t[1]), jnp.where(low, v[2], t[3])]
+                else:
+                    parts = [jnp.where(low, t[0], v[1]), jnp.where(low, t[2], v[3])]
+                result.append(jnp.concatenate(parts, axis=1))
+            return result
+
+        for g, r, begin, count in chunks:
+            quarters = [
+                zg[q, begin : begin + count, :].astype(f32).reshape(halves[g], images[g], chan_in)
+                for q in range(4)
+            ]
+            for p, value in enumerate(planes_of(quarters, g)):
+                zp[g][p, 1 + r, 1 : 1 + halves[g]] = value.astype(bf16)
+        if stop == 2:
+            return finish(net, locals())
+
+        def strided_patch(g, tap):
+            a, b = tap
+            p = 2 * (a % 2 == 0) + (b % 2 == 0)
+            r, s = 1 - (a == 0), 1 - (b == 0)
+            return flat(zp[g][p, r : r + halves[g], s : s + halves[g]])
+
+        for g in range(2):
+            span = slice(starts[g], starts[g] + sizes[g])
+            both = mm(strided_patch(g, (1, 1)), jnp.concatenate([w1[4], ws[...]], axis=1), 1, 0)
+            zs[span, :] = both[:, chan_part:]
+            acc = both[:, :chan_part]
+            for tap in TAPS:
+                if tap != (1, 1):
+                    acc = acc + mm(strided_patch(g, tap), w1[3 * tap[0] + tap[1]], 1, 0)
+            z1[span, :] = acc
+
+        def rowsum(value):
+            return jnp.sum(value.reshape(-1, 8, LANES), axis=0)
+
+        def message(sums):
+            parts = [jnp.sum(v, axis=0, keepdims=True) if v.shape[0] > 1 else v for v in sums]
+            parts.append(jnp.zeros((8 - len(parts), LANES), f32))
+            return jnp.concatenate(parts, axis=0)
+
+        def share(rnd, value):
+            slots[rnd, i] = value
+            first = net.slot(n_dp)
+            for d in range(1, n_dp):
+                j = (i + d) % n_dp
+                net.send(slots.at[rnd, i], slots.at[rnd, i], first + i, (j, k))
+            return first
+
+        def total(rnd, first):
+            for d in range(1, n_dp):
+                j = (i + d) % n_dp
+                net.arrived(slots.at[rnd, j], first + j, (j, k))
+            return jnp.sum(slots[rnd], axis=0)
+
+        acc = [jnp.zeros((8, LANES), f32)] * 4
+        for g, r, begin, count in chunks:
+            span = slice(begin, begin + count)
+            ok = valid[span, :]
+            u, w = z1[span, :], zs[span, :]
+            uv, wv = u * ok, w * ok
+            acc = [acc[0] + rowsum(uv), acc[1] + rowsum(uv * u), acc[2] + rowsum(wv), acc[3] + rowsum(wv * w)]
+        first = share(0, message(acc + [population]))
+        tot = total(0, first)
+        if stop == 3:
+            return finish(net, locals())
+        inv_pop = 1.0 / tot[4:5]
+        mean1, means = tot[0:1] * inv_pop, tot[2:3] * inv_pop
+        sc1 = lax.rsqrt(tot[1:2] * inv_pop - mean1 * mean1 + epsilon)
+        scs = lax.rsqrt(tot[3:4] * inv_pop - means * means + epsilon)
+        gain1, shift1 = g1[...], b1[...]
+        for g, r, begin, count in chunks:
+            span = slice(begin, begin + count)
+            hat = (z1[span, :] - mean1) * sc1
+            z1[span, :] = hat
+            v = hat * gain1 + shift1
+            act = (v * sigma(v) * valid[span, :]).astype(bf16)
+            a1[g][k, 1 + r, 1 : 1 + halves[g]] = act.reshape(halves[g], images[g], chan_part)
+
+        def inner(g, q):
+            return a1[g].at[q, 1 : 1 + halves[g], 1 : 1 + halves[g]]
+
+        slot = net.slot(8)
+        for where in (k2, k1):
+            for g in range(2):
+                net.send(inner(g, k), inner(g, k), slot + 4 * g + k, (i, where))
+        for g in range(2):
+            span = slice(starts[g], starts[g] + sizes[g])
+        for g in range(2):
+            net.arrived(inner(g, k2), slot + 4 * g + k2, (i, k2))
+            net.send(inner(g, k2), inner(g, k2), slot + 4 * g + k2, (i, k1))
+        for g in range(2):
+            net.arrived(inner(g, k1), slot + 4 * g + k1, (i, k1))
+            net.arrived(inner(g, k3), slot + 4 * g + k3, (i, k1))
+        if stop == 4:
+            return finish(net, locals())
+
+        def plain_patch(g, tap):
+            a, b = tap
+            return lanes_cat(
+                [flat(a1[g][q, a : a + halves[g], b : b + halves[g]]) for q in range(4)]
+            )
+
+        z2 = hp
+        for g in range(2):
+            acc = None
+            for tap in TAPS:
+                part = mm(plain_patch(g, tap), w2[3 * tap[0] + tap[1]], 1, 0)
+                acc = part if acc is None else acc + part
+            gv[starts[g] : starts[g] + sizes[g], :] = acc
+        acc = [jnp.zeros((8, LANES), f32)] * 2
+        for g, r, begin, count in chunks:
+            span = slice(begin, begin + count)
+            u = gv[span, :]
+            uv = u * valid[span, :]
+            acc = [acc[0] + rowsum(uv), acc[1] + rowsum(uv * u)]
+        first = share(1, message(acc))
+        for g, r, begin, count in chunks:
+            span = slice(begin, begin + count)
+            zs[span, :] = (zs[span, :] - means) * scs
+        tot = total(1, first)
+        if stop == 5:
+            return finish(net, locals())
+        mean2 = tot[0:1] * inv_pop
+        sc2 = lax.rsqrt(tot[1:2] * inv_pop - mean2 * mean2 + epsilon)
+        gain2, gains = g2[...], gs[...]
+        shifts = b2[...] + bs[...]
+        acc = [jnp.zeros((8, LANES), f32)] * 3
+        for g, r, begin, count in chunks:
+            span = slice(begin, begin + count)
+            ok = valid[span, :]
+            hat2 = (gv[span, :] - mean2) * sc2
+            hats = zs[span, :]
+            v = hat2 * gain2 + hats * gains + shifts
+            sig = sigma(v)
+            outr[span, :] = v * sig * ok
+            grad = up[span, :] * ok * (sig * (1.0 + v * (1.0 - sig)))
+            up[span, :] = grad
+            gv[span, :] = hat2
+            acc = [acc[0] + rowsum(grad), acc[1] + rowsum(grad * hat2), acc[2] + rowsum(grad * hats)]
+        first = share(2, message(acc))
+        for g, target in enumerate((oa, ob)):
+            n, cells = images[g], halves[g] ** 2
+            for cell in range(cells):
+                gu[pl.ds(starts[g] + cell, n, stride=cells), :] = outr[
+                    starts[g] + cell * n : starts[g] + (cell + 1) * n, :
+                ]
+            target[...] = gu[starts[g] : starts[g] + sizes[g], :].astype(bf16)
+        tot = total(2, first)
+        sum_tail, sum_gain2, sum_gains = tot[0:1], tot[1:2], tot[2:3]
+        if stop == 6:
+            return finish(net, locals())
+
+        k2g, ksg = gain2 * sc2, gains * scs
+        db, dg2, dgs = sum_tail * inv_pop, sum_gain2 * inv_pop, sum_gains * inv_pop
+        for g, r, begin, count in chunks:
+            span = slice(begin, begin + count)
+            ok = valid[span, :]
+            grad = up[span, :]
+            shape = (halves[g], images[g], chan_part)
+            value = k2g * (grad - ok * (db + gv[span, :] * dg2))
+            dz[g][1 + r, 1 : 1 + halves[g]] = value.astype(bf16).reshape(shape)
+            value = ksg * (grad - ok * (db + zs[span, :] * dgs))
+            dzsr[span, :] = value.astype(bf16)
+        for g in range(2):
+            for t, (a, b) in enumerate(TAPS):
+                dd[starts[g] : starts[g] + sizes[g], t * LANES : (t + 1) * LANES] = flat(
+                    dz[g][2 - a : 2 - a + halves[g], 2 - b : 2 - b + halves[g]]
+                )
+
+        def back_second(q):
+            weights = lanes_cat(
+                [w2[t, pl.ds(pl.multiple_of(q * chan_part, LANES), chan_part), :] for t in range(9)]
+            )
+            hp[q] = mm(dd[...], weights, 1, 1).astype(bf16)
+
+        slot = net.slot(3)
+        back_second(k3)
+        net.send(hp.at[k3], hr1.at[1], slot + 1, (i, k1))
+        back_second(k2)
+        net.arrived(hr1.at[1], slot + 1, (i, k1))
+        hs[...] = (hp[k2].astype(f32) + hr1[1].astype(f32)).astype(bf16)
+        net.send(hs, hr2, slot + 2, (i, k2))
+        back_second(k1)
+        net.send(hp.at[k1], hr1.at[0], slot, (i, k1))
+        back_second(k)
+
+        n_z = n_dp // 2
+        acts = [
+            lanes_cat([flat(a1[g][q, 1 : 1 + halves[g], 1 : 1 + halves[g]]) for q in range(4)])
+            for g in range(2)
+        ]
+        grad_w2 = mm(acts[0], dd[: sizes[0], :], 0, 0) + mm(acts[1], dd[sizes[0] :, :], 0, 0)
+        wg2[...] = grad_w2.astype(bf16).reshape(n_dp, out_rows, 9 * LANES)
+
+        def halve(part, got, slot):
+            for z in range(n_z):
+                net.send(part.at[2 * z + 1 - ix], got.at[z], slot + z, (mate, k))
+
+        def spread(part, got, both, last, slot, slot_z):
+            for z in range(n_z):
+                net.arrived(got.at[z], slot + z, (mate, k))
+                both[z] = (part[2 * z + ix].astype(f32) + got[z].astype(f32)).astype(bf16)
+            iz = i // 2
+            for d in range(1, n_z):
+                z = (iz + d) % n_z
+                net.send(both.at[z], last.at[iz], slot_z + iz, (2 * z + ix, k))
+
+        def collect(both, last, slot_z):
+            iz = i // 2
+            value = both[iz].astype(f32)
+            for d in range(1, n_z):
+                z = (iz + d) % n_z
+                net.arrived(last.at[z], slot_z + z, (2 * z + ix, k))
+                value = value + last[z].astype(f32)
+            return value
+
+        slot_w2 = net.slot(2 * n_z)
+        halve(wg2, wr2, slot_w2)
+        net.arrived(hr1.at[0], slot, (i, k1))
+        net.arrived(hr2, slot + 2, (i, k2))
+        if stop == 7:
+            spread(wg2, wr2, wx2, wz2, slot_w2, slot_w2 + n_z)
+            collect(wx2, wz2, slot_w2 + n_z)
+            return finish(net, locals())
+        acc = [jnp.zeros((8, LANES), f32)] * 2
+        for g, r, begin, count in chunks:
+            span = slice(begin, begin + count)
+            hat = z1[span, :]
+            v = hat * gain1 + shift1
+            sig = sigma(v)
+            grad = hp[k, span, :].astype(f32) + hr1[0, span, :].astype(f32) + hr2[span, :].astype(f32)
+            grad = grad * valid[span, :] * (sig * (1.0 + v * (1.0 - sig)))
+            gu[span, :] = grad
+            acc = [acc[0] + rowsum(grad), acc[1] + rowsum(grad * hat)]
+        first = share(3, message(acc))
+        spread(wg2, wr2, wx2, wz2, slot_w2, slot_w2 + n_z)
+        tot = total(3, first)
+        sum_head, sum_gain1 = tot[0:1], tot[1:2]
+        if stop == 8:
+            collect(wx2, wz2, slot_w2 + n_z)
+            return finish(net, locals())
+        k1g = gain1 * sc1
+        db, dg1 = sum_head * inv_pop, sum_gain1 * inv_pop
+        for g, r, begin, count in chunks:
+            span = slice(begin, begin + count)
+            value = k1g * (gu[span, :] - valid[span, :] * (db + z1[span, :] * dg1))
+            d1[g][r, : halves[g]] = value.astype(bf16).reshape(halves[g], images[g], chan_part)
+
+        def back_patch(g, p):
+            parts = [
+                flat(d1[g][(a == 0) : (a == 0) + halves[g], (b == 0) : (b == 0) + halves[g]])
+                for a, b in PLANE_TAPS[p]
+            ]
+            if p == 0:
+                parts.append(dzsr[starts[g] : starts[g] + sizes[g], :])
+            return lanes_cat(parts)
+
+        for g in range(2):
+            planes = []
+            for p in range(4):
+                weights = [w1[3 * a + b] for a, b in PLANE_TAPS[p]]
+                if p == 0:
+                    weights.append(ws[...])
+                value = mm(back_patch(g, p), lanes_cat(weights), 1, 1)
+                planes.append(value.reshape(halves[g] ** 2, images[g], chan_in))
+            for q, value in enumerate(planes_of(planes, g)):
+                gp[q, starts[g] : starts[g] + sizes[g], :] = flat(value).astype(bf16)
+        slot = net.slot(3)
+        net.send(gp.at[k3], gr1.at[1], slot + 1, (i, k1))
+        net.send(gp.at[k1], gr1.at[0], slot, (i, k1))
+        net.arrived(gr1.at[1], slot + 1, (i, k1))
+        for begin in range(0, rows, 16):
+            span = slice(begin, begin + 16)
+            gsum[span, :] = (gp[k2, span, :].astype(f32) + gr1[1, span, :].astype(f32)).astype(bf16)
+        net.send(gsum, gr2, slot + 2, (i, k2))
+
+        blocks = []
+        for p in range(4):
+            value = 0.0
+            for g in range(2):
+                cells = flat(zp[g][p, 1 : 1 + halves[g], 1 : 1 + halves[g]])
+                value = value + mm(cells, back_patch(g, p), 0, 0)
+            blocks.append(value.astype(bf16))
+        wg1[...] = lanes_cat(blocks).reshape(n_dp, in_local, 10 * LANES)
+        slot_w1 = net.slot(2 * n_z)
+        halve(wg1, wr1, slot_w1)
+        spread(wg1, wr1, wx1, wz1, slot_w1, slot_w1 + n_z)
+        net.arrived(gr1.at[0], slot, (i, k1))
+        net.arrived(gr2, slot + 2, (i, k2))
+        if stop == 9:
+            collect(wx2, wz2, slot_w2 + n_z)
+            collect(wx1, wz1, slot_w1 + n_z)
+            return finish(net, locals())
+        for begin in range(0, rows, 16):
+            span = slice(begin, begin + 16)
+            gsum_ = gp[k, span, :].astype(f32) + gr1[0, span, :].astype(f32) + gr2[span, :].astype(f32)
+            gp[k, span, :] = gsum_.astype(bf16)
+        part_a = mm(gp[k, : sizes[0], :], pa[...], 0, 0)
+        part_b = mm(gp[k, sizes[0] :, :], pb[...], 0, 0)
+        lane = lax.broadcasted_iota(jnp.int32, (chan_in, LANES), 1)
+        seam = jnp.where(lane < b_skip, part_a[:, b_tile : b_tile + LANES], part_b[:, :LANES])
+        gt[...] = (
+            jnp.concatenate([part_a[:, :b_tile], seam, part_b[:, LANES:]], axis=1)
+            .astype(bf16)
+            .reshape(n_dp, in_local, slab_lanes)
+        )
+        slot = net.slot(n_dp)
+        for d in range(1, n_dp):
+            j = (i + d) % n_dp
+            net.send(gt.at[j], gr.at[i], slot + i, (j, k))
+        gr[i] = gt[i]
+        gw2[...] = collect(wx2, wz2, slot_w2 + n_z)
+        gw1[...] = collect(wx1, wz1, slot_w1 + n_z)
+        vecs[...] = message([sum_gain1, sum_head, sum_gain2, sum_tail, sum_gains])
+        for d in range(1, n_dp):
+            j = (i + d) % n_dp
+            net.arrived(gr.at[j], slot + j, (j, k))
+        net.drain()
+
+    def finish(net, env):
+        net.drain()
+
+    bf, f = jnp.bfloat16, jnp.float32
+    V = pltpu.VMEM
+    pads = [(h + 2, h + 2, n, chan_part) for h, n in zip(halves, images)]
+    scratch = [
+        V((n_dp, in_local, slab_lanes), bf),
+        V((n_dp, in_local, slab_lanes), bf),
+        V((4, rows, chan_in), bf),
+        V((4, halves[0] + 1, halves[0] + 1, images[0], chan_in), bf),
+        V((4, halves[1] + 1, halves[1] + 1, images[1], chan_in), bf),
+        V((rows, LANES), f),
+        V((rows, chan_part), f),
+        V((rows, chan_part), f),
+        V((4,) + pads[0], bf),
+        V((4,) + pads[1], bf),
+        V((4, n_dp, 8, LANES), f),
+        V((rows, chan_part), f),
+        V((rows, chan_part), f),
+        V((rows, chan_part), f),
+        V(pads[0], bf),
+        V(pads[1], bf),
+        V((rows, chan_part), bf),
+        V((rows, 9 * chan_part), bf),
+        V((4, rows, chan_part), bf),
+        V((2, rows, chan_part), bf),
+        V((rows, chan_part), bf),
+        V((rows, chan_part), bf),
+        V((rows, chan_part), f),
+        V((halves[0] + 1, halves[0] + 1, images[0], chan_part), bf),
+        V((halves[1] + 1, halves[1] + 1, images[1], chan_part), bf),
+        V((n_dp, out_rows, 9 * LANES), bf),
+        V((n_dp // 2, out_rows, 9 * LANES), bf),
+        V((n_dp // 2, out_rows, 9 * LANES), bf),
+        V((n_dp // 2, out_rows, 9 * LANES), bf),
+        V((n_dp, in_local, 10 * LANES), bf),
+        V((n_dp // 2, in_local, 10 * LANES), bf),
+        V((n_dp // 2, in_local, 10 * LANES), bf),
+        V((n_dp // 2, in_local, 10 * LANES), bf),
+        V((4, rows, chan_in), bf),
+        V((2, rows, chan_in), bf),
+        V((rows, chan_in), bf),
+        V((rows, chan_in), bf),
+        V((n_dp, in_local, slab_lanes), bf),
+        pltpu.SemaphoreType.DMA((96,)),
+        pltpu.SemaphoreType.DMA((96,)),
+    ]
+    outs = [
+        jax.ShapeDtypeStruct((sizes[0], chan_part), bf),
+        jax.ShapeDtypeStruct((sizes[1], chan_part), bf),
+        jax.ShapeDtypeStruct((n_dp, in_local, slab_lanes), bf),
+        jax.ShapeDtypeStruct((in_local, 10 * LANES), f),
+        jax.ShapeDtypeStruct((out_rows, 9 * LANES), f),
+        jax.ShapeDtypeStruct((8, LANES), f),
+    ]
+    vmem = pl.BlockSpec(memory_space=pltpu.VMEM)
+    main = pl.pallas_call(
+        kernel,
+        out_shape=outs,
+        in_specs=[vmem] * 17,
+        out_specs=[vmem] * len(outs),
+        scratch_shapes=scratch,
+        compiler_params=pltpu.CompilerParams(
+            collective_id=1, has_side_effects=True, vmem_limit_bytes=60 * 2**20
+        ),
+        name="block",
+    )
+
+    def closing(oa, ob, gr, gw1, gw2, vecs, turn, *outs):
+        fa, fb, ia, ib, f1, f2, fs, c1, h1, c2, h2, cs, hs = outs
+        fa[...] = oa[...]
+        fb[...] = ob[...]
+        moved = mm(turn[...], gr[...].reshape(n_dp * in_local, slab_lanes), 1, 0)
+        ia[...] = moved[:, : qlanes[0]].astype(bf).reshape(in_local, n_dp, qlanes[0])
+        ib[...] = moved[:, qlanes[0] : qlanes[0] + qlanes[1]].astype(bf).reshape(in_local, n_dp, qlanes[1])
+        for t, tap in enumerate(TAPS):
+            f2[t] = gw2[:, t * LANES : (t + 1) * LANES]
+            place = ORDER.index(tap)
+            place = place + (place > 0)
+            f1[t] = gw1[:, place * LANES : (place + 1) * LANES]
+        fs[...] = gw1[:, LANES : 2 * LANES]
+        for ref, row in ((c1, 0), (h1, 1), (c2, 2), (h2, 3), (cs, 4), (hs, 3)):
+            ref[...] = vecs[row : row + 1, :]
+
+    last = pl.pallas_call(
+        closing,
+        out_shape=[
+            jax.ShapeDtypeStruct((sizes[0], chan_part), bf),
+            jax.ShapeDtypeStruct((sizes[1], chan_part), bf),
+            jax.ShapeDtypeStruct((in_local, n_dp, qlanes[0]), bf),
+            jax.ShapeDtypeStruct((in_local, n_dp, qlanes[1]), bf),
+            jax.ShapeDtypeStruct((9, in_local, LANES), f),
+            jax.ShapeDtypeStruct((9, out_rows, LANES), f),
+            jax.ShapeDtypeStruct((in_local, LANES), f),
+        ]
+        + [jax.ShapeDtypeStruct((1, LANES), f)] * 6,
+        in_specs=[vmem] * 7,
+        out_specs=[vmem] * 13,
+        compiler_params=pltpu.CompilerParams(vmem_limit_bytes=40 * 2**20),
+        name="closing",
+    )
+    order_a = quarter_order(quarter[0], sides[0], 0, win[0]).astype(jnp.bfloat16)
+    order_b = quarter_order(quarter[1], sides[1], b_skip, slab_lanes - b_tile).astype(jnp.bfloat16)
+    total_rows = n_dp * in_local
+    turn = np.zeros((total_rows, total_rows), np.float32)
+    for c in range(in_local):
+        for j in range(n_dp):
+            turn[c * n_dp + j, j * in_local + c] = 1.0
+    turn = turn.astype(jnp.bfloat16)
+    return main, last, order_a, order_b, turn
+
+
+STOP = 99
+
+
+def fused_body(
+    input_a, input_b, boxes_a, boxes_b, weight_first, weight_second, weight_short,
+    gain_first, shift_first, gain_second, shift_second, gain_short, shift_short,
+    upstream_a, upstream_b,
+):
+    n_dp = lax.axis_size("dp")
+    chan_part = weight_first.shape[2]
+    main, last, order_a, order_b, turn = make_fused(
+        n_dp, input_a.shape[0], (boxes_a.shape[0], boxes_b.shape[0]), (SA, SB),
+        weight_first.shape[1], chan_part, STOP,
+    )
+    vectors = [
+        v.reshape(1, chan_part)
+        for v in (gain_first, shift_first, gain_second, shift_second, gain_short, shift_short)
+    ]
+    mid = main(
+        input_a, input_b, boxes_a.T, boxes_b.T, weight_first, weight_second, weight_short,
+        *vectors, upstream_a.T, upstream_b.T, order_a, order_b,
+    )
+    res = last(*mid, turn)
+    in_local = input_a.shape[0]
+    return (
+        res[0].T, res[1].T,
+        res[2].reshape(in_local, n_dp, 1, -1), res[3].reshape(in_local, n_dp, 1, -1),
+        res[4], res[5], res[6],
+    ) + tuple(v.reshape(chan_part) for v in res[7:])
+
+
+def choose_body(mesh):
+    return fused_body if mesh.shape["dp"] == 8 and mesh.shape["chan"] == 4 else plain_body
+
+
 def solution(mesh):
     placed = (
         P("dp", None),
@@ -378,7 +1054,7 @@
         P("chan", "dp"),
     )
     return jax.shard_map(
-        body,
+        choose_body(mesh),
         mesh=mesh,
         in_specs=placed,
         out_specs=(

time: 1140 us -> 131 us (0.11); the launches traced: 1120 us -> 128 us
  local copies, waits for them, and re-layouts: 695 us -> 5.43 us
  blocking collectives: 176 us -> 0 us
  waiting for transfers between devices: 151 us -> 0 us
  Pallas kernels: 0 us -> 122 us
  matrix products: 36.3 us -> 0 us
  other arithmetic: 29.2 us -> 0 us
  between operations: 17.1 us -> 0.77 us
  starting transfers between devices: 15.5 us -> 0 us
    slice x28 -> x0, local copies, waits for them, and re-layouts: 506 us -> none  [the longest x18 405 us: taps_strided(): padded[:, :, tap_row:tap_row + extent:2, tap_col:tap_col + extent:2]]
    pallas_call x0 -> x2, Pallas kernels: none -> 122 us  [the longest x1 121 us: fused_body(): main(input_a, input_b, boxes_a.T, boxes_b.T, weight_first, weight_second,...]
    psum x1 -> x0, waiting for transfers between devices: 90.8 us -> none  [body(): lax.psum((grad_first_local, grad_second_local, grad_short_local), 'dp')]
    all_to_all x1 -> x0, blocking collectives: 80.2 us -> none  [body(): lax.all_to_all(partial_inputs[0].astype(jnp.bfloat16), 'dp', split_axis=0...]
    psum x4 -> x0, blocking collectives: 80.2 us -> none  [the longest x2 40.6 us: body(): lax.psum((shift_tail, gain_tail, gain_side), 'dp')]
    squeeze x36 -> x0, local copies, waits for them, and re-layouts: 65.5 us -> none  [the longest x18 37.8 us: untaps_plain(): pieces[3 * tap_row + tap_col]]
    unnamed x232 -> x14, local copies, waits for them, and re-layouts: 51 us -> 5.43 us
    dot_general x18 -> x0, matrix products: 36.3 us -> none  [the longest x6 14.9 us: weight_product(): lax.dot_general(columns, gradient, (((1,), (1,)), ((), ())), preferred_el...]
  transfers between devices with their start and end apart: 8 -> 0, of which waited for: 5 -> 0; matrix products, arithmetic and copies ran while one was open for 23% -> 0% of each run, Pallas kernels for 0% -> 0%
where the time goes in v1:
time: 131 us; the launch traced here: 128 us
  Pallas kernels  122 us (93%)
  local copies, waits for them, and re-layouts  5.43 us (4%)
    pallas_call x1, Pallas kernels, fused_body(): main(input_a, input_b, boxes_a.T, boxes_b.T, weight_first, weight_second,...  121 us
    unnamed x14, local copies, waits for them, and re-layouts  5.43 us

profile of v1, /device:TPU:0, one launch (start us, length us, event | category | flops | bytes accessed | tf_op | source)
XLA Modules:
  0.0 128.5 jit_solution(18080855415183494614)
XLA Ops:
  0.7 0.0 copy-start.4
  0.7 120.8 %block.1 = (bf16[784,128]{1,0:T(8,128)(2,1)}, bf16[288,128]{1,0:T(8,128)(2,1)}, bf16[8,32,1152]{2,1,0:T(8,128)(2,1)}, f32[32,1280]{1,0:T(8,128)}, f32[64,1152]{1,0:T(8,128)}, /*index=5*/f32[8,128]{1,0:T(8,128)}) custom-call(bf16[32,25088]{1,0:T(8,128)(2,1)} %xa.1, bf16[32,9216]{1,0:T(8,128)(2,1)} %xb.1, s32[4,16]{1,0:T(4,128)} %bitcast.26, ...), custom_call_target="tpu_custom_call" | custom-call | tf_op jit(solution)/shard_map/block/pallas_call | solution.py:1021
  121.5 0.0 copy-done.4
  121.5 0.0 copy-start
  121.5 1.1 copy-done
  122.6 0.0 copy-start.1
  122.6 1.0 copy-done.1
  123.5 0.0 copy-start.2
  123.5 0.9 copy-done.2
  124.5 0.0 copy-start.3
  124.5 0.9 copy-done.3
  125.4 0.0 copy-start.5
  125.4 0.9 copy-done.5
  126.3 0.0 copy-start.6
  126.3 0.7 copy-done.6
  126.9 1.4 %closing.1 = (bf16[784,128]{1,0:T(8,128)(2,1)}, bf16[288,128]{1,0:T(8,128)(2,1)}, bf16[32,8,784]{2,1,0:T(8,128)(2,1)}, bf16[32,8,288]{2,1,0:T(8,128)(2,1)}, f32[...) custom-call(bf16[784,128]{1,0:T(8,128)(2,1)S(1)} %copy-done.2, ...), custom_call_target="tpu_custom_call" | custom-call | tf_op jit(solution)/shard_map/closing/pallas_call | solution.py:1025
Async XLA Ops:
  0.7 120.8 %copy-start.4 = (bf16[256,256]{1,0:T(8,128)(2,1)S(1)}, bf16[256,256]{1,0:T(8,128)(2,1)}, u32[]{:S(2)}) copy-start(bf16[256,256]{1,0:T(8,128)(2,1)} %constant.8.clone.turn) | copy-start | bytes 393220
  121.5 1.1 copy-start
  122.6 1.0 copy-start.1
  123.5 0.9 copy-start.2
  124.5 0.9 copy-start.3
  125.4 0.9 copy-start.5
  126.3 0.7 copy-start.6

commit v2 on v0

--- a/solution.py
+++ b/solution.py
@@ -1,6 +1,9 @@
 import jax
 import jax.numpy as jnp
 from jax import lax
+import numpy as np
+from jax.experimental import pallas as pl
+from jax.experimental.pallas import tpu as pltpu
 from jax.sharding import PartitionSpec as P
 
 SA = 14
@@ -131,7 +134,7 @@
     )
 
 
-def body(
+def plain_body(
     input_a,
     input_b,
     boxes_a,
@@ -359,6 +362,913 @@
     )
 
 
+MESH = pl.DeviceIdType.MESH
+TAPS = tuple((a, b) for a in range(3) for b in range(3))
+PLANE_TAPS = (
+    ((1, 1),),
+    ((1, 0), (1, 2)),
+    ((0, 1), (2, 1)),
+    ((0, 0), (0, 2), (2, 0), (2, 2)),
+)
+ORDER = [tap for taps in PLANE_TAPS for tap in taps]
+LANES = 128
+
+
+class Links:
+    def __init__(self, send_sems, recv_sems):
+        self.send_sems, self.recv_sems = send_sems, recv_sems
+        self.sends = self.slots = 0
+        self.open = []
+
+    def slot(self, count=1):
+        first = self.slots
+        self.slots += count
+        return first
+
+    def send(self, source, target, slot, where):
+        copy = pltpu.make_async_remote_copy(
+            source, target, self.send_sems.at[self.sends], self.recv_sems.at[slot],
+            device_id=where, device_id_type=MESH,
+        )
+        self.sends += 1
+        copy.start()
+        self.open.append(copy)
+
+    def arrived(self, target, slot, where):
+        pltpu.make_async_remote_copy(
+            target, target, self.send_sems.at[0], self.recv_sems.at[slot],
+            device_id=where, device_id_type=MESH,
+        ).wait_recv()
+
+    def drain(self):
+        for copy in self.open:
+            copy.wait_send()
+
+
+def mm(a, b, ca, cb):
+    return lax.dot_general(a, b, (((ca,), (cb,)), ((), ())), preferred_element_type=jnp.float32)
+
+
+def lanes_cat(parts):
+    return jnp.concatenate(parts, axis=1) if len(parts) > 1 else parts[0]
+
+
+def regroup(value, runs):
+    return jnp.concatenate([value[:, a:b] for a, b in runs], axis=1)
+
+
+def sigma(v):
+    return 0.5 * jnp.tanh(0.5 * v) + 0.5
+
+
+class Reduce:
+    def __init__(self, net, i, k, part, bufs, windows):
+        self.net, self.part, self.windows = net, part, windows
+        self.b1, self.s1, self.b2, self.s2, self.b3 = bufs
+        self.ix, self.pz, self.hz = i % 2, (i // 2) % 2, i // 4
+        self.peers = (
+            (i + 1 - 2 * self.ix, k),
+            (i + 2 - 4 * self.pz, k),
+            (i + 4 - 8 * self.hz, k),
+        )
+        self.slots = [net.slot(3) for _ in windows]
+
+    def first(self, w):
+        cols = self.windows[w]
+        self.net.send(
+            self.part.at[:, :, 1 - self.ix, :, cols], self.b1.at[:, :, :, cols],
+            self.slots[w], self.peers[0],
+        )
+
+    def second(self, w):
+        cols = self.windows[w]
+        self.net.arrived(self.b1.at[:, :, :, cols], self.slots[w], self.peers[0])
+        for h in range(2):
+            for p in range(2):
+                value = self.part[h, p, self.ix, :, cols].astype(jnp.float32)
+                value = value + self.b1[h, p, :, cols].astype(jnp.float32)
+                self.s1[h, p, :, cols] = value.astype(jnp.bfloat16)
+        self.net.send(
+            self.s1.at[:, 1 - self.pz, :, cols], self.b2.at[:, :, cols],
+            self.slots[w] + 1, self.peers[1],
+        )
+
+    def third(self, w):
+        cols = self.windows[w]
+        self.net.arrived(self.b2.at[:, :, cols], self.slots[w] + 1, self.peers[1])
+        for h in range(2):
+            value = self.s1[h, self.pz, :, cols].astype(jnp.float32)
+            value = value + self.b2[h, :, cols].astype(jnp.float32)
+            self.s2[h, :, cols] = value.astype(jnp.bfloat16)
+        self.net.send(
+            self.s2.at[1 - self.hz, :, cols], self.b3.at[:, cols],
+            self.slots[w] + 2, self.peers[2],
+        )
+
+    def last(self, w):
+        cols = self.windows[w]
+        self.net.arrived(self.b3.at[:, cols], self.slots[w] + 2, self.peers[2])
+        return self.s2[self.hz, :, cols].astype(jnp.float32) + self.b3[:, cols].astype(jnp.float32)
+
+
+def make_fused(n_dp, in_local, images, sides, chan_in, chan_part, stop):
+    f32, bf16 = jnp.float32, jnp.bfloat16
+    halves = tuple(side // 2 for side in sides)
+    sizes = tuple(h * h * n for h, n in zip(halves, images))
+    rows = sum(sizes)
+    quarter = tuple(n // 4 for n in images)
+    qlanes = tuple(q * side * side for q, side in zip(quarter, sides))
+    n_parts = 3
+    step = -(-sum(qlanes) // (n_parts * LANES)) * LANES
+    slab_lanes = n_parts * step
+    b_tile = qlanes[0] // LANES * LANES
+    b_skip = qlanes[0] - b_tile
+    chan_full = 4 * chan_part
+    out_rows = chan_full // n_dp
+    starts = (0, sizes[0])
+    chunks = [
+        (g, r, starts[g] + r * halves[g] * images[g], halves[g] * images[g])
+        for g in range(2)
+        for r in range(halves[g])
+    ]
+    win = [-(-q // LANES) * LANES for q in qlanes]
+    part_chunks = [[] for _ in range(n_parts)]
+    for chunk in chunks:
+        part_chunks[n_parts - 1 if chunk[0] else -(-(chunk[2] + chunk[3]) // step) - 1].append(chunk)
+    spans = [(part[0][2], part[-1][2] + part[-1][3]) for part in part_chunks]
+    pieces = []
+    for part in part_chunks:
+        found = [[c for c in part if c[0] == g] for g in range(2)]
+        pieces.append([(g, f[0][1], f[-1][1] + 1) for g, f in enumerate(found) if f])
+    in_win = [(a // LANES * LANES, min(-(-b // LANES) * LANES, slab_lanes)) for a, b in spans]
+    out_win = []
+    for c in range(n_parts):
+        hit = [span for span in spans if span[0] < (c + 1) * step and span[1] > c * step]
+        out_win.append((hit[0][0], hit[-1][1]))
+    runs = []
+    for part in pieces:
+        for g, r0, r1 in part:
+            side, base = sides[g], (0, qlanes[0])[g]
+            runs += [
+                (base + (image * side + 2 * r0) * side, base + (image * side + 2 * r1) * side)
+                for image in range(quarter[g])
+            ]
+    runs.append((sum(qlanes), slab_lanes))
+    lane_of, order = 0, []
+    for a, b in runs:
+        order.append((a, lane_of, lane_of + b - a))
+        lane_of += b - a
+    back_runs = [(a, b) for _, a, b in sorted(order)]
+    split = halves[0] // 2 + 1
+    act_pieces = [(1, 0, halves[1]), (0, 0, split), (0, split, halves[0])]
+    mid = (rows // 32 + 1) * 16
+    row_halves = (slice(0, mid), slice(mid, rows))
+    cols2 = (slice(0, 5 * LANES), slice(5 * LANES, 9 * LANES))
+    cols1 = (slice(0, 10 * LANES),)
+
+    def kernel(*refs):
+        (xa_h, xb_h, bxa_h, bxb_h, w1_h, w2_h, ws_h, g1_h, b1_h, g2_h, b2_h, gs_h, bs_h, ua_h, ub_h,
+         oa, ob, gr, gw1, gws, gw2, vecs,
+         xa, xb, bxa, bxb, w1, w2, ws, g1, b1, g2, b2, gs, bs, ua, ub, cells,
+         xs, xt, xr, zg, zpa, zpb, valid, z1, zs, a1a, a1b, slots, up, outr, gv, dza, dzb, dzsr,
+         dd, hp, hr1, hs, hr2, gu, d1a, d1b,
+         wg2, p21, p22, p23, p24, p25, wg1, p11, p12, p13, p14, p15,
+         gp, gr1, gsum, gr2, zt, gt, lsem, ssem, rsem) = refs
+        i, k = lax.axis_index("dp"), lax.axis_index("chan")
+        k1 = k + 1 - 2 * (k % 2)
+        k2 = (k + 2) % 4
+        k3 = (k1 + 2) % 4
+        net = Links(ssem, rsem)
+        zp, a1, dz, d1 = (zpa, zpb), (a1a, a1b), (dza, dzb), (d1a, d1b)
+
+        def flat(value):
+            return value.reshape(-1, value.shape[-1])
+
+        def zeros(count):
+            return [jnp.zeros((8, LANES), f32)] * count
+
+        loads = {}
+        pairs_of = (
+            ("xa", xa_h, xa), ("xb", xb_h, xb),
+            ("bxa", bxa_h, bxa), ("bxb", bxb_h, bxb), ("ua", ua_h, ua), ("ub", ub_h, ub),
+            ("w1", w1_h, w1), ("ws", ws_h, ws), ("g1", g1_h, g1), ("b1", b1_h, b1), ("g2", g2_h, g2),
+            ("b2", b2_h, b2), ("gs", gs_h, gs), ("bs", bs_h, bs), ("w2", w2_h, w2),
+        )
+        for index, (name, source, target) in enumerate(pairs_of):
+            loads[name] = pltpu.make_async_copy(source, target, lsem.at[index])
+        loads["xa"].start()
+        loads["xb"].start()
+
+        def need(*names):
+            for name in names:
+                loads.pop(name).wait()
+
+        barrier = pltpu.get_barrier_semaphore()
+        for d in range(1, n_dp):
+            pl.semaphore_signal(barrier, inc=1, device_id=((i + d) % n_dp, k), device_id_type=MESH)
+        pl.semaphore_signal(barrier, inc=1, device_id=(i, k1), device_id_type=MESH)
+        pl.semaphore_signal(barrier, inc=1, device_id=(i, k2), device_id_type=MESH)
+
+        if stop == -6:
+            need("xa", "xb")
+            for copy in loads.values():
+                copy.start()
+            pl.semaphore_wait(barrier, n_dp + 1)
+            need(*list(loads))
+            return net.drain()
+        need("xa", "xb")
+        for copy in loads.values():
+            copy.start()
+        lane = lax.broadcasted_iota(jnp.int32, (in_local, LANES), 1)
+        for d in range(n_dp):
+            j = (i + d) % n_dp
+            begin = 4 * qlanes[0] * j + qlanes[0] * k
+            tile = begin // LANES
+            part_a = xa[:, pl.ds(pl.multiple_of(tile * LANES, LANES), win[0])].astype(f32)
+            part_a = pltpu.roll(part_a, (win[0] - (begin - tile * LANES)) % win[0], 1)
+            begin = 4 * qlanes[1] * j + qlanes[1] * k
+            tile = begin // LANES
+            part_b = xb[:, pl.ds(pl.multiple_of(tile * LANES, LANES), win[1])].astype(f32)
+            part_b = jnp.concatenate([part_b, jnp.zeros((in_local, LANES), f32)], axis=1)
+            wide = win[1] + LANES
+            part_b = pltpu.roll(part_b, (wide + b_skip - (begin - tile * LANES)) % wide, 1)
+            seam = jnp.where(lane < b_skip, part_a[:, b_tile : b_tile + LANES], part_b[:, :LANES])
+            xs[d * in_local : (d + 1) * in_local, :] = jnp.concatenate(
+                [part_a[:, :b_tile], seam, part_b[:, LANES : slab_lanes - b_tile]], axis=1
+            ).astype(bf16)
+        if stop == -5:
+            pl.semaphore_wait(barrier, n_dp + 1)
+            need(*list(loads))
+            return net.drain()
+        slot_x = [net.slot(n_dp) for _ in range(n_parts)]
+        for c in range(n_parts):
+            cols = slice(c * step, (c + 1) * step)
+            if c == 0:
+                ordered = regroup(xs[...], runs)
+            moved = ordered[:, cols]
+            xt[:, :, cols] = moved.reshape(n_dp, in_local, step)
+            xr[i, :, cols] = moved[:in_local]
+            if c == 0:
+                pl.semaphore_wait(barrier, n_dp + 1)
+            for d in range(1, n_dp):
+                net.send(xt.at[d, :, cols], xr.at[i, :, cols], slot_x[c] + i, ((i + d) % n_dp, k))
+
+        if stop in (-3,-4):
+            for c in range(n_parts):
+                for d in range(1, n_dp):
+                    j = (i + d) % n_dp
+                    net.arrived(xr.at[j, :, c*step:(c+1)*step], slot_x[c] + j, (j, k))
+            need(*list(loads))
+            return net.drain()
+
+        for buf in (zpa, zpb, a1a, a1b, dza, dzb, d1a, d1b):
+            side = buf.shape[1] if len(buf.shape) == 5 else buf.shape[0]
+            lead = (slice(None),) if len(buf.shape) == 5 else ()
+            for edge in (0, side - 1):
+                for index in (lead + (edge,), lead + (slice(None), edge)):
+                    region = buf.at[index]
+                    region[...] = jnp.zeros(region.shape, buf.dtype)
+        need("bxa", "bxb", "ua", "ub")
+        population = zeros(1)[0]
+        for g, box in enumerate((bxa, bxb)):
+            n, half = images[g], halves[g]
+            diag = lax.broadcasted_iota(jnp.int32, (n, n), 0) == lax.broadcasted_iota(jnp.int32, (n, n), 1)
+            ends = [
+                jnp.sum(jnp.where(diag, box[q : q + 1, :].astype(f32), 0.0), axis=1, keepdims=True)
+                for q in range(4)
+            ]
+            inside = [
+                [((p >= ends[q]) & (p < ends[q] + ends[q + 2])).astype(f32) for p in range(half)]
+                for q in range(2)
+            ]
+            for r in range(half):
+                for s in range(half):
+                    cell = jnp.broadcast_to(inside[0][r] * inside[1][s], (n, LANES))
+                    begin = starts[g] + (r * half + s) * n
+                    valid[begin : begin + n, :] = cell
+                    population = population + jnp.sum(cell.reshape(n // 8, 8, LANES), axis=0)
+        population = jnp.sum(population, axis=0, keepdims=True)
+        for g, source in enumerate((ua, ub)):
+            n, count = images[g], halves[g] ** 2
+            gu[starts[g] : starts[g] + sizes[g], :] = source[...].astype(f32)
+            for cell in range(count):
+                up[starts[g] + cell * n : starts[g] + (cell + 1) * n, :] = gu[
+                    pl.ds(starts[g] + cell, n, stride=count), :
+                ]
+
+        lane = lax.broadcasted_iota(jnp.int32, (16, slab_lanes), 1)
+        for part, (a, b) in zip(pieces, spans):
+            for g, r0, r1 in part:
+                n, half, side, width = quarter[g], halves[g], sides[g], halves[g] * images[g]
+                for r in range(r0, r1):
+                    for begin in range(0, width, 16):
+                        at = begin + lax.broadcasted_iota(jnp.int32, (16, 1), 0)
+                        image, plane, s = at % n, (at // n) % 4, at // (4 * n)
+                        first = starts[g] + r0 * width + 2 * (r - r0) * side
+                        place = first + image * (2 * (r1 - r0) * side) + (plane // 2) * side + 2 * s + plane % 2
+                        row = starts[g] + r * width + begin
+                        cells[row : row + 16, :] = jnp.where(lane == place, 1.0, 0.0).astype(bf16)
+        slot_z = [net.slot(4) for _ in range(n_parts)]
+
+        if stop == -2:
+            for c in range(n_parts):
+                for d in range(1, n_dp):
+                    j = (i + d) % n_dp
+                    net.arrived(xr.at[j, :, c*step:(c+1)*step], slot_x[c] + j, (j, k))
+            need(*list(loads))
+            return net.drain()
+
+        def quarter_in(c):
+            lo, hi = c * step, (c + 1) * step
+            for d in range(1, n_dp):
+                j = (i + d) % n_dp
+                net.arrived(xr.at[j, :, lo:hi], slot_x[c] + j, (j, k))
+            (a, b), (lo, hi) = spans[c], in_win[c]
+            whole = jnp.concatenate([xr[q, :, lo:hi] for q in range(n_dp)], axis=0)
+            zg[k, a:b, :] = mm(cells[a:b, lo:hi], whole, 1, 1).astype(bf16)
+            for where in (k2, k1):
+                net.send(zg.at[k, a:b], zg.at[k, a:b], slot_z[c] + k, (i, where))
+
+        def quarter_on(c):
+            a, b = spans[c]
+            net.arrived(zg.at[k2, a:b], slot_z[c] + k2, (i, k2))
+            net.send(zg.at[k2, a:b], zg.at[k2, a:b], slot_z[c] + k2, (i, k1))
+
+        def planes_of(quarters, g):
+            count = quarter[g]
+            if count % 8 == 0:
+                return [
+                    jnp.concatenate([v[:, count * p : count * (p + 1)] for v in quarters], axis=1)
+                    for p in range(4)
+                ]
+            low = lax.broadcasted_iota(jnp.int32, (1, 8, 1), 1) < 4
+            parts = [[v[:, 8 * h : 8 * h + 8] for v in quarters] for h in range(2)]
+            turned = [[pltpu.roll(v, 4, 1) for v in side] for side in parts]
+            result = []
+            for p in range(4):
+                v, t = parts[p // 2], turned[p // 2]
+                if p % 2 == 0:
+                    both = [jnp.where(low, v[0], t[1]), jnp.where(low, v[2], t[3])]
+                else:
+                    both = [jnp.where(low, t[0], v[1]), jnp.where(low, t[2], v[3])]
+                result.append(jnp.concatenate(both, axis=1))
+            return result
+
+        def strided_patch(c, tap):
+            a, b = tap
+            p = 2 * (a % 2 == 0) + (b % 2 == 0)
+            r, s = 1 - (a == 0), 1 - (b == 0)
+            return jnp.concatenate(
+                [flat(zp[g][p, r0 + r : r1 + r, s : s + halves[g]]) for g, r0, r1 in pieces[c]], axis=0
+            )
+
+        def rowsum(value):
+            return jnp.sum(value.reshape(-1, 8, LANES), axis=0)
+
+        def first_conv(c, acc):
+            a, b = spans[c]
+            net.arrived(zg.at[k1, a:b], slot_z[c] + k1, (i, k1))
+            net.arrived(zg.at[k3, a:b], slot_z[c] + k3, (i, k1))
+            for g, r, begin, count in part_chunks[c]:
+                quarters = [
+                    zg[q, begin : begin + count, :].astype(f32).reshape(halves[g], images[g], chan_in)
+                    for q in range(4)
+                ]
+                for p, value in enumerate(planes_of(quarters, g)):
+                    zp[g][p, 1 + r, 1 : 1 + halves[g]] = value.astype(bf16)
+            both = mm(strided_patch(c, (1, 1)), jnp.concatenate([w1[4], ws[...]], axis=1), 1, 0)
+            zs[a:b, :] = both[:, chan_part:]
+            value = both[:, :chan_part]
+            for tap in TAPS:
+                if tap != (1, 1):
+                    value = value + mm(strided_patch(c, tap), w1[3 * tap[0] + tap[1]], 1, 0)
+            z1[a:b, :] = value
+            for g, r, begin, count in part_chunks[c]:
+                span = slice(begin, begin + count)
+                ok = valid[span, :]
+                u, w = z1[span, :], zs[span, :]
+                uv, wv = u * ok, w * ok
+                acc = [
+                    acc[0] + rowsum(uv), acc[1] + rowsum(uv * u),
+                    acc[2] + rowsum(wv), acc[3] + rowsum(wv * w),
+                ]
+            return acc
+
+        acc = zeros(4)
+        for c in range(n_parts):
+            quarter_in(c)
+            if c >= 1:
+                quarter_on(c - 1)
+        if stop == 1:
+            quarter_on(n_parts - 1)
+            for c in range(n_parts):
+                net.arrived(zg.at[k1, spans[c][0]:spans[c][1]], slot_z[c] + k1, (i, k1))
+                net.arrived(zg.at[k3, spans[c][0]:spans[c][1]], slot_z[c] + k3, (i, k1))
+            need(*list(loads))
+            return net.drain()
+        need("w1", "ws")
+        for c in range(n_parts):
+            if c == 1:
+                quarter_on(n_parts - 1)
+            acc = first_conv(c, acc)
+
+        def message(sums):
+            parts = [jnp.sum(v, axis=0, keepdims=True) if v.shape[0] > 1 else v for v in sums]
+            parts.append(jnp.zeros((8 - len(parts), LANES), f32))
+            return jnp.concatenate(parts, axis=0)
+
+        def share(rnd, value):
+            slots[rnd, i] = value
+            first = net.slot(n_dp)
+            for d in range(1, n_dp):
+                net.send(slots.at[rnd, i], slots.at[rnd, i], first + i, ((i + d) % n_dp, k))
+            return first
+
+        def total(rnd, first):
+            for d in range(1, n_dp):
+                j = (i + d) % n_dp
+                net.arrived(slots.at[rnd, j], first + j, (j, k))
+            return jnp.sum(slots[rnd], axis=0)
+
+        if stop == 2:
+            valid[0:8, :] = acc[0] + acc[1] + acc[2] + acc[3]
+            need(*list(loads))
+            return net.drain()
+        first = share(0, message(acc + [population]))
+        need(*list(loads))
+        tot = total(0, first)
+        inv_pop = 1.0 / tot[4:5]
+        mean1, means = tot[0:1] * inv_pop, tot[2:3] * inv_pop
+        sc1 = lax.rsqrt(tot[1:2] * inv_pop - mean1 * mean1 + epsilon)
+        scs = lax.rsqrt(tot[3:4] * inv_pop - means * means + epsilon)
+        gain1, shift1 = g1[...], b1[...]
+        if stop == 3:
+            valid[0:1, :] = sc1 + scs
+            return net.drain()
+
+        def act_ref(piece, q):
+            g, r0, r1 = piece
+            return a1[g].at[q, 1 + r0 : 1 + r1, 1 : 1 + halves[g]]
+
+        slot_a = [net.slot(4) for _ in act_pieces]
+        for piece, slot in zip(act_pieces, slot_a):
+            for g, r, begin, count in chunks:
+                if g == piece[0] and piece[1] <= r < piece[2]:
+                    span = slice(begin, begin + count)
+                    hat = (z1[span, :] - mean1) * sc1
+                    z1[span, :] = hat
+                    v = hat * gain1 + shift1
+                    act = (v * sigma(v) * valid[span, :]).astype(bf16)
+                    a1[g][k, 1 + r, 1 : 1 + halves[g]] = act.reshape(halves[g], images[g], chan_part)
+            for where in (k2, k1):
+                net.send(act_ref(piece, k), act_ref(piece, k), slot + k, (i, where))
+
+        def act_on(n):
+            piece, slot = act_pieces[n], slot_a[n]
+            net.arrived(act_ref(piece, k2), slot + k2, (i, k2))
+            net.send(act_ref(piece, k2), act_ref(piece, k2), slot + k2, (i, k1))
+
+        def act_in(n):
+            piece, slot = act_pieces[n], slot_a[n]
+            net.arrived(act_ref(piece, k1), slot + k1, (i, k1))
+            net.arrived(act_ref(piece, k3), slot + k3, (i, k1))
+
+        def second_conv(piece, acc):
+            g, r0, r1 = piece
+            width = halves[g] * images[g]
+            begin, end = starts[g] + r0 * width, starts[g] + r1 * width
+            value = None
+            for a, b in TAPS:
+                patch = lanes_cat(
+                    [flat(a1[g][q, r0 + a : r1 + a, b : b + halves[g]]) for q in range(4)]
+                )
+                part = mm(patch, w2[3 * a + b], 1, 0)
+                value = part if value is None else value + part
+            gv[begin:end, :] = value
+            for row in range(begin, end, width):
+                span = slice(row, row + width)
+                u = gv[span, :]
+                uv = u * valid[span, :]
+                acc = [acc[0] + rowsum(uv), acc[1] + rowsum(uv * u)]
+            return acc
+
+        acc = zeros(2)
+        act_on(0)
+        act_in(0)
+        acc = second_conv((1, 0, halves[1]), acc)
+        act_on(1)
+        act_in(1)
+        acc = second_conv((0, 0, split - 1), acc)
+        act_on(2)
+        act_in(2)
+        acc = second_conv((0, split - 1, halves[0]), acc)
+        first = share(1, message(acc))
+        for g, r, begin, count in chunks:
+            span = slice(begin, begin + count)
+            zs[span, :] = (zs[span, :] - means) * scs
+        tot = total(1, first)
+        mean2 = tot[0:1] * inv_pop
+        sc2 = lax.rsqrt(tot[1:2] * inv_pop - mean2 * mean2 + epsilon)
+        if stop == 5:
+            valid[0:1, :] = sc2
+            return net.drain()
+        gain2, gains = g2[...], gs[...]
+        shifts = b2[...] + bs[...]
+        acc = zeros(3)
+        for g, r, begin, count in chunks:
+            span = slice(begin, begin + count)
+            ok = valid[span, :]
+            hat2 = (gv[span, :] - mean2) * sc2
+            hats = zs[span, :]
+            v = hat2 * gain2 + hats * gains + shifts
+            sig = sigma(v)
+            outr[span, :] = v * sig * ok
+            grad = up[span, :] * ok * (sig * (1.0 + v * (1.0 - sig)))
+            up[span, :] = grad
+            gv[span, :] = hat2
+            acc = [acc[0] + rowsum(grad), acc[1] + rowsum(grad * hat2), acc[2] + rowsum(grad * hats)]
+        first = share(2, message(acc))
+        for g, target in enumerate((oa, ob)):
+            n, count = images[g], halves[g] ** 2
+            for cell in range(count):
+                gu[pl.ds(starts[g] + cell, n, stride=count), :] = outr[
+                    starts[g] + cell * n : starts[g] + (cell + 1) * n, :
+                ]
+            target[...] = gu[starts[g] : starts[g] + sizes[g], :].astype(bf16)
+        tot = total(2, first)
+        sum_tail, sum_gain2, sum_gains = tot[0:1], tot[1:2], tot[2:3]
+        if stop == 6:
+            valid[0:1, :] = sum_tail
+            return net.drain()
+
+        k2g, ksg = gain2 * sc2, gains * scs
+        db, dg2, dgs = sum_tail * inv_pop, sum_gain2 * inv_pop, sum_gains * inv_pop
+        for g, r, begin, count in chunks:
+            span = slice(begin, begin + count)
+            value = k2g * (up[span, :] - valid[span, :] * (db + gv[span, :] * dg2))
+            dz[g][1 + r, 1 : 1 + halves[g]] = value.astype(bf16).reshape(halves[g], images[g], chan_part)
+        for g in range(2):
+            for t, (a, b) in enumerate(TAPS):
+                dd[starts[g] : starts[g] + sizes[g], t * LANES : (t + 1) * LANES] = flat(
+                    dz[g][2 - a : 2 - a + halves[g], 2 - b : 2 - b + halves[g]]
+                )
+
+        def back_second(first, span):
+            begin = pl.multiple_of(first * chan_part, LANES)
+            weights = lanes_cat([w2[t, pl.ds(begin, 2 * chan_part), :] for t in range(9)])
+            value = mm(dd[span, :], weights, 1, 1).astype(bf16)
+            hp[first, span, :] = value[:, :chan_part]
+            hp[first + 1, span, :] = value[:, chan_part:]
+
+        slot_h = [net.slot(3) for _ in row_halves]
+        for span, slot in zip(row_halves, slot_h):
+            back_second(2 * (k2 // 2), span)
+            net.send(hp.at[k3, span], hr1.at[1, span], slot + 1, (i, k1))
+        for span, slot in zip(row_halves, slot_h):
+            net.arrived(hr1.at[1, span], slot + 1, (i, k1))
+            hs[span, :] = (hp[k2, span, :].astype(f32) + hr1[1, span, :].astype(f32)).astype(bf16)
+            net.send(hs.at[span], hr2.at[span], slot + 2, (i, k2))
+        back_second(2 * (k // 2), slice(0, rows))
+        for span, slot in zip(row_halves, slot_h):
+            net.send(hp.at[k1, span], hr1.at[0, span], slot, (i, k1))
+
+        acts = [
+            lanes_cat([flat(a1[g][q, 1 : 1 + halves[g], 1 : 1 + halves[g]]) for q in range(4)])
+            for g in range(2)
+        ]
+        sum2 = Reduce(net, i, k, wg2, (p21, p22, p23, p24, p25), cols2)
+        for w, cols in enumerate(cols2):
+            value = mm(acts[0], dd[: sizes[0], cols], 0, 0) + mm(acts[1], dd[sizes[0] :, cols], 0, 0)
+            wg2[:, :, :, :, cols] = value.astype(bf16).reshape(2, 2, 2, out_rows, value.shape[1])
+            sum2.first(w)
+        for g, r, begin, count in chunks:
+            span = slice(begin, begin + count)
+            value = ksg * (up[span, :] - valid[span, :] * (db + zs[span, :] * dgs))
+            dzsr[span, :] = value.astype(bf16)
+        acc = zeros(2)
+        for n, (span, slot) in enumerate(zip(row_halves, slot_h)):
+            net.arrived(hr1.at[0, span], slot, (i, k1))
+            net.arrived(hr2.at[span], slot + 2, (i, k2))
+            for begin in range(span.start, span.stop, 16):
+                part = slice(begin, begin + 16)
+                hat = z1[part, :]
+                v = hat * gain1 + shift1
+                sig = sigma(v)
+                grad = hp[k, part, :].astype(f32) + hr1[0, part, :].astype(f32) + hr2[part, :].astype(f32)
+                grad = grad * valid[part, :] * (sig * (1.0 + v * (1.0 - sig)))
+                gu[part, :] = grad
+                acc = [acc[0] + rowsum(grad), acc[1] + rowsum(grad * hat)]
+        first = share(3, message(acc))
+        sum2.second(0)
+        tot = total(3, first)
+        sum_head, sum_gain1 = tot[0:1], tot[1:2]
+
+        def close_second():
+            for w, cols in enumerate(cols2):
+                value = sum2.last(w)
+                for t in range(cols.start // LANES, cols.stop // LANES):
+                    gw2[t] = value[:, t * LANES - cols.start : (t + 1) * LANES - cols.start]
+
+        if stop == 8:
+            valid[0:1, :] = sum_head
+            sum2.second(1)
+            for w in range(2):
+                sum2.third(w)
+            close_second()
+            return net.drain()
+        k1g = gain1 * sc1
+        db, dg1 = sum_head * inv_pop, sum_gain1 * inv_pop
+        for g, r, begin, count in chunks:
+            span = slice(begin, begin + count)
+            value = k1g * (gu[span, :] - valid[span, :] * (db + z1[span, :] * dg1))
+            d1[g][r, : halves[g]] = value.astype(bf16).reshape(halves[g], images[g], chan_part)
+
+        def back_patch(pieces, p):
+            parts = []
+            for g, r0, r1 in pieces:
+                width = halves[g] * images[g]
+                taps = [
+                    flat(d1[g][r0 + (a == 0) : r1 + (a == 0), (b == 0) : (b == 0) + halves[g]])
+                    for a, b in PLANE_TAPS[p]
+                ]
+                if p == 0:
+                    taps.append(dzsr[starts[g] + r0 * width : starts[g] + r1 * width, :])
+                parts.append(lanes_cat(taps))
+            return jnp.concatenate(parts, axis=0) if len(parts) > 1 else parts[0]
+
+        slot_g = [net.slot(3) for _ in range(n_parts)]
+
+        def back_first(c):
+            a, b = spans[c]
+            planes = []
+            for p in range(4):
+                weights = [w1[3 * ta + tb] for ta, tb in PLANE_TAPS[p]]
+                if p == 0:
+                    weights.append(ws[...])
+                planes.append(mm(back_patch(pieces[c], p), lanes_cat(weights), 1, 1))
+            for g, r, begin, count in part_chunks[c]:
+                values = [
+                    v[begin - a : begin - a + count].reshape(halves[g], images[g], chan_in)
+                    for v in planes
+                ]
+                for q, value in enumerate(planes_of(values, g)):
+                    gp[q, begin : begin + count, :] = flat(value).astype(bf16)
+            net.send(gp.at[k3, a:b], gr1.at[1, a:b], slot_g[c] + 1, (i, k1))
+            net.send(gp.at[k1, a:b], gr1.at[0, a:b], slot_g[c], (i, k1))
+
+        def back_cross(c):
+            a, b = spans[c]
+            net.arrived(gr1.at[1, a:b], slot_g[c] + 1, (i, k1))
+            for begin in range(a, b, 16):
+                span = slice(begin, begin + 16)
+                value = gp[k2, span, :].astype(f32) + gr1[1, span, :].astype(f32)
+                gsum[span, :] = value.astype(bf16)
+            net.send(gsum.at[a:b], gr2.at[a:b], slot_g[c] + 2, (i, k2))
+
+        slot_o = [net.slot(n_dp) for _ in range(n_parts)]
+
+        def back_out(c):
+            a, b = spans[c]
+            net.arrived(gr1.at[0, a:b], slot_g[c], (i, k1))
+            net.arrived(gr2.at[a:b], slot_g[c] + 2, (i, k2))
+            for begin in range(a, b, 16):
+                span = slice(begin, begin + 16)
+                value = gp[k, span, :].astype(f32) + gr1[0, span, :].astype(f32)
+                zt[span, :] = (value + gr2[span, :].astype(f32)).astype(bf16)
+            cols = slice(c * step, (c + 1) * step)
+            a, b = out_win[c]
+            value = mm(zt[a:b, :], cells[a:b, cols], 0, 0).astype(bf16)
+            gt[:, :, cols] = value.reshape(n_dp, in_local, step)
+            for d in range(1, n_dp):
+                j = (i + d) % n_dp
+                net.send(gt.at[j, :, cols], gr.at[i, :, cols], slot_o[c] + i, (j, k))
+
+        sum1 = Reduce(net, i, k, wg1, (p11, p12, p13, p14, p15), cols1)
+
+        def weight_first():
+            everything = [(0, 0, halves[0]), (1, 0, halves[1])]
+            blocks = []
+            for p in range(4):
+                value = 0.0
+                for g, r0, r1 in everything:
+                    cell = flat(zp[g][p, 1 : 1 + halves[g], 1 : 1 + halves[g]])
+                    value = value + mm(cell, back_patch([(g, r0, r1)], p), 0, 0)
+                blocks.append(value.astype(bf16))
+            wg1[...] = lanes_cat(blocks).reshape(2, 2, 2, in_local, 10 * LANES)
+            sum1.first(0)
+
+        order = list(reversed(range(n_parts)))
+        for n, c in enumerate(order):
+            back_first(c)
+            if n >= 1:
+                back_cross(order[n - 1])
+        back_cross(order[-1])
+        weight_first()
+        sum2.second(1)
+        sum2.third(0)
+        for n, c in enumerate(order):
+            back_out(c)
+            if n == 0:
+                sum2.third(1)
+            if n == 1:
+                sum1.second(0)
+        sum1.third(0)
+        own = pltpu.make_async_copy(gt.at[i], gr.at[i], lsem.at[len(pairs_of)])
+        own.start()
+        close_second()
+        value = sum1.last(0)
+        for t, tap in enumerate(TAPS):
+            place = ORDER.index(tap)
+            place = place + (place > 0)
+            gw1[t] = value[:, place * LANES : (place + 1) * LANES]
+        gws[...] = value[:, LANES : 2 * LANES]
+        vecs[...] = message([sum_gain1, sum_head, sum_gain2, sum_tail, sum_gains])
+        for c in range(n_parts):
+            cols = slice(c * step, (c + 1) * step)
+            for d in range(1, n_dp):
+                j = (i + d) % n_dp
+                net.arrived(gr.at[j, :, cols], slot_o[c] + j, (j, k))
+        own.wait()
+        net.drain()
+
+    V = pltpu.VMEM
+    pads = [(h + 2, h + 2, n, chan_part) for h, n in zip(halves, images)]
+    half_pads = [(h + 1, h + 1, n) for h, n in zip(halves, images)]
+
+    def ladder(count, width):
+        return [
+            V((2, 2, 2, count, width), bf16), V((2, 2, count, width), bf16), V((2, 2, count, width), bf16),
+            V((2, count, width), bf16), V((2, count, width), bf16), V((count, width), bf16),
+        ]
+
+    inputs = [
+        V((in_local, n_dp * 4 * qlanes[0]), bf16), V((in_local, n_dp * 4 * qlanes[1]), bf16),
+        V((4, images[0]), jnp.int32), V((4, images[1]), jnp.int32),
+        V((9, chan_in, chan_part), bf16), V((9, chan_full, chan_part), bf16), V((chan_in, chan_part), bf16),
+    ] + [V((1, chan_part), f32)] * 6 + [
+        V((sizes[0], chan_part), bf16), V((sizes[1], chan_part), bf16),
+    ]
+    scratch = inputs + [
+        V((rows, slab_lanes), bf16),
+        V((n_dp * in_local, slab_lanes), bf16),
+        V((n_dp, in_local, slab_lanes), bf16),
+        V((n_dp, in_local, slab_lanes), bf16),
+        V((4, rows, chan_in), bf16),
+        V((4,) + half_pads[0] + (chan_in,), bf16),
+        V((4,) + half_pads[1] + (chan_in,), bf16),
+        V((rows, LANES), f32),
+        V((rows, chan_part), f32),
+        V((rows, chan_part), f32),
+        V((4,) + pads[0], bf16),
+        V((4,) + pads[1], bf16),
+        V((4, n_dp, 8, LANES), f32),
+        V((rows, chan_part), f32),
+        V((rows, chan_part), f32),
+        V((rows, chan_part), f32),
+        V(pads[0], bf16),
+        V(pads[1], bf16),
+        V((rows, chan_part), bf16),
+        V((rows, 9 * chan_part), bf16),
+        V((4, rows, chan_part), bf16),
+        V((2, rows, chan_part), bf16),
+        V((rows, chan_part), bf16),
+        V((rows, chan_part), bf16),
+        V((rows, chan_part), f32),
+        V(half_pads[0] + (chan_part,), bf16),
+        V(half_pads[1] + (chan_part,), bf16),
+    ]
+    scratch += ladder(out_rows, 9 * LANES) + ladder(in_local, 10 * LANES)
+    scratch += [
+        V((4, rows, chan_in), bf16),
+        V((2, rows, chan_in), bf16),
+        V((rows, chan_in), bf16),
+        V((rows, chan_in), bf16),
+        V((rows, chan_in), bf16),
+        V((n_dp, in_local, slab_lanes), bf16),
+        pltpu.SemaphoreType.DMA((len(inputs) + 1,)),
+        pltpu.SemaphoreType.DMA((160,)),
+        pltpu.SemaphoreType.DMA((160,)),
+    ]
+    mid_outs = [
+        jax.ShapeDtypeStruct((sizes[0], chan_part), bf16),
+        jax.ShapeDtypeStruct((sizes[1], chan_part), bf16),
+        jax.ShapeDtypeStruct((n_dp, in_local, slab_lanes), bf16),
+        jax.ShapeDtypeStruct((9, in_local, LANES), f32),
+        jax.ShapeDtypeStruct((in_local, LANES), f32),
+        jax.ShapeDtypeStruct((9, out_rows, LANES), f32),
+        jax.ShapeDtypeStruct((8, LANES), f32),
+    ]
+    vmem = pl.BlockSpec(memory_space=pltpu.VMEM)
+    hbm = pl.BlockSpec(memory_space=pl.ANY)
+    main = pl.pallas_call(
+        kernel,
+        out_shape=mid_outs,
+        in_specs=[hbm] * len(inputs),
+        out_specs=[vmem, vmem, hbm, vmem, vmem, vmem, vmem],
+        scratch_shapes=scratch,
+        compiler_params=pltpu.CompilerParams(
+            collective_id=1, has_side_effects=True, vmem_limit_bytes=60 * 2**20
+        ),
+        name="block",
+    )
+
+    def closing(oa_h, ob_h, gr_h, gw1_h, gws_h, gw2_h, vecs_h, turn_h,
+                fa, fb, ia, ib, f1, f2, fs, c1, h1, c2, h2, cs, hs,
+                oa, ob, gr, gw1, gws, gw2, vecs, turn, sems):
+        moves = [
+            pltpu.make_async_copy(source, target, sems.at[index])
+            for index, (source, target) in enumerate(
+                (
+                    (gr_h, gr), (turn_h, turn), (vecs_h, vecs), (gw2_h, gw2), (gw1_h, gw1),
+                    (oa_h, oa), (ob_h, ob), (gws_h, gws),
+                )
+            )
+        ]
+        outs = [
+            pltpu.make_async_copy(source, target, sems.at[len(moves) + index])
+            for index, (source, target) in enumerate(
+                ((gw2, f2), (gw1, f1), (oa, fa), (ob, fb), (gws, fs))
+            )
+        ]
+        for move in moves:
+            move.start()
+        for move in moves[:3]:
+            move.wait()
+        for move, out in zip(moves[3:], outs):
+            move.wait()
+            out.start()
+        moved = mm(turn[...], gr[...].reshape(n_dp * in_local, slab_lanes), 1, 0)
+        natural = regroup(moved, back_runs)
+        ia[...] = natural[:, : qlanes[0]].reshape(in_local, n_dp, qlanes[0]).astype(bf16)
+        tail = natural[:, qlanes[0] : qlanes[0] + qlanes[1]]
+        ib[...] = tail.reshape(in_local, n_dp, qlanes[1]).astype(bf16)
+        for ref, row in ((c1, 0), (h1, 1), (c2, 2), (h2, 3), (cs, 4), (hs, 3)):
+            ref[...] = vecs[row : row + 1, :]
+        for out in outs:
+            out.wait()
+
+    last = pl.pallas_call(
+        closing,
+        out_shape=[
+            jax.ShapeDtypeStruct((sizes[0], chan_part), bf16),
+            jax.ShapeDtypeStruct((sizes[1], chan_part), bf16),
+            jax.ShapeDtypeStruct((in_local, n_dp, qlanes[0]), bf16),
+            jax.ShapeDtypeStruct((in_local, n_dp, qlanes[1]), bf16),
+            jax.ShapeDtypeStruct((9, in_local, LANES), f32),
+            jax.ShapeDtypeStruct((9, out_rows, LANES), f32),
+            jax.ShapeDtypeStruct((in_local, LANES), f32),
+        ]
+        + [jax.ShapeDtypeStruct((1, LANES), f32)] * 6,
+        in_specs=[hbm] * 8,
+        out_specs=[hbm, hbm, vmem, vmem, hbm, hbm, hbm] + [vmem] * 6,
+        scratch_shapes=[V(o.shape, o.dtype) for o in mid_outs]
+        + [V((n_dp * in_local, n_dp * in_local), bf16), pltpu.SemaphoreType.DMA((13,))],
+        compiler_params=pltpu.CompilerParams(vmem_limit_bytes=60 * 2**20),
+        name="closing",
+    )
+    total_rows = n_dp * in_local
+    turn = np.zeros((total_rows, total_rows), np.float32)
+    for c in range(in_local):
+        for j in range(n_dp):
+            turn[c * n_dp + j, j * in_local + c] = 1.0
+    return main, last, turn.astype(jnp.bfloat16)
+
+
+STOP = 99
+
+
+def fused_body(
+    input_a, input_b, boxes_a, boxes_b, weight_first, weight_second, weight_short,
+    gain_first, shift_first, gain_second, shift_second, gain_short, shift_short,
+    upstream_a, upstream_b,
+):
+    n_dp = lax.axis_size("dp")
+    chan_part = weight_first.shape[2]
+    in_local = input_a.shape[0]
+    main, last, turn = make_fused(
+        n_dp, in_local, (boxes_a.shape[0], boxes_b.shape[0]), (SA, SB),
+        weight_first.shape[1], chan_part, STOP,
+    )
+    vectors = [
+        v.reshape(1, chan_part)
+        for v in (gain_first, shift_first, gain_second, shift_second, gain_short, shift_short)
+    ]
+    mid = main(
+        input_a, input_b, boxes_a.T, boxes_b.T, weight_first, weight_second, weight_short,
+        *vectors, upstream_a.T, upstream_b.T,
+    )
+    res = last(*mid, turn)
+    return (
+        res[0].T, res[1].T,
+        res[2].reshape(in_local, n_dp, 1, -1), res[3].reshape(in_local, n_dp, 1, -1),
+        res[4], res[5], res[6],
+    ) + tuple(v.reshape(chan_part) for v in res[7:])
+
+
+def choose_body(mesh):
+    return fused_body if mesh.shape["dp"] == 8 and mesh.shape["chan"] == 4 else plain_body
+
+
 def solution(mesh):
     placed = (
         P("dp", None),
@@ -378,7 +1288,7 @@
         P("chan", "dp"),
     )
     return jax.shard_map(
-        body,
+        choose_body(mesh),
         mesh=mesh,
         in_specs=placed,
         out_specs=(

time: 1140 us -> 115 us (0.10); the launches traced: 1120 us -> 114 us
  local copies, waits for them, and re-layouts: 695 us -> 0 us
  blocking collectives: 176 us -> 0 us
  waiting for transfers between devices: 151 us -> 0 us
  Pallas kernels: 0 us -> 114 us
  matrix products: 36.3 us -> 0 us
  other arithmetic: 29.2 us -> 0 us
  between operations: 17.1 us -> 0.82 us
  starting transfers between devices: 15.5 us -> 0 us
    slice x28 -> x0, local copies, waits for them, and re-layouts: 506 us -> none  [the longest x18 405 us: taps_strided(): padded[:, :, tap_row:tap_row + extent:2, tap_col:tap_col + extent:2]]
    pallas_call x0 -> x2, Pallas kernels: none -> 114 us  [the longest x1 111 us: fused_body(): main(input_a, input_b, boxes_a.T, boxes_b.T, weight_first, weight_second,...]
    psum x1 -> x0, waiting for transfers between devices: 90.8 us -> none  [body(): lax.psum((grad_first_local, grad_second_local, grad_short_local), 'dp')]
    all_to_all x1 -> x0, blocking collectives: 80.2 us -> none  [body(): lax.all_to_all(partial_inputs[0].astype(jnp.bfloat16), 'dp', split_axis=0...]
    psum x4 -> x0, blocking collectives: 80.2 us -> none  [the longest x2 40.6 us: body(): lax.psum((shift_tail, gain_tail, gain_side), 'dp')]
    squeeze x36 -> x0, local copies, waits for them, and re-layouts: 65.5 us -> none  [the longest x18 37.8 us: untaps_plain(): pieces[3 * tap_row + tap_col]]
    unnamed x232 -> x0, local copies, waits for them, and re-layouts: 51 us -> none
    dot_general x18 -> x0, matrix products: 36.3 us -> none  [the longest x6 14.9 us: weight_product(): lax.dot_general(columns, gradient, (((1,), (1,)), ((), ())), preferred_el...]
  transfers between devices with their start and end apart: 8 -> 0, of which waited for: 5 -> 0; matrix products, arithmetic and copies ran while one was open for 23% -> 0% of each run, Pallas kernels for 0% -> 0%
where the time goes in v2:
time: 115 us; the launch traced here: 114 us
  Pallas kernels  114 us (99%)
    pallas_call x1, Pallas kernels, fused_body(): main(input_a, input_b, boxes_a.T, boxes_b.T, weight_first, weight_second,...  111 us
    pallas_call x1, Pallas kernels, fused_body(): res = last(*mid, turn)  3 us

profile of v2, /device:TPU:0, one launch (start us, length us, event | category | flops | bytes accessed | tf_op | source)
XLA Modules:
  0.0 114.3 jit_solution(7692592097730537559)
XLA Ops:
  0.7 110.5 %block.1 = (bf16[784,128]{1,0:T(8,128)(2,1)}, bf16[288,128]{1,0:T(8,128)(2,1)}, bf16[8,32,1152]{2,1,0:T(8,128)(2,1)}, f32[9,32,128]{2,1,0:T(8,128)}, f32[32,128]...) custom-call(bf16[32,25088]{1,0:T(8,128)(2,1)} %refs_0_.1, bf16[32,9216]{1,0:T(8,128)(2,1)} %refs_1_.1, ...), custom_call_target="tpu_custom_call" | custom-call | tf_op jit(solution)/shard_map/block/pallas_call | solution.py:1256
  111.2 3.0 %closing.1 = (bf16[784,128]{1,0:T(8,128)(2,1)}, bf16[288,128]{1,0:T(8,128)(2,1)}, bf16[32,8,784]{2,1,0:T(8,128)(2,1)}, bf16[32,8,288]{2,1,0:T(8,128)(2,1)}, f32[...) custom-call(bf16[784,128]{1,0:T(8,128)(2,1)} %get-tuple-element.33.o, ...), custom_call_target="tpu_custom_call" | custom-call | tf_op jit(solution)/shard_map/closing/pallas_call | solution.py:1260

commit v3 on v2

--- a/solution.py
+++ b/solution.py
@@ -413,6 +413,35 @@
     return jnp.concatenate(parts, axis=1) if len(parts) > 1 else parts[0]
 
 
+def quarter_matrices(images, sides, segments, seg_lane, seg_row, q_rows, lanes):
+    def lane(g, image, row, col):
+        for (seg_g, r0, r1), first in zip(segments, seg_lane):
+            if seg_g == g and 2 * r0 <= row < 2 * r1:
+                return first + (image * 2 * (r1 - r0) + row - 2 * r0) * sides[g] + col
+
+    taps = np.zeros((9, q_rows, lanes), np.float32)
+    for (g, r0, r1), first in zip(segments, seg_row):
+        half = sides[g] // 2
+        for r in range(r0, r1):
+            for s in range(half):
+                for image in range(images[g]):
+                    target = first + ((r - r0) * half + s) * images[g] + image
+                    for t, (a, b) in enumerate(TAPS):
+                        row, col = 2 * r + a - 1, 2 * s + b - 1
+                        if row >= 0 and col >= 0:
+                            taps[t, target, lane(g, image, row, col)] = 1.0
+    sizes = [n * side * side for n, side in zip(images, sides)]
+    cells = np.zeros((sum(sizes), lanes), np.float32)
+    for g, (n, side) in enumerate(zip(images, sides)):
+        for image in range(n):
+            for row in range(side):
+                for col in range(side):
+                    cell = (row // 2) * (side // 2) + col // 2
+                    target = g * sizes[0] + (cell * 4 + 2 * (row % 2) + col % 2) * n + image
+                    cells[target, lane(g, image, row, col)] = 1.0
+    return taps, cells
+
+
 def regroup(value, runs):
     return jnp.concatenate([value[:, a:b] for a, b in runs], axis=1)
 
@@ -478,49 +507,61 @@
     rows = sum(sizes)
     quarter = tuple(n // 4 for n in images)
     qlanes = tuple(q * side * side for q, side in zip(quarter, sides))
-    n_parts = 3
-    step = -(-sum(qlanes) // (n_parts * LANES)) * LANES
-    slab_lanes = n_parts * step
-    b_tile = qlanes[0] // LANES * LANES
-    b_skip = qlanes[0] - b_tile
+    slab_lanes = -(-sum(qlanes) // LANES) * LANES
     chan_full = 4 * chan_part
     out_rows = chan_full // n_dp
     starts = (0, sizes[0])
-    chunks = [
-        (g, r, starts[g] + r * halves[g] * images[g], halves[g] * images[g])
-        for g in range(2)
-        for r in range(halves[g])
+    widths = tuple(h * n for h, n in zip(halves, images))
+    chunks = [(g, r, starts[g] + r * widths[g], widths[g]) for g in range(2) for r in range(halves[g])]
+    win = [-(-q // LANES) * LANES for q in qlanes]
+    b_tile = qlanes[0] // LANES * LANES
+    b_skip = qlanes[0] - b_tile
+    rs = halves[0] // 2
+    segments = [(1, 0, halves[1]), (0, 0, rs), (0, rs, halves[0])]
+    seg_lane, runs = [], []
+    lane_of = 0
+    for g, r0, r1 in segments:
+        side, base = sides[g], (0, qlanes[0])[g]
+        seg_lane.append(lane_of)
+        lane_of += quarter[g] * 2 * (r1 - r0) * side
+        runs += [
+            (base + (image * side + 2 * r0) * side, base + (image * side + 2 * r1) * side)
+            for image in range(quarter[g])
+        ]
+    runs.append((sum(qlanes), slab_lanes))
+    at, order = 0, []
+    for a, b in runs:
+        order.append((a, at, at + b - a))
+        at += b - a
+    back_runs = [(a, b) for _, a, b in sorted(order)]
+    cut_lane = -(-seg_lane[2] // LANES) * LANES
+    lane_parts = (slice(0, cut_lane), slice(cut_lane, slab_lanes))
+    seg_cells = [(r1 - r0) * halves[g] for g, r0, r1 in segments]
+    seg_rows = [cells * quarter[seg[0]] for cells, seg in zip(seg_cells, segments)]
+    top = -(-(seg_rows[0] + seg_rows[1]) // 16) * 16
+    seg_row = [0, seg_rows[0], top]
+    q_rows = top + -(-seg_rows[2] // 16) * 16
+    row_parts = (slice(0, top), slice(top, q_rows))
+    patch_win = (slice(0, cut_lane), slice(seg_lane[1] // LANES * LANES, slab_lanes))
+    patch_m, cells_m = quarter_matrices(
+        quarter, sides, segments, seg_lane, seg_row, q_rows, slab_lanes
+    )
+    patch_ms = [
+        np.concatenate([m[rows_, lanes_] for m in patch_m], axis=0)
+        for rows_, lanes_ in zip(row_parts, patch_win)
     ]
-    win = [-(-q // LANES) * LANES for q in qlanes]
-    part_chunks = [[] for _ in range(n_parts)]
-    for chunk in chunks:
-        part_chunks[n_parts - 1 if chunk[0] else -(-(chunk[2] + chunk[3]) // step) - 1].append(chunk)
-    spans = [(part[0][2], part[-1][2] + part[-1][3]) for part in part_chunks]
-    pieces = []
-    for part in part_chunks:
-        found = [[c for c in part if c[0] == g] for g in range(2)]
-        pieces.append([(g, f[0][1], f[-1][1] + 1) for g, f in enumerate(found) if f])
-    in_win = [(a // LANES * LANES, min(-(-b // LANES) * LANES, slab_lanes)) for a, b in spans]
-    out_win = []
-    for c in range(n_parts):
-        hit = [span for span in spans if span[0] < (c + 1) * step and span[1] > c * step]
-        out_win.append((hit[0][0], hit[-1][1]))
-    runs = []
-    for part in pieces:
-        for g, r0, r1 in part:
-            side, base = sides[g], (0, qlanes[0])[g]
-            runs += [
-                (base + (image * side + 2 * r0) * side, base + (image * side + 2 * r1) * side)
-                for image in range(quarter[g])
-            ]
-    runs.append((sum(qlanes), slab_lanes))
-    lane_of, order = 0, []
-    for a, b in runs:
-        order.append((a, lane_of, lane_of + b - a))
-        lane_of += b - a
-    back_runs = [(a, b) for _, a, b in sorted(order)]
-    split = halves[0] // 2 + 1
-    act_pieces = [(1, 0, halves[1]), (0, 0, split), (0, split, halves[0])]
+    spans = [
+        (starts[g] + r0 * widths[g], starts[g] + r1 * widths[g])
+        for g, r0, r1 in (segments[0], segments[2], segments[1])
+    ]
+    pieces = [[segments[0]], [segments[2]], [segments[1]]]
+    part_chunks = [
+        [ch for ch in chunks if ch[0] == p[0][0] and p[0][1] <= ch[1] < p[0][2]] for p in pieces
+    ]
+    low_lane = seg_lane[1] // LANES * LANES
+    out_lanes = [slice(0, low_lane), slice(cut_lane, slab_lanes), slice(low_lane, cut_lane)]
+    out_win = [spans[0], spans[1], (0, rows)]
+    n_parts = 3
     mid = (rows // 32 + 1) * 16
     row_halves = (slice(0, mid), slice(mid, rows))
     cols2 = (slice(0, 5 * LANES), slice(5 * LANES, 9 * LANES))
@@ -528,9 +569,11 @@
 
     def kernel(*refs):
         (xa_h, xb_h, bxa_h, bxb_h, w1_h, w2_h, ws_h, g1_h, b1_h, g2_h, b2_h, gs_h, bs_h, ua_h, ub_h,
+         pm0_h, pm1_h, cells_h,
          oa, ob, gr, gw1, gws, gw2, vecs,
-         xa, xb, bxa, bxb, w1, w2, ws, g1, b1, g2, b2, gs, bs, ua, ub, cells,
-         xs, xt, xr, zg, zpa, zpb, valid, z1, zs, a1a, a1b, slots, up, outr, gv, dza, dzb, dzsr,
+         xa, xb, bxa, bxb, w1g, w2, wsg, vg, g2, b2, gs, bs, ua, ub, pm0, pm1, cells,
+         xs, xt, xr, zb, zsq, zsr, zg, zpa, zpb, valid, vq, hat, mask, zs, a1a, a1b,
+         cslots, slots, stat, up, outr, gv, dza, dzb, dzsr,
          dd, hp, hr1, hs, hr2, gu, d1a, d1b,
          wg2, p21, p22, p23, p24, p25, wg1, p11, p12, p13, p14, p15,
          gp, gr1, gsum, gr2, zt, gt, lsem, ssem, rsem) = refs
@@ -550,9 +593,10 @@
         loads = {}
         pairs_of = (
             ("xa", xa_h, xa), ("xb", xb_h, xb),
-            ("bxa", bxa_h, bxa), ("bxb", bxb_h, bxb), ("ua", ua_h, ua), ("ub", ub_h, ub),
-            ("w1", w1_h, w1), ("ws", ws_h, ws), ("g1", g1_h, g1), ("b1", b1_h, b1), ("g2", g2_h, g2),
-            ("b2", b2_h, b2), ("gs", gs_h, gs), ("bs", bs_h, bs), ("w2", w2_h, w2),
+            ("w1", w1_h, w1g.at[k]), ("ws", ws_h, wsg.at[k]), ("g1", g1_h, vg.at[k, 0]), ("b1", b1_h, vg.at[k, 1]),
+            ("bxa", bxa_h, bxa), ("bxb", bxb_h, bxb), ("pm0", pm0_h, pm0), ("pm1", pm1_h, pm1),
+            ("ua", ua_h, ua), ("ub", ub_h, ub), ("g2", g2_h, g2),
+            ("b2", b2_h, b2), ("gs", gs_h, gs), ("bs", bs_h, bs), ("w2", w2_h, w2), ("cells", cells_h, cells),
         )
         for index, (name, source, target) in enumerate(pairs_of):
             loads[name] = pltpu.make_async_copy(source, target, lsem.at[index])
@@ -566,16 +610,9 @@
         barrier = pltpu.get_barrier_semaphore()
         for d in range(1, n_dp):
             pl.semaphore_signal(barrier, inc=1, device_id=((i + d) % n_dp, k), device_id_type=MESH)
-        pl.semaphore_signal(barrier, inc=1, device_id=(i, k1), device_id_type=MESH)
-        pl.semaphore_signal(barrier, inc=1, device_id=(i, k2), device_id_type=MESH)
-
-        if stop == -6:
-            need("xa", "xb")
-            for copy in loads.values():
-                copy.start()
-            pl.semaphore_wait(barrier, n_dp + 1)
-            need(*list(loads))
-            return net.drain()
+        for where in (k1, k2, k3):
+            pl.semaphore_signal(barrier, inc=1, device_id=(i, where), device_id_type=MESH)
+
         need("xa", "xb")
         for copy in loads.values():
             copy.start()
@@ -596,30 +633,37 @@
             xs[d * in_local : (d + 1) * in_local, :] = jnp.concatenate(
                 [part_a[:, :b_tile], seam, part_b[:, LANES : slab_lanes - b_tile]], axis=1
             ).astype(bf16)
-        if stop == -5:
-            pl.semaphore_wait(barrier, n_dp + 1)
-            need(*list(loads))
-            return net.drain()
-        slot_x = [net.slot(n_dp) for _ in range(n_parts)]
-        for c in range(n_parts):
-            cols = slice(c * step, (c + 1) * step)
-            if c == 0:
-                ordered = regroup(xs[...], runs)
+        slot_x = [net.slot(n_dp) for _ in lane_parts]
+        w_taps = (slice(0, 3), slice(3, 6), slice(6, 9))
+        slot_w = [net.slot(4) for _ in range(len(w_taps) + 2)]
+
+        def weight_refs(q):
+            return [w1g.at[q, taps] for taps in w_taps] + [wsg.at[q], vg.at[q]]
+
+        ordered = regroup(xs[...], runs)
+        for c, cols in enumerate(lane_parts):
             moved = ordered[:, cols]
-            xt[:, :, cols] = moved.reshape(n_dp, in_local, step)
+            xt[:, :, cols] = moved.reshape(n_dp, in_local, moved.shape[1])
             xr[i, :, cols] = moved[:in_local]
             if c == 0:
-                pl.semaphore_wait(barrier, n_dp + 1)
+                pl.semaphore_wait(barrier, n_dp + 2)
             for d in range(1, n_dp):
                 net.send(xt.at[d, :, cols], xr.at[i, :, cols], slot_x[c] + i, ((i + d) % n_dp, k))
-
-        if stop in (-3,-4):
-            for c in range(n_parts):
-                for d in range(1, n_dp):
-                    j = (i + d) % n_dp
-                    net.arrived(xr.at[j, :, c*step:(c+1)*step], slot_x[c] + j, (j, k))
-            need(*list(loads))
-            return net.drain()
+            if c == 0:
+                need("w1", "ws", "g1", "b1")
+                for where in (k2, k1):
+                    for ref, slot in zip(weight_refs(k), slot_w):
+                        net.send(ref, ref, slot + k, (i, where))
+
+        def weights_on(n):
+            ref = weight_refs(k2)[n]
+            net.arrived(ref, slot_w[n] + k2, (i, k2))
+            net.send(ref, ref, slot_w[n] + k2, (i, k1))
+
+        def weights_in():
+            for q in (k1, k3):
+                for ref, slot in zip(weight_refs(q), slot_w):
+                    net.arrived(ref, slot + q, (i, k1))
 
         for buf in (zpa, zpb, a1a, a1b, dza, dzb, d1a, d1b):
             side = buf.shape[1] if len(buf.shape) == 5 else buf.shape[0]
@@ -630,24 +674,46 @@
                     region[...] = jnp.zeros(region.shape, buf.dtype)
         need("bxa", "bxb", "ua", "ub")
         population = zeros(1)[0]
+        low = lax.broadcasted_iota(jnp.int32, (8, LANES), 0) < 4
         for g, box in enumerate((bxa, bxb)):
-            n, half = images[g], halves[g]
+            n, half, count = images[g], halves[g], quarter[g]
             diag = lax.broadcasted_iota(jnp.int32, (n, n), 0) == lax.broadcasted_iota(jnp.int32, (n, n), 1)
             ends = [
                 jnp.sum(jnp.where(diag, box[q : q + 1, :].astype(f32), 0.0), axis=1, keepdims=True)
                 for q in range(4)
             ]
-            inside = [
-                [((p >= ends[q]) & (p < ends[q] + ends[q + 2])).astype(f32) for p in range(half)]
-                for q in range(2)
-            ]
+            ends = [jnp.broadcast_to(e, (n, LANES)) for e in ends]
+            ends[2], ends[3] = ends[0] + ends[2], ends[1] + ends[3]
+
+            def inside(ends, r, s):
+                both = (r >= ends[0]) & (r < ends[2]) & (s >= ends[1]) & (s < ends[3])
+                return both.astype(f32)
+
             for r in range(half):
                 for s in range(half):
-                    cell = jnp.broadcast_to(inside[0][r] * inside[1][s], (n, LANES))
+                    cell = inside(ends, r, s)
                     begin = starts[g] + (r * half + s) * n
                     valid[begin : begin + n, :] = cell
                     population = population + jnp.sum(cell.reshape(n // 8, 8, LANES), axis=0)
-        population = jnp.sum(population, axis=0, keepdims=True)
+            mine = [pltpu.roll(e, (n - count * k) % n, 0)[:8] for e in ends]
+            if count < 8:
+                mine = [jnp.where(low, e, pltpu.roll(e, 4, 0)) for e in mine]
+            for (seg_g, r0, r1), first, cells_n in zip(segments, seg_row, seg_cells):
+                if seg_g != g:
+                    continue
+                per = 8 // count
+                for t in range(-(-cells_n // per)):
+                    spots = [divmod(min(per * t + e, cells_n - 1), half) for e in range(per)]
+                    spots = [(float(r0 + r), float(s)) for r, s in spots]
+                    if per == 2:
+                        r, s = (jnp.where(low, spots[0][e], spots[1][e]) for e in range(2))
+                    else:
+                        r, s = spots[0]
+                    cell = inside(mine, r, s)
+                    if per == 2 and per * t + 1 >= cells_n:
+                        cell = jnp.where(low, cell, 0.0)
+                    vq[first + 8 * t : first + 8 * t + 8, :] = cell
+        population = jnp.broadcast_to(jnp.sum(population, axis=0, keepdims=True), (8, LANES))
         for g, source in enumerate((ua, ub)):
             n, count = images[g], halves[g] ** 2
             gu[starts[g] : starts[g] + sizes[g], :] = source[...].astype(f32)
@@ -656,43 +722,220 @@
                     pl.ds(starts[g] + cell, n, stride=count), :
                 ]
 
-        lane = lax.broadcasted_iota(jnp.int32, (16, slab_lanes), 1)
-        for part, (a, b) in zip(pieces, spans):
-            for g, r0, r1 in part:
-                n, half, side, width = quarter[g], halves[g], sides[g], halves[g] * images[g]
-                for r in range(r0, r1):
-                    for begin in range(0, width, 16):
-                        at = begin + lax.broadcasted_iota(jnp.int32, (16, 1), 0)
-                        image, plane, s = at % n, (at // n) % 4, at // (4 * n)
-                        first = starts[g] + r0 * width + 2 * (r - r0) * side
-                        place = first + image * (2 * (r1 - r0) * side) + (plane // 2) * side + 2 * s + plane % 2
-                        row = starts[g] + r * width + begin
-                        cells[row : row + 16, :] = jnp.where(lane == place, 1.0, 0.0).astype(bf16)
-        slot_z = [net.slot(4) for _ in range(n_parts)]
-
-        if stop == -2:
-            for c in range(n_parts):
-                for d in range(1, n_dp):
-                    j = (i + d) % n_dp
-                    net.arrived(xr.at[j, :, c*step:(c+1)*step], slot_x[c] + j, (j, k))
-            need(*list(loads))
-            return net.drain()
-
-        def quarter_in(c):
-            lo, hi = c * step, (c + 1) * step
+        def rowsum(value):
+            return jnp.sum(value.reshape(-1, 8, value.shape[-1]), axis=0)
+
+        def message(sums):
+            parts = [jnp.sum(v, axis=0, keepdims=True) if v.shape[0] > 1 else v for v in sums]
+            if len(parts) % 8:
+                parts.append(jnp.zeros((8 - len(parts) % 8, LANES), f32))
+            return jnp.concatenate(parts, axis=0)
+
+        def by_chan(value):
+            return [value[:, q * LANES : (q + 1) * LANES] for q in range(4)]
+
+        def share(rnd, value):
+            mine = slots.at[rnd, i, : value.shape[0]]
+            mine[...] = value
+            first = net.slot(n_dp)
+            for d in range(1, n_dp):
+                net.send(mine, mine, first + i, ((i + d) % n_dp, k))
+            return first
+
+        def total(rnd, first, count=8):
             for d in range(1, n_dp):
                 j = (i + d) % n_dp
-                net.arrived(xr.at[j, :, lo:hi], slot_x[c] + j, (j, k))
-            (a, b), (lo, hi) = spans[c], in_win[c]
-            whole = jnp.concatenate([xr[q, :, lo:hi] for q in range(n_dp)], axis=0)
-            zg[k, a:b, :] = mm(cells[a:b, lo:hi], whole, 1, 1).astype(bf16)
+                net.arrived(slots.at[rnd, j, :count], first + j, (j, k))
+            return jnp.sum(slots[rnd, :, :count], axis=0)
+
+        def chan_share(rnd, value):
+            mine = cslots.at[rnd, k, : value.shape[0]]
+            mine[...] = value
+            first = net.slot(4)
+            for where in (k2, k3, k1):
+                net.send(mine, mine, first + k, (i, where))
+            return first
+
+        def chan_total(rnd, first, count=8):
+            for where in (k1, k2, k3):
+                net.arrived(cslots.at[rnd, where, :count], first + where, (i, where))
+            return jnp.sum(cslots[rnd, :, :count], axis=0)
+
+        pop_first = share(4, population)
+
+        def quarter_in(c):
+            for d in range(1, n_dp):
+                j = (i + d) % n_dp
+                net.arrived(xr.at[j, :, lane_parts[c]], slot_x[c] + j, (j, k))
+
+        def patches(c):
+            whole = jnp.concatenate([xr[q, :, patch_win[c]] for q in range(n_dp)], axis=0)
+            value = mm((pm0, pm1)[c][...], whole, 1, 1).astype(bf16)
+            count = value.shape[0] // 9
+            return [value[t * count : (t + 1) * count] for t in range(9)]
+
+        slot_z = [net.slot(4) for _ in row_parts]
+        slot_s = net.slot(4)
+
+        def first_conv(c, taps, acc):
+            part = row_parts[c]
+            weights = lanes_cat([w1g[q].reshape(9 * chan_in, chan_part) for q in range(4)])
+            value = mm(lanes_cat(taps), weights, 1, 0).astype(bf16)
+            zb[k, part, :] = value
             for where in (k2, k1):
-                net.send(zg.at[k, a:b], zg.at[k, a:b], slot_z[c] + k, (i, where))
-
-        def quarter_on(c):
-            a, b = spans[c]
-            net.arrived(zg.at[k2, a:b], slot_z[c] + k2, (i, k2))
-            net.send(zg.at[k2, a:b], zg.at[k2, a:b], slot_z[c] + k2, (i, k1))
+                net.send(zb.at[k, part], zb.at[k, part], slot_z[c] + k, (i, where))
+            side = mm(taps[4], lanes_cat([wsg[q] for q in range(4)]), 1, 0).astype(bf16)
+            ok = lanes_cat([vq[part, :]] * 4)
+            for n, z in enumerate((value, side)):
+                z = z.astype(f32)
+                u = z * ok
+                acc[2 * n] = acc[2 * n] + rowsum(u)
+                acc[2 * n + 1] = acc[2 * n + 1] + rowsum(u * z)
+            for q, z in enumerate(by_chan(side)):
+                zsq[q, part, :] = z
+            return acc
+
+        def act_on(c):
+            part = row_parts[c]
+            net.arrived(zb.at[k2, part], slot_z[c] + k2, (i, k2))
+            net.send(zb.at[k2, part], zb.at[k2, part], slot_z[c] + k2, (i, k1))
+
+        def act_in(c):
+            part = row_parts[c]
+            net.arrived(zb.at[k1, part], slot_z[c] + k1, (i, k1))
+            net.arrived(zb.at[k3, part], slot_z[c] + k3, (i, k1))
+
+        acc = [jnp.zeros((8, chan_full), f32)] * 4
+        need("pm0", "pm1")
+        weights_on(0)
+        weights_on(1)
+        quarter_in(0)
+        taps = patches(0)
+        for n in range(2, 5):
+            weights_on(n)
+        weights_in()
+        acc = first_conv(0, taps, acc)
+        quarter_in(1)
+        acc = first_conv(1, patches(1), acc)
+        acc = [jnp.sum(v, axis=0, keepdims=True) for v in acc]
+        first = chan_share(0, message(sum((by_chan(v) for v in acc), [])))
+        for where in (k2, k3, k1):
+            net.send(zsq.at[where], zsr.at[k], slot_s + k, (i, where))
+        zsr[k] = zsq[k]
+        act_on(0)
+        value = chan_total(0, first, 16)
+        first = share(0, value)
+        act_on(1)
+        need(*list(loads))
+        inv_pop = 1.0 / total(4, pop_first)[0:1]
+        act_in(0)
+        tot = total(0, first, 16)
+        stat[...] = tot
+        tot_first = (stat[pl.ds(k, 1), :], stat[pl.ds(4 + k, 1), :])
+        if stop == 3:
+            act_in(1)
+            for where in (k2, k3, k1):
+                net.arrived(zsr.at[where], slot_s + where, (i, where))
+            valid[0:1, :] = inv_pop
+            return net.drain()
+
+        def moments(total_, square):
+            mean = total_ * inv_pop
+            return mean, lax.rsqrt(square * inv_pop - mean * mean + epsilon)
+
+        mean1, sc1 = moments(tot[0:4], tot[4:8])
+        mean1, sc1 = (lanes_cat([v[q : q + 1] for q in range(4)]) for v in (mean1, sc1))
+        gain1, shift1 = (lanes_cat([vg[q, e] for q in range(4)]) for e in range(2))
+
+        turn_low = lax.broadcasted_iota(jnp.int32, (8, 1), 0) < 4
+
+        def whole_cells(read, c):
+            for begin in range(row_parts[c].start, row_parts[c].stop, 16):
+                blocks = [read(q, slice(begin, begin + 16)).astype(f32) for q in range(4)]
+                for at in (begin, begin + 8):
+                    seg = max(e for e in range(3) if seg_row[e] <= at)
+                    g, r0, r1 = segments[seg]
+                    per = 8 // quarter[g]
+                    v = [block[at - begin : at - begin + 8] for block in blocks]
+                    cell = (at - seg_row[seg]) // 8 * per
+                    if per == 1:
+                        found = [jnp.concatenate(v, axis=0)]
+                    else:
+                        t = [pltpu.roll(e, 4, 0) for e in v]
+                        found = [
+                            jnp.concatenate(
+                                [jnp.where(turn_low, v[0], t[1]), jnp.where(turn_low, v[2], t[3])], axis=0
+                            ),
+                            jnp.concatenate(
+                                [jnp.where(turn_low, t[0], v[1]), jnp.where(turn_low, t[2], v[3])], axis=0
+                            ),
+                        ]
+                    for e, value in enumerate(found):
+                        if cell + e < seg_cells[seg]:
+                            r, s = divmod(cell + e, halves[g])
+                            yield g, r0 + r, s, value
+
+        def activate(c):
+            for g, r, s, z in whole_cells(lambda q, span: zb[q, span, :], c):
+                begin = starts[g] + (r * halves[g] + s) * images[g]
+                span = slice(begin, begin + images[g])
+                h = (z - mean1) * sc1
+                hat[span, :] = h
+                v = h * gain1 + shift1
+                act = v * sigma(v) * lanes_cat([valid[span, :]] * 4)
+                a1[g][1 + r, 1 + s] = act.astype(bf16)
+
+        def second_conv(parts, acc):
+            value = None
+            for a, b in TAPS:
+                patch = jnp.concatenate(
+                    [flat(a1[g][r0 + a : r1 + a, b : b + halves[g]]) for g, r0, r1 in parts], axis=0
+                )
+                part = mm(patch, w2[3 * a + b], 1, 0)
+                value = part if value is None else value + part
+            at = 0
+            for g, r0, r1 in parts:
+                for r in range(r0, r1):
+                    begin = starts[g] + r * widths[g]
+                    span = slice(begin, begin + widths[g])
+                    u = value[at : at + widths[g]]
+                    at += widths[g]
+                    gv[span, :] = u
+                    uv = u * valid[span, :]
+                    acc = [acc[0] + rowsum(uv), acc[1] + rowsum(uv * u)]
+            return acc
+
+        activate(0)
+        acc = second_conv([(1, 0, halves[1]), (0, 0, rs - 1)], zeros(2))
+        act_in(1)
+        activate(1)
+        acc = second_conv([(0, rs - 1, halves[0])], acc)
+        first = share(1, message(acc))
+
+        for where in (k2, k3, k1):
+            net.arrived(zsr.at[where], slot_s + where, (i, where))
+        means, scs = moments(stat[pl.ds(8 + k, 1), :], stat[pl.ds(12 + k, 1), :])
+        for c in range(2):
+            for g, r, s, z in whole_cells(lambda q, span: zsr[q, span, :], c):
+                begin = starts[g] + (r * halves[g] + s) * images[g]
+                zs[begin : begin + images[g], :] = (z - means) * scs
+        row_cuts = (slice(0, rows // 32 * 16), slice(rows // 32 * 16, rows))
+        slot_g0 = [net.slot(4) for _ in row_cuts]
+        whole = jnp.concatenate([xr[q] for q in range(n_dp)], axis=0)
+        for span, slot in zip(row_cuts, slot_g0):
+            zg[k, span, :] = mm(cells[span, :], whole, 1, 1).astype(bf16)
+            for where in (k2, k1):
+                net.send(zg.at[k, span], zg.at[k, span], slot + k, (i, where))
+
+        def slab_on(n):
+            span, slot = row_cuts[n], slot_g0[n]
+            net.arrived(zg.at[k2, span], slot + k2, (i, k2))
+            net.send(zg.at[k2, span], zg.at[k2, span], slot + k2, (i, k1))
+
+        def slab_in(n):
+            span, slot = row_cuts[n], slot_g0[n]
+            net.arrived(zg.at[k1, span], slot + k1, (i, k1))
+            net.arrived(zg.at[k3, span], slot + k3, (i, k1))
 
         def planes_of(quarters, g):
             count = quarter[g]
@@ -714,163 +957,23 @@
                 result.append(jnp.concatenate(both, axis=1))
             return result
 
-        def strided_patch(c, tap):
-            a, b = tap
-            p = 2 * (a % 2 == 0) + (b % 2 == 0)
-            r, s = 1 - (a == 0), 1 - (b == 0)
-            return jnp.concatenate(
-                [flat(zp[g][p, r0 + r : r1 + r, s : s + halves[g]]) for g, r0, r1 in pieces[c]], axis=0
-            )
-
-        def rowsum(value):
-            return jnp.sum(value.reshape(-1, 8, LANES), axis=0)
-
-        def first_conv(c, acc):
-            a, b = spans[c]
-            net.arrived(zg.at[k1, a:b], slot_z[c] + k1, (i, k1))
-            net.arrived(zg.at[k3, a:b], slot_z[c] + k3, (i, k1))
-            for g, r, begin, count in part_chunks[c]:
+        def make_planes():
+            for g, r, begin, count in chunks:
                 quarters = [
                     zg[q, begin : begin + count, :].astype(f32).reshape(halves[g], images[g], chan_in)
                     for q in range(4)
                 ]
                 for p, value in enumerate(planes_of(quarters, g)):
                     zp[g][p, 1 + r, 1 : 1 + halves[g]] = value.astype(bf16)
-            both = mm(strided_patch(c, (1, 1)), jnp.concatenate([w1[4], ws[...]], axis=1), 1, 0)
-            zs[a:b, :] = both[:, chan_part:]
-            value = both[:, :chan_part]
-            for tap in TAPS:
-                if tap != (1, 1):
-                    value = value + mm(strided_patch(c, tap), w1[3 * tap[0] + tap[1]], 1, 0)
-            z1[a:b, :] = value
-            for g, r, begin, count in part_chunks[c]:
-                span = slice(begin, begin + count)
-                ok = valid[span, :]
-                u, w = z1[span, :], zs[span, :]
-                uv, wv = u * ok, w * ok
-                acc = [
-                    acc[0] + rowsum(uv), acc[1] + rowsum(uv * u),
-                    acc[2] + rowsum(wv), acc[3] + rowsum(wv * w),
-                ]
-            return acc
-
-        acc = zeros(4)
-        for c in range(n_parts):
-            quarter_in(c)
-            if c >= 1:
-                quarter_on(c - 1)
-        if stop == 1:
-            quarter_on(n_parts - 1)
-            for c in range(n_parts):
-                net.arrived(zg.at[k1, spans[c][0]:spans[c][1]], slot_z[c] + k1, (i, k1))
-                net.arrived(zg.at[k3, spans[c][0]:spans[c][1]], slot_z[c] + k3, (i, k1))
-            need(*list(loads))
-            return net.drain()
-        need("w1", "ws")
-        for c in range(n_parts):
-            if c == 1:
-                quarter_on(n_parts - 1)
-            acc = first_conv(c, acc)
-
-        def message(sums):
-            parts = [jnp.sum(v, axis=0, keepdims=True) if v.shape[0] > 1 else v for v in sums]
-            parts.append(jnp.zeros((8 - len(parts), LANES), f32))
-            return jnp.concatenate(parts, axis=0)
-
-        def share(rnd, value):
-            slots[rnd, i] = value
-            first = net.slot(n_dp)
-            for d in range(1, n_dp):
-                net.send(slots.at[rnd, i], slots.at[rnd, i], first + i, ((i + d) % n_dp, k))
-            return first
-
-        def total(rnd, first):
-            for d in range(1, n_dp):
-                j = (i + d) % n_dp
-                net.arrived(slots.at[rnd, j], first + j, (j, k))
-            return jnp.sum(slots[rnd], axis=0)
-
-        if stop == 2:
-            valid[0:8, :] = acc[0] + acc[1] + acc[2] + acc[3]
-            need(*list(loads))
-            return net.drain()
-        first = share(0, message(acc + [population]))
-        need(*list(loads))
-        tot = total(0, first)
-        inv_pop = 1.0 / tot[4:5]
-        mean1, means = tot[0:1] * inv_pop, tot[2:3] * inv_pop
-        sc1 = lax.rsqrt(tot[1:2] * inv_pop - mean1 * mean1 + epsilon)
-        scs = lax.rsqrt(tot[3:4] * inv_pop - means * means + epsilon)
-        gain1, shift1 = g1[...], b1[...]
-        if stop == 3:
-            valid[0:1, :] = sc1 + scs
-            return net.drain()
-
-        def act_ref(piece, q):
-            g, r0, r1 = piece
-            return a1[g].at[q, 1 + r0 : 1 + r1, 1 : 1 + halves[g]]
-
-        slot_a = [net.slot(4) for _ in act_pieces]
-        for piece, slot in zip(act_pieces, slot_a):
-            for g, r, begin, count in chunks:
-                if g == piece[0] and piece[1] <= r < piece[2]:
-                    span = slice(begin, begin + count)
-                    hat = (z1[span, :] - mean1) * sc1
-                    z1[span, :] = hat
-                    v = hat * gain1 + shift1
-                    act = (v * sigma(v) * valid[span, :]).astype(bf16)
-                    a1[g][k, 1 + r, 1 : 1 + halves[g]] = act.reshape(halves[g], images[g], chan_part)
-            for where in (k2, k1):
-                net.send(act_ref(piece, k), act_ref(piece, k), slot + k, (i, where))
-
-        def act_on(n):
-            piece, slot = act_pieces[n], slot_a[n]
-            net.arrived(act_ref(piece, k2), slot + k2, (i, k2))
-            net.send(act_ref(piece, k2), act_ref(piece, k2), slot + k2, (i, k1))
-
-        def act_in(n):
-            piece, slot = act_pieces[n], slot_a[n]
-            net.arrived(act_ref(piece, k1), slot + k1, (i, k1))
-            net.arrived(act_ref(piece, k3), slot + k3, (i, k1))
-
-        def second_conv(piece, acc):
-            g, r0, r1 = piece
-            width = halves[g] * images[g]
-            begin, end = starts[g] + r0 * width, starts[g] + r1 * width
-            value = None
-            for a, b in TAPS:
-                patch = lanes_cat(
-                    [flat(a1[g][q, r0 + a : r1 + a, b : b + halves[g]]) for q in range(4)]
-                )
-                part = mm(patch, w2[3 * a + b], 1, 0)
-                value = part if value is None else value + part
-            gv[begin:end, :] = value
-            for row in range(begin, end, width):
-                span = slice(row, row + width)
-                u = gv[span, :]
-                uv = u * valid[span, :]
-                acc = [acc[0] + rowsum(uv), acc[1] + rowsum(uv * u)]
-            return acc
-
-        acc = zeros(2)
-        act_on(0)
-        act_in(0)
-        acc = second_conv((1, 0, halves[1]), acc)
-        act_on(1)
-        act_in(1)
-        acc = second_conv((0, 0, split - 1), acc)
-        act_on(2)
-        act_in(2)
-        acc = second_conv((0, split - 1, halves[0]), acc)
-        first = share(1, message(acc))
-        for g, r, begin, count in chunks:
-            span = slice(begin, begin + count)
-            zs[span, :] = (zs[span, :] - means) * scs
+
         tot = total(1, first)
-        mean2 = tot[0:1] * inv_pop
-        sc2 = lax.rsqrt(tot[1:2] * inv_pop - mean2 * mean2 + epsilon)
+        mean2, sc2 = moments(tot[0:1], tot[1:2])
         if stop == 5:
             valid[0:1, :] = sc2
+            for n in range(2):
+                slab_on(n)
+            for n in range(2):
+                slab_in(n)
             return net.drain()
         gain2, gains = g2[...], gs[...]
         shifts = b2[...] + bs[...]
@@ -895,10 +998,19 @@
                     starts[g] + cell * n : starts[g] + (cell + 1) * n, :
                 ]
             target[...] = gu[starts[g] : starts[g] + sizes[g], :].astype(bf16)
+        for begin in range(0, rows, 16):
+            span = slice(begin, begin + 16)
+            v = hat[span, :] * gain1 + shift1
+            sig = sigma(v)
+            mask[span, :] = sig * (1.0 + v * (1.0 - sig)) * lanes_cat([valid[span, :]] * 4)
         tot = total(2, first)
         sum_tail, sum_gain2, sum_gains = tot[0:1], tot[1:2], tot[2:3]
         if stop == 6:
             valid[0:1, :] = sum_tail
+            for n in range(2):
+                slab_on(n)
+            for n in range(2):
+                slab_in(n)
             return net.drain()
 
         k2g, ksg = gain2 * sc2, gains * scs
@@ -932,36 +1044,34 @@
         for span, slot in zip(row_halves, slot_h):
             net.send(hp.at[k1, span], hr1.at[0, span], slot, (i, k1))
 
-        acts = [
-            lanes_cat([flat(a1[g][q, 1 : 1 + halves[g], 1 : 1 + halves[g]]) for q in range(4)])
-            for g in range(2)
-        ]
+        acc = [jnp.zeros((8, chan_full), f32)] * 2
+        for begin in range(0, rows, 16):
+            span = slice(begin, begin + 16)
+            part = lanes_cat([hp[q, span, :] for q in range(4)]).astype(f32) * mask[span, :]
+            acc = [acc[0] + rowsum(part), acc[1] + rowsum(part * hat[span, :])]
+        acc = [jnp.sum(v, axis=0, keepdims=True) for v in acc]
+        first = chan_share(1, message(sum((by_chan(v) for v in acc), [])))
+
+        acts = [flat(a1[g][1 : 1 + halves[g], 1 : 1 + halves[g]]) for g in range(2)]
         sum2 = Reduce(net, i, k, wg2, (p21, p22, p23, p24, p25), cols2)
         for w, cols in enumerate(cols2):
             value = mm(acts[0], dd[: sizes[0], cols], 0, 0) + mm(acts[1], dd[sizes[0] :, cols], 0, 0)
             wg2[:, :, :, :, cols] = value.astype(bf16).reshape(2, 2, 2, out_rows, value.shape[1])
             sum2.first(w)
+            if w == 0:
+                first = share(3, chan_total(1, first))
         for g, r, begin, count in chunks:
             span = slice(begin, begin + count)
             value = ksg * (up[span, :] - valid[span, :] * (db + zs[span, :] * dgs))
             dzsr[span, :] = value.astype(bf16)
-        acc = zeros(2)
-        for n, (span, slot) in enumerate(zip(row_halves, slot_h)):
-            net.arrived(hr1.at[0, span], slot, (i, k1))
-            net.arrived(hr2.at[span], slot + 2, (i, k2))
-            for begin in range(span.start, span.stop, 16):
-                part = slice(begin, begin + 16)
-                hat = z1[part, :]
-                v = hat * gain1 + shift1
-                sig = sigma(v)
-                grad = hp[k, part, :].astype(f32) + hr1[0, part, :].astype(f32) + hr2[part, :].astype(f32)
-                grad = grad * valid[part, :] * (sig * (1.0 + v * (1.0 - sig)))
-                gu[part, :] = grad
-                acc = [acc[0] + rowsum(grad), acc[1] + rowsum(grad * hat)]
-        first = share(3, message(acc))
-        sum2.second(0)
+        for n in range(2):
+            slab_on(n)
+        for n in range(2):
+            slab_in(n)
+        make_planes()
         tot = total(3, first)
-        sum_head, sum_gain1 = tot[0:1], tot[1:2]
+        stat[0:8, :] = tot
+        sum_head, sum_gain1 = stat[pl.ds(k, 1), :], stat[pl.ds(4 + k, 1), :]
 
         def close_second():
             for w, cols in enumerate(cols2):
@@ -969,19 +1079,31 @@
                 for t in range(cols.start // LANES, cols.stop // LANES):
                     gw2[t] = value[:, t * LANES - cols.start : (t + 1) * LANES - cols.start]
 
+        own = pl.ds(pl.multiple_of(k * chan_part, LANES), chan_part)
+        mean1, sc1 = moments(tot_first[0], tot_first[1])
+        k1g = vg[k, 0] * sc1
+        db, dg1 = sum_head * inv_pop, sum_gain1 * inv_pop
+        per_cell = [(g, r, s) for g in range(2) for r in range(halves[g]) for s in range(halves[g])]
+        waiting = list(zip(row_halves, slot_h))
+        for g, r, s in per_cell:
+            begin = starts[g] + (r * halves[g] + s) * images[g]
+            part = slice(begin, begin + images[g])
+            while waiting and waiting[0][0].start < part.stop:
+                span, slot = waiting.pop(0)
+                net.arrived(hr1.at[0, span], slot, (i, k1))
+                net.arrived(hr2.at[span], slot + 2, (i, k2))
+            grad = hp[k, part, :].astype(f32) + hr1[0, part, :].astype(f32) + hr2[part, :].astype(f32)
+            grad = grad * mask[part, own]
+            value = k1g * (grad - valid[part, :] * (db + hat[part, own] * dg1))
+            d1[g][r, s] = value.astype(bf16)
         if stop == 8:
             valid[0:1, :] = sum_head
-            sum2.second(1)
+            for w in range(2):
+                sum2.second(w)
             for w in range(2):
                 sum2.third(w)
             close_second()
             return net.drain()
-        k1g = gain1 * sc1
-        db, dg1 = sum_head * inv_pop, sum_gain1 * inv_pop
-        for g, r, begin, count in chunks:
-            span = slice(begin, begin + count)
-            value = k1g * (gu[span, :] - valid[span, :] * (db + z1[span, :] * dg1))
-            d1[g][r, : halves[g]] = value.astype(bf16).reshape(halves[g], images[g], chan_part)
 
         def back_patch(pieces, p):
             parts = []
@@ -1002,9 +1124,9 @@
             a, b = spans[c]
             planes = []
             for p in range(4):
-                weights = [w1[3 * ta + tb] for ta, tb in PLANE_TAPS[p]]
+                weights = [w1g[k, 3 * ta + tb] for ta, tb in PLANE_TAPS[p]]
                 if p == 0:
-                    weights.append(ws[...])
+                    weights.append(wsg[k])
                 planes.append(mm(back_patch(pieces[c], p), lanes_cat(weights), 1, 1))
             for g, r, begin, count in part_chunks[c]:
                 values = [
@@ -1035,10 +1157,10 @@
                 span = slice(begin, begin + 16)
                 value = gp[k, span, :].astype(f32) + gr1[0, span, :].astype(f32)
                 zt[span, :] = (value + gr2[span, :].astype(f32)).astype(bf16)
-            cols = slice(c * step, (c + 1) * step)
+            cols = out_lanes[c]
             a, b = out_win[c]
             value = mm(zt[a:b, :], cells[a:b, cols], 0, 0).astype(bf16)
-            gt[:, :, cols] = value.reshape(n_dp, in_local, step)
+            gt[:, :, cols] = value.reshape(n_dp, in_local, value.shape[1])
             for d in range(1, n_dp):
                 j = (i + d) % n_dp
                 net.send(gt.at[j, :, cols], gr.at[i, :, cols], slot_o[c] + i, (j, k))
@@ -1057,24 +1179,24 @@
             wg1[...] = lanes_cat(blocks).reshape(2, 2, 2, in_local, 10 * LANES)
             sum1.first(0)
 
-        order = list(reversed(range(n_parts)))
-        for n, c in enumerate(order):
-            back_first(c)
-            if n >= 1:
-                back_cross(order[n - 1])
-        back_cross(order[-1])
+        back_first(0)
+        back_first(1)
+        back_cross(0)
+        sum2.second(0)
+        back_first(2)
+        back_cross(1)
+        back_cross(2)
         weight_first()
         sum2.second(1)
+        back_out(0)
         sum2.third(0)
-        for n, c in enumerate(order):
-            back_out(c)
-            if n == 0:
-                sum2.third(1)
-            if n == 1:
-                sum1.second(0)
+        back_out(1)
+        sum2.third(1)
+        sum1.second(0)
+        back_out(2)
         sum1.third(0)
-        own = pltpu.make_async_copy(gt.at[i], gr.at[i], lsem.at[len(pairs_of)])
-        own.start()
+        kept = pltpu.make_async_copy(gt.at[i], gr.at[i], lsem.at[len(pairs_of)])
+        kept.start()
         close_second()
         value = sum1.last(0)
         for t, tap in enumerate(TAPS):
@@ -1084,11 +1206,11 @@
         gws[...] = value[:, LANES : 2 * LANES]
         vecs[...] = message([sum_gain1, sum_head, sum_gain2, sum_tail, sum_gains])
         for c in range(n_parts):
-            cols = slice(c * step, (c + 1) * step)
+            cols = out_lanes[c]
             for d in range(1, n_dp):
                 j = (i + d) % n_dp
                 net.arrived(gr.at[j, :, cols], slot_o[c] + j, (j, k))
-        own.wait()
+        kept.wait()
         net.drain()
 
     V = pltpu.VMEM
@@ -1104,24 +1226,31 @@
     inputs = [
         V((in_local, n_dp * 4 * qlanes[0]), bf16), V((in_local, n_dp * 4 * qlanes[1]), bf16),
         V((4, images[0]), jnp.int32), V((4, images[1]), jnp.int32),
-        V((9, chan_in, chan_part), bf16), V((9, chan_full, chan_part), bf16), V((chan_in, chan_part), bf16),
-    ] + [V((1, chan_part), f32)] * 6 + [
+        V((4, 9, chan_in, chan_part), bf16), V((9, chan_full, chan_part), bf16),
+        V((4, chan_in, chan_part), bf16), V((4, 2, 1, chan_part), f32),
+    ] + [V((1, chan_part), f32)] * 4 + [
         V((sizes[0], chan_part), bf16), V((sizes[1], chan_part), bf16),
-    ]
+    ] + [V(m.shape, bf16) for m in patch_ms] + [V((rows, slab_lanes), bf16)]
     scratch = inputs + [
-        V((rows, slab_lanes), bf16),
         V((n_dp * in_local, slab_lanes), bf16),
         V((n_dp, in_local, slab_lanes), bf16),
         V((n_dp, in_local, slab_lanes), bf16),
+        V((4, q_rows, chan_full), bf16),
+        V((4, q_rows, chan_part), bf16),
+        V((4, q_rows, chan_part), bf16),
         V((4, rows, chan_in), bf16),
         V((4,) + half_pads[0] + (chan_in,), bf16),
         V((4,) + half_pads[1] + (chan_in,), bf16),
         V((rows, LANES), f32),
+        V((q_rows, LANES), f32),
+        V((rows, chan_full), f32),
+        V((rows, chan_full), f32),
         V((rows, chan_part), f32),
-        V((rows, chan_part), f32),
-        V((4,) + pads[0], bf16),
-        V((4,) + pads[1], bf16),
-        V((4, n_dp, 8, LANES), f32),
+        V(pads[0][:3] + (chan_full,), bf16),
+        V(pads[1][:3] + (chan_full,), bf16),
+        V((2, 4, 16, LANES), f32),
+        V((5, n_dp, 16, LANES), f32),
+        V((16, LANES), f32),
         V((rows, chan_part), f32),
         V((rows, chan_part), f32),
         V((rows, chan_part), f32),
@@ -1145,9 +1274,9 @@
         V((rows, chan_in), bf16),
         V((rows, chan_in), bf16),
         V((n_dp, in_local, slab_lanes), bf16),
-        pltpu.SemaphoreType.DMA((len(inputs) + 1,)),
-        pltpu.SemaphoreType.DMA((160,)),
-        pltpu.SemaphoreType.DMA((160,)),
+        pltpu.SemaphoreType.DMA((19,)),
+        pltpu.SemaphoreType.DMA((192,)),
+        pltpu.SemaphoreType.DMA((192,)),
     ]
     mid_outs = [
         jax.ShapeDtypeStruct((sizes[0], chan_part), bf16),
@@ -1163,7 +1292,7 @@
     main = pl.pallas_call(
         kernel,
         out_shape=mid_outs,
-        in_specs=[hbm] * len(inputs),
+        in_specs=[hbm] * 18,
         out_specs=[vmem, vmem, hbm, vmem, vmem, vmem, vmem],
         scratch_shapes=scratch,
         compiler_params=pltpu.CompilerParams(
@@ -1231,7 +1360,7 @@
     for c in range(in_local):
         for j in range(n_dp):
             turn[c * n_dp + j, j * in_local + c] = 1.0
-    return main, last, turn.astype(jnp.bfloat16)
+    return (main, last) + tuple(m.astype(jnp.bfloat16) for m in (turn, *patch_ms, cells_m))
 
 
 STOP = 99
@@ -1245,7 +1374,7 @@
     n_dp = lax.axis_size("dp")
     chan_part = weight_first.shape[2]
     in_local = input_a.shape[0]
-    main, last, turn = make_fused(
+    main, last, turn, *matrices = make_fused(
         n_dp, in_local, (boxes_a.shape[0], boxes_b.shape[0]), (SA, SB),
         weight_first.shape[1], chan_part, STOP,
     )
@@ -1255,7 +1384,7 @@
     ]
     mid = main(
         input_a, input_b, boxes_a.T, boxes_b.T, weight_first, weight_second, weight_short,
-        *vectors, upstream_a.T, upstream_b.T,
+        *vectors, upstream_a.T, upstream_b.T, *matrices,
     )
     res = last(*mid, turn)
     return (

time: 115 us -> 107 us (0.930)
  Pallas kernels: 114 us -> 106 us
    pallas_call x1, Pallas kernels: 111 us -> 103 us  [fused_body(): main(input_a, input_b, boxes_a.T, boxes_b.T, weight_first, weight_second,...]
where the time goes in v3:
time: 107 us
  Pallas kernels  106 us (99%)
    pallas_call x1, Pallas kernels, fused_body(): main(input_a, input_b, boxes_a.T, boxes_b.T, weight_first, weight_second,...  103 us
    pallas_call x1, Pallas kernels, fused_body(): res = last(*mid, turn)  3 us

profile of v3, /device:TPU:0, one launch (start us, length us, event | category | flops | bytes accessed | tf_op | source)
XLA Modules:
  0.0 107.1 jit_solution(16981383380920282014)
XLA Ops:
  0.7 103.3 %block.1 = (bf16[784,128]{1,0:T(8,128)(2,1)}, bf16[288,128]{1,0:T(8,128)(2,1)}, bf16[8,32,1152]{2,1,0:T(8,128)(2,1)}, f32[9,32,128]{2,1,0:T(8,128)}, f32[32,128]...) custom-call(bf16[32,25088]{1,0:T(8,128)(2,1)} %refs_0_.1, bf16[32,9216]{1,0:T(8,128)(2,1)} %refs_1_.1, ...), custom_call_target="tpu_custom_call" | custom-call | tf_op jit(solution)/shard_map/block/pallas_call | solution.py:1385
  104.0 3.0 %closing.1 = (bf16[784,128]{1,0:T(8,128)(2,1)}, bf16[288,128]{1,0:T(8,128)(2,1)}, bf16[32,8,784]{2,1,0:T(8,128)(2,1)}, bf16[32,8,288]{2,1,0:T(8,128)(2,1)}, f32[...) custom-call(bf16[784,128]{1,0:T(8,128)(2,1)} %get-tuple-element.33.o, ...), custom_call_target="tpu_custom_call" | custom-call | tf_op jit(solution)/shard_map/closing/pallas_call | solution.py:1389

commit v4 on v3

--- a/solution.py
+++ b/solution.py
@@ -451,7 +451,8 @@
 
 
 class Reduce:
-    def __init__(self, net, i, k, part, bufs, windows):
+    def __init__(self, net, i, k, part, bufs, windows, b4=None):
+        self.b4 = b4
         self.net, self.part, self.windows = net, part, windows
         self.b1, self.s1, self.b2, self.s2, self.b3 = bufs
         self.ix, self.pz, self.hz = i % 2, (i // 2) % 2, i // 4
@@ -481,6 +482,36 @@
             self.s1.at[:, 1 - self.pz, :, cols], self.b2.at[:, :, cols],
             self.slots[w] + 1, self.peers[1],
         )
+
+    def second_of(self, w, value):
+        cols = self.windows[w]
+        self.s1[:, :, :, cols] = value.reshape(2, 2, -1, value.shape[1])
+        self.net.send(
+            self.s1.at[:, 1 - self.pz, :, cols], self.b2.at[:, :, cols],
+            self.slots[w] + 1, self.peers[1],
+        )
+
+    def spread_of(self, w, value):
+        cols = self.windows[w]
+        self.s1[:, :, :, cols] = value.reshape(2, 2, -1, value.shape[1])
+        z = 2 * self.hz + self.pz
+        self.direct = self.net.slot(4)
+        for d in range(1, 4):
+            to = (z + d) % 4
+            self.net.send(
+                self.s1.at[to // 2, to % 2, :, cols], self.b4.at[z],
+                self.direct + z, (2 * to + self.ix, self.peers[0][1]),
+            )
+
+    def spread_last(self, w):
+        cols = self.windows[w]
+        z = 2 * self.hz + self.pz
+        value = self.s1[self.hz, self.pz, :, cols].astype(jnp.float32)
+        for d in range(1, 4):
+            to = (z + d) % 4
+            self.net.arrived(self.b4.at[to], self.direct + to, (2 * to + self.ix, self.peers[0][1]))
+            value = value + self.b4[to].astype(jnp.float32)
+        return value
 
     def third(self, w):
         cols = self.windows[w]
@@ -565,24 +596,28 @@
     mid = (rows // 32 + 1) * 16
     row_halves = (slice(0, mid), slice(mid, rows))
     cols2 = (slice(0, 5 * LANES), slice(5 * LANES, 9 * LANES))
-    cols1 = (slice(0, 10 * LANES),)
+    cols1 = (slice(6 * LANES, 10 * LANES), slice(0, 6 * LANES))
 
     def kernel(*refs):
         (xa_h, xb_h, bxa_h, bxb_h, w1_h, w2_h, ws_h, g1_h, b1_h, g2_h, b2_h, gs_h, bs_h, ua_h, ub_h,
          pm0_h, pm1_h, cells_h,
-         oa, ob, gr, gw1, gws, gw2, vecs,
+         turn_h,
+         oa, ob, gr, gw1, gws, gw2, vecs, turn,
          xa, xb, bxa, bxb, w1g, w2, wsg, vg, g2, b2, gs, bs, ua, ub, pm0, pm1, cells,
          xs, xt, xr, zb, zsq, zsr, zg, zpa, zpb, valid, vq, hat, mask, zs, a1a, a1b,
-         cslots, slots, stat, up, outr, gv, dza, dzb, dzsr,
+         cslots, slots, stat, up, outr, gv, dza, dzb, dzma, dzmb, apk, arx, gacc, dzsr,
          dd, hp, hr1, hs, hr2, gu, d1a, d1b,
-         wg2, p21, p22, p23, p24, p25, wg1, p11, p12, p13, p14, p15,
+         p22, p23, p24, p25, p26, wg1, p11, p12, p13, p14, p15,
          gp, gr1, gsum, gr2, zt, gt, lsem, ssem, rsem) = refs
         i, k = lax.axis_index("dp"), lax.axis_index("chan")
         k1 = k + 1 - 2 * (k % 2)
         k2 = (k + 2) % 4
         k3 = (k1 + 2) % 4
+        ix = i % 2
+        mate = (i + 1 - 2 * ix, k)
         net = Links(ssem, rsem)
         zp, a1, dz, d1 = (zpa, zpb), (a1a, a1b), (dza, dzb), (d1a, d1b)
+        dzm = (dzma, dzmb)
 
         def flat(value):
             return value.reshape(-1, value.shape[-1])
@@ -597,6 +632,7 @@
             ("bxa", bxa_h, bxa), ("bxb", bxb_h, bxb), ("pm0", pm0_h, pm0), ("pm1", pm1_h, pm1),
             ("ua", ua_h, ua), ("ub", ub_h, ub), ("g2", g2_h, g2),
             ("b2", b2_h, b2), ("gs", gs_h, gs), ("bs", bs_h, bs), ("w2", w2_h, w2), ("cells", cells_h, cells),
+            ("turn", turn_h, turn),
         )
         for index, (name, source, target) in enumerate(pairs_of):
             loads[name] = pltpu.make_async_copy(source, target, lsem.at[index])
@@ -665,7 +701,7 @@
                 for ref, slot in zip(weight_refs(q), slot_w):
                     net.arrived(ref, slot + q, (i, k1))
 
-        for buf in (zpa, zpb, a1a, a1b, dza, dzb, d1a, d1b):
+        for buf in (zpa, zpb, a1a, a1b, dza, dzb, dzma, dzmb, d1a, d1b):
             side = buf.shape[1] if len(buf.shape) == 5 else buf.shape[0]
             lead = (slice(None),) if len(buf.shape) == 5 else ()
             for edge in (0, side - 1):
@@ -818,18 +854,17 @@
         quarter_in(1)
         acc = first_conv(1, patches(1), acc)
         acc = [jnp.sum(v, axis=0, keepdims=True) for v in acc]
-        first = chan_share(0, message(sum((by_chan(v) for v in acc), [])))
+        first = share(0, message(sum((by_chan(v) for v in acc), [])))
+        act_on(0)
+        need(*list(loads))
+        inv_pop = 1.0 / total(4, pop_first)[0:1]
+        first = chan_share(0, total(0, first, 16))
         for where in (k2, k3, k1):
             net.send(zsq.at[where], zsr.at[k], slot_s + k, (i, where))
         zsr[k] = zsq[k]
-        act_on(0)
-        value = chan_total(0, first, 16)
-        first = share(0, value)
         act_on(1)
-        need(*list(loads))
-        inv_pop = 1.0 / total(4, pop_first)[0:1]
         act_in(0)
-        tot = total(0, first, 16)
+        tot = chan_total(0, first, 16)
         stat[...] = tot
         tot_first = (stat[pl.ds(k, 1), :], stat[pl.ds(4 + k, 1), :])
         if stop == 3:
@@ -905,12 +940,44 @@
                     acc = [acc[0] + rowsum(uv), acc[1] + rowsum(uv * u)]
             return acc
 
+        left = lax.broadcasted_iota(jnp.int32, (1, LANES), 1) < out_rows
+
+        def pack(g, r0, r1):
+            for r in range(r0, r1):
+                v = by_chan(flat(a1[g][1 + r, 1 : 1 + halves[g]]).astype(f32))
+                t = [pltpu.roll(e, out_rows, 1) for e in v]
+                begin = starts[g] + r * widths[g]
+                span = slice(begin, begin + widths[g])
+                for p in range(2):
+                    cols = slice(p * LANES, (p + 1) * LANES)
+                    apk[0, span, cols] = jnp.where(left, v[2 * p], t[2 * p + 1]).astype(bf16)
+                    apk[1, span, cols] = jnp.where(left, t[2 * p], v[2 * p + 1]).astype(bf16)
+
+        early = starts[1] + sizes[1] * 3 // 64 * 16
+        third_cut = rs * widths[0] + (sizes[0] - rs * widths[0]) * 4 // 80 * 16
+        pack_spans = [
+            [slice(starts[1], early)],
+            [slice(early, rows), slice(0, rs * widths[0])],
+            [slice(rs * widths[0], third_cut)],
+            [slice(third_cut, sizes[0])],
+        ]
+        slot_p = [[net.slot() for _ in spans_] for spans_ in pack_spans]
+
+        def pack_send(n):
+            for span, slot in zip(pack_spans[n], slot_p[n]):
+                net.send(apk.at[1 - ix, span], arx.at[span], slot, mate)
+
+        act_in(1)
         activate(0)
+        pack(1, 0, halves[1])
+        pack(0, 0, rs)
         acc = second_conv([(1, 0, halves[1]), (0, 0, rs - 1)], zeros(2))
-        act_in(1)
+        pack_send(0)
         activate(1)
+        pack(0, rs, halves[0])
         acc = second_conv([(0, rs - 1, halves[0])], acc)
         first = share(1, message(acc))
+        pack_send(1)
 
         for where in (k2, k3, k1):
             net.arrived(zsr.at[where], slot_s + where, (i, where))
@@ -991,6 +1058,7 @@
             gv[span, :] = hat2
             acc = [acc[0] + rowsum(grad), acc[1] + rowsum(grad * hat2), acc[2] + rowsum(grad * hats)]
         first = share(2, message(acc))
+        pack_send(2)
         for g, target in enumerate((oa, ob)):
             n, count = images[g], halves[g] ** 2
             for cell in range(count):
@@ -1019,11 +1087,23 @@
             span = slice(begin, begin + count)
             value = k2g * (up[span, :] - valid[span, :] * (db + gv[span, :] * dg2))
             dz[g][1 + r, 1 : 1 + halves[g]] = value.astype(bf16).reshape(halves[g], images[g], chan_part)
+        slot_d = net.slot(2)
+
+        def dz_inner(buf, g):
+            return buf[g].at[1 : 1 + halves[g], 1 : 1 + halves[g]]
+
+        pack_send(3)
         for g in range(2):
-            for t, (a, b) in enumerate(TAPS):
-                dd[starts[g] : starts[g] + sizes[g], t * LANES : (t + 1) * LANES] = flat(
-                    dz[g][2 - a : 2 - a + halves[g], 2 - b : 2 - b + halves[g]]
-                )
+            net.send(dz_inner(dz, g), dz_inner(dzm, g), slot_d + g, mate)
+
+        def columns(buf):
+            for g in range(2):
+                for t, (a, b) in enumerate(TAPS):
+                    dd[starts[g] : starts[g] + sizes[g], t * LANES : (t + 1) * LANES] = flat(
+                        buf[g][2 - a : 2 - a + halves[g], 2 - b : 2 - b + halves[g]]
+                    )
+
+        columns(dz)
 
         def back_second(first, span):
             begin = pl.multiple_of(first * chan_part, LANES)
@@ -1050,32 +1130,33 @@
             part = lanes_cat([hp[q, span, :] for q in range(4)]).astype(f32) * mask[span, :]
             acc = [acc[0] + rowsum(part), acc[1] + rowsum(part * hat[span, :])]
         acc = [jnp.sum(v, axis=0, keepdims=True) for v in acc]
-        first = chan_share(1, message(sum((by_chan(v) for v in acc), [])))
-
-        acts = [flat(a1[g][1 : 1 + halves[g], 1 : 1 + halves[g]]) for g in range(2)]
-        sum2 = Reduce(net, i, k, wg2, (p21, p22, p23, p24, p25), cols2)
-        for w, cols in enumerate(cols2):
-            value = mm(acts[0], dd[: sizes[0], cols], 0, 0) + mm(acts[1], dd[sizes[0] :, cols], 0, 0)
-            wg2[:, :, :, :, cols] = value.astype(bf16).reshape(2, 2, 2, out_rows, value.shape[1])
-            sum2.first(w)
-            if w == 0:
-                first = share(3, chan_total(1, first))
+        first = share(3, message(sum((by_chan(v) for v in acc), [])))
+
+        sum2 = Reduce(net, i, k, None, (None, p22, p23, p24, p25), cols2, p26)
+        gacc[...] = mm(apk[ix], dd[...], 0, 0)
+        first = chan_share(1, total(3, first))
         for g, r, begin, count in chunks:
             span = slice(begin, begin + count)
             value = ksg * (up[span, :] - valid[span, :] * (db + zs[span, :] * dgs))
             dzsr[span, :] = value.astype(bf16)
         for n in range(2):
             slab_on(n)
-        for n in range(2):
-            slab_in(n)
-        make_planes()
-        tot = total(3, first)
+        for spans_, slots_ in zip(pack_spans, slot_p):
+            for span, slot in zip(spans_, slots_):
+                net.arrived(arx.at[span], slot, mate)
+        for g in range(2):
+            net.arrived(dz_inner(dzm, g), slot_d + g, mate)
+        columns(dzm)
+        for w, cols in enumerate(cols2):
+            value = (gacc[:, cols] + mm(arx[...], dd[:, cols], 0, 0)).astype(bf16)
+            (sum2.spread_of, sum2.second_of)[w](w, value)
+        tot = chan_total(1, first)
         stat[0:8, :] = tot
         sum_head, sum_gain1 = stat[pl.ds(k, 1), :], stat[pl.ds(4 + k, 1), :]
 
         def close_second():
             for w, cols in enumerate(cols2):
-                value = sum2.last(w)
+                value = (sum2.spread_last, sum2.last)[w](w)
                 for t in range(cols.start // LANES, cols.stop // LANES):
                     gw2[t] = value[:, t * LANES - cols.start : (t + 1) * LANES - cols.start]
 
@@ -1098,11 +1179,10 @@
             d1[g][r, s] = value.astype(bf16)
         if stop == 8:
             valid[0:1, :] = sum_head
-            for w in range(2):
-                sum2.second(w)
-            for w in range(2):
-                sum2.third(w)
+            sum2.third(1)
             close_second()
+            for n in range(2):
+                slab_in(n)
             return net.drain()
 
         def back_patch(pieces, p):
@@ -1136,7 +1216,6 @@
                 for q, value in enumerate(planes_of(values, g)):
                     gp[q, begin : begin + count, :] = flat(value).astype(bf16)
             net.send(gp.at[k3, a:b], gr1.at[1, a:b], slot_g[c] + 1, (i, k1))
-            net.send(gp.at[k1, a:b], gr1.at[0, a:b], slot_g[c], (i, k1))
 
         def back_cross(c):
             a, b = spans[c]
@@ -1146,6 +1225,7 @@
                 value = gp[k2, span, :].astype(f32) + gr1[1, span, :].astype(f32)
                 gsum[span, :] = value.astype(bf16)
             net.send(gsum.at[a:b], gr2.at[a:b], slot_g[c] + 2, (i, k2))
+            net.send(gp.at[k1, a:b], gr1.at[0, a:b], slot_g[c], (i, k1))
 
         slot_o = [net.slot(n_dp) for _ in range(n_parts)]
 
@@ -1167,50 +1247,54 @@
 
         sum1 = Reduce(net, i, k, wg1, (p11, p12, p13, p14, p15), cols1)
 
-        def weight_first():
-            everything = [(0, 0, halves[0]), (1, 0, halves[1])]
+        def weight_first(w):
+            cols = cols1[w]
             blocks = []
-            for p in range(4):
+            for p in ((3,), (0, 1, 2))[w]:
                 value = 0.0
-                for g, r0, r1 in everything:
+                for g, r0, r1 in ((0, 0, halves[0]), (1, 0, halves[1])):
                     cell = flat(zp[g][p, 1 : 1 + halves[g], 1 : 1 + halves[g]])
                     value = value + mm(cell, back_patch([(g, r0, r1)], p), 0, 0)
                 blocks.append(value.astype(bf16))
-            wg1[...] = lanes_cat(blocks).reshape(2, 2, 2, in_local, 10 * LANES)
-            sum1.first(0)
+            wg1[:, :, :, :, cols] = lanes_cat(blocks).reshape(2, 2, 2, in_local, cols.stop - cols.start)
+            sum1.first(w)
 
         back_first(0)
+        for n in range(2):
+            slab_in(n)
+        make_planes()
+        weight_first(0)
+        back_cross(0)
+        weight_first(1)
         back_first(1)
-        back_cross(0)
-        sum2.second(0)
         back_first(2)
         back_cross(1)
         back_cross(2)
-        weight_first()
-        sum2.second(1)
         back_out(0)
-        sum2.third(0)
-        back_out(1)
         sum2.third(1)
         sum1.second(0)
+        sum1.second(1)
+        back_out(1)
+        sum1.third(0)
         back_out(2)
-        sum1.third(0)
-        kept = pltpu.make_async_copy(gt.at[i], gr.at[i], lsem.at[len(pairs_of)])
-        kept.start()
+        sum1.third(1)
+        gr[i] = gt[i]
         close_second()
-        value = sum1.last(0)
-        for t, tap in enumerate(TAPS):
-            place = ORDER.index(tap)
-            place = place + (place > 0)
-            gw1[t] = value[:, place * LANES : (place + 1) * LANES]
-        gws[...] = value[:, LANES : 2 * LANES]
+        for w, cols in enumerate(cols1):
+            value = sum1.last(w)
+            for t, tap in enumerate(TAPS):
+                place = ORDER.index(tap)
+                place = (place + (place > 0)) * LANES
+                if cols.start <= place < cols.stop:
+                    gw1[t] = value[:, place - cols.start : place - cols.start + LANES]
+            if cols.start <= LANES < cols.stop:
+                gws[...] = value[:, LANES - cols.start : 2 * LANES - cols.start]
         vecs[...] = message([sum_gain1, sum_head, sum_gain2, sum_tail, sum_gains])
         for c in range(n_parts):
             cols = out_lanes[c]
             for d in range(1, n_dp):
                 j = (i + d) % n_dp
                 net.arrived(gr.at[j, :, cols], slot_o[c] + j, (j, k))
-        kept.wait()
         net.drain()
 
     V = pltpu.VMEM
@@ -1256,6 +1340,11 @@
         V((rows, chan_part), f32),
         V(pads[0], bf16),
         V(pads[1], bf16),
+        V(pads[0], bf16),
+        V(pads[1], bf16),
+        V((2, rows, chan_full // 2), bf16),
+        V((rows, chan_full // 2), bf16),
+        V((chan_full // 2, 9 * chan_part), f32),
         V((rows, chan_part), bf16),
         V((rows, 9 * chan_part), bf16),
         V((4, rows, chan_part), bf16),
@@ -1266,7 +1355,8 @@
         V(half_pads[0] + (chan_part,), bf16),
         V(half_pads[1] + (chan_part,), bf16),
     ]
-    scratch += ladder(out_rows, 9 * LANES) + ladder(in_local, 10 * LANES)
+    scratch += ladder(out_rows, 9 * LANES)[2:]
+    scratch += [V((n_dp // 2, out_rows, cols2[0].stop), bf16)] + ladder(in_local, 10 * LANES)
     scratch += [
         V((4, rows, chan_in), bf16),
         V((2, rows, chan_in), bf16),
@@ -1274,57 +1364,43 @@
         V((rows, chan_in), bf16),
         V((rows, chan_in), bf16),
         V((n_dp, in_local, slab_lanes), bf16),
-        pltpu.SemaphoreType.DMA((19,)),
+        pltpu.SemaphoreType.DMA((20,)),
         pltpu.SemaphoreType.DMA((192,)),
         pltpu.SemaphoreType.DMA((192,)),
     ]
     mid_outs = [
-        jax.ShapeDtypeStruct((sizes[0], chan_part), bf16),
-        jax.ShapeDtypeStruct((sizes[1], chan_part), bf16),
-        jax.ShapeDtypeStruct((n_dp, in_local, slab_lanes), bf16),
-        jax.ShapeDtypeStruct((9, in_local, LANES), f32),
-        jax.ShapeDtypeStruct((in_local, LANES), f32),
-        jax.ShapeDtypeStruct((9, out_rows, LANES), f32),
-        jax.ShapeDtypeStruct((8, LANES), f32),
+        V((sizes[0], chan_part), bf16),
+        V((sizes[1], chan_part), bf16),
+        V((n_dp, in_local, slab_lanes), bf16),
+        V((9, in_local, LANES), f32),
+        V((in_local, LANES), f32),
+        V((9, out_rows, LANES), f32),
+        V((8, LANES), f32),
+        V((n_dp * in_local, n_dp * in_local), bf16),
     ]
     vmem = pl.BlockSpec(memory_space=pltpu.VMEM)
     hbm = pl.BlockSpec(memory_space=pl.ANY)
     main = pl.pallas_call(
         kernel,
         out_shape=mid_outs,
-        in_specs=[hbm] * 18,
-        out_specs=[vmem, vmem, hbm, vmem, vmem, vmem, vmem],
+        in_specs=[hbm] * 19,
+        out_specs=[vmem] * len(mid_outs),
         scratch_shapes=scratch,
         compiler_params=pltpu.CompilerParams(
-            collective_id=1, has_side_effects=True, vmem_limit_bytes=60 * 2**20
+            collective_id=1, has_side_effects=True, vmem_limit_bytes=58 * 2**20
         ),
         name="block",
     )
 
-    def closing(oa_h, ob_h, gr_h, gw1_h, gws_h, gw2_h, vecs_h, turn_h,
-                fa, fb, ia, ib, f1, f2, fs, c1, h1, c2, h2, cs, hs,
-                oa, ob, gr, gw1, gws, gw2, vecs, turn, sems):
-        moves = [
+    def closing(oa, ob, gr, gw1, gws, gw2, vecs, turn,
+                fa, fb, ia, ib, f1, f2, fs, c1, h1, c2, h2, cs, hs, sems):
+        outs = [
             pltpu.make_async_copy(source, target, sems.at[index])
-            for index, (source, target) in enumerate(
-                (
-                    (gr_h, gr), (turn_h, turn), (vecs_h, vecs), (gw2_h, gw2), (gw1_h, gw1),
-                    (oa_h, oa), (ob_h, ob), (gws_h, gws),
-                )
-            )
-        ]
-        outs = [
-            pltpu.make_async_copy(source, target, sems.at[len(moves) + index])
             for index, (source, target) in enumerate(
                 ((gw2, f2), (gw1, f1), (oa, fa), (ob, fb), (gws, fs))
             )
         ]
-        for move in moves:
-            move.start()
-        for move in moves[:3]:
-            move.wait()
-        for move, out in zip(moves[3:], outs):
-            move.wait()
+        for out in outs:
             out.start()
         moved = mm(turn[...], gr[...].reshape(n_dp * in_local, slab_lanes), 1, 0)
         natural = regroup(moved, back_runs)
@@ -1348,11 +1424,10 @@
             jax.ShapeDtypeStruct((in_local, LANES), f32),
         ]
         + [jax.ShapeDtypeStruct((1, LANES), f32)] * 6,
-        in_specs=[hbm] * 8,
+        in_specs=[vmem] * 8,
         out_specs=[hbm, hbm, vmem, vmem, hbm, hbm, hbm] + [vmem] * 6,
-        scratch_shapes=[V(o.shape, o.dtype) for o in mid_outs]
-        + [V((n_dp * in_local, n_dp * in_local), bf16), pltpu.SemaphoreType.DMA((13,))],
-        compiler_params=pltpu.CompilerParams(vmem_limit_bytes=60 * 2**20),
+        scratch_shapes=[pltpu.SemaphoreType.DMA((5,))],
+        compiler_params=pltpu.CompilerParams(vmem_limit_bytes=32 * 2**20),
         name="closing",
     )
     total_rows = n_dp * in_local
@@ -1360,7 +1435,7 @@
     for c in range(in_local):
         for j in range(n_dp):
             turn[c * n_dp + j, j * in_local + c] = 1.0
-    return (main, last) + tuple(m.astype(jnp.bfloat16) for m in (turn, *patch_ms, cells_m))
+    return (main, last) + tuple(m.astype(jnp.bfloat16) for m in (*patch_ms, cells_m, turn))
 
 
 STOP = 99
@@ -1374,7 +1449,7 @@
     n_dp = lax.axis_size("dp")
     chan_part = weight_first.shape[2]
     in_local = input_a.shape[0]
-    main, last, turn, *matrices = make_fused(
+    main, last, *matrices = make_fused(
         n_dp, in_local, (boxes_a.shape[0], boxes_b.shape[0]), (SA, SB),
         weight_first.shape[1], chan_part, STOP,
     )
@@ -1386,7 +1461,7 @@
         input_a, input_b, boxes_a.T, boxes_b.T, weight_first, weight_second, weight_short,
         *vectors, upstream_a.T, upstream_b.T, *matrices,
     )
-    res = last(*mid, turn)
+    res = last(*mid)
     return (
         res[0].T, res[1].T,
         res[2].reshape(in_local, n_dp, 1, -1), res[3].reshape(in_local, n_dp, 1, -1),

time: 107 us -> 92.2 us (0.86)
  Pallas kernels: 106 us -> 91.2 us
    pallas_call x1, Pallas kernels: 103 us -> 89.1 us  [fused_body(): main(input_a, input_b, boxes_a.T, boxes_b.T, weight_first, weight_second,...]
where the time goes in v4:
time: 92.2 us; the launch traced here: 92 us
  Pallas kernels  91.2 us (99%)
    pallas_call x1, Pallas kernels, fused_body(): main(input_a, input_b, boxes_a.T, boxes_b.T, weight_first, weight_second,...  89.1 us
    pallas_call x1, Pallas kernels, fused_body(): res = last(*mid)  2.12 us

profile of v4, /device:TPU:0, one launch (start us, length us, event | category | flops | bytes accessed | tf_op | source)
XLA Modules:
  0.0 92.0 jit_solution(18361600026817091744)
XLA Ops:
  0.7 89.1 %block.1 = (bf16[784,128]{1,0:T(8,128)(2,1)S(1)}, bf16[288,128]{1,0:T(8,128)(2,1)S(1)}, bf16[8,32,1152]{2,1,0:T(8,128)(2,1)S(1)}, f32[9,32,128]{2,1,0:T(8,128)S(...) custom-call(bf16[32,25088]{1,0:T(8,128)(2,1)} %refs_0_.1, ...), custom_call_target="tpu_custom_call" | custom-call | tf_op jit(solution)/shard_map/block/pallas_call | solution.py:1460
  89.8 2.1 %closing.1 = (bf16[784,128]{1,0:T(8,128)(2,1)}, bf16[288,128]{1,0:T(8,128)(2,1)}, bf16[32,8,784]{2,1,0:T(8,128)(2,1)}, bf16[32,8,288]{2,1,0:T(8,128)(2,1)}, f32[...) custom-call(bf16[784,128]{1,0:T(8,128)(2,1)S(1)} %get-tuple-element., ...), custom_call_target="tpu_custom_call" | custom-call | tf_op jit(solution)/shard_map/closing/pallas_call | solution.py:1464

commit v5 on v4

--- a/solution.py
+++ b/solution.py
@@ -593,9 +593,12 @@
     out_lanes = [slice(0, low_lane), slice(cut_lane, slab_lanes), slice(low_lane, cut_lane)]
     out_win = [spans[0], spans[1], (0, rows)]
     n_parts = 3
-    mid = (rows // 32 + 1) * 16
-    row_halves = (slice(0, mid), slice(mid, rows))
-    cols2 = (slice(0, 5 * LANES), slice(5 * LANES, 9 * LANES))
+    back_pieces = (((0, 0, 2),), ((0, 2, halves[0] - 1),), ((0, halves[0] - 1, halves[0]), (1, 0, halves[1])))
+    row_halves = [
+        slice(starts[p[0][0]] + p[0][1] * widths[p[0][0]], starts[p[-1][0]] + p[-1][2] * widths[p[-1][0]])
+        for p in back_pieces
+    ]
+    cols2 = (slice(0, 6 * LANES), slice(6 * LANES, 9 * LANES))
     cols1 = (slice(6 * LANES, 10 * LANES), slice(0, 6 * LANES))
 
     def kernel(*refs):
@@ -616,6 +619,17 @@
         ix = i % 2
         mate = (i + 1 - 2 * ix, k)
         net = Links(ssem, rsem)
+        bits = n_dp.bit_length() - 1
+
+        def flip(d):
+            j = i
+            for b in range(bits):
+                if d >> b & 1:
+                    j = j + (1 << b) * (1 - 2 * ((i // (1 << b)) % 2))
+            return j
+
+        peers = [flip(d) for d in sorted(range(n_dp), key=lambda d: (d == 0, -(d >> 1), d & 1))]
+        peers, home = peers[:-1], peers[-1]
         zp, a1, dz, d1 = (zpa, zpb), (a1a, a1b), (dza, dzb), (d1a, d1b)
         dzm = (dzma, dzmb)
 
@@ -644,8 +658,8 @@
                 loads.pop(name).wait()
 
         barrier = pltpu.get_barrier_semaphore()
-        for d in range(1, n_dp):
-            pl.semaphore_signal(barrier, inc=1, device_id=((i + d) % n_dp, k), device_id_type=MESH)
+        for j in peers:
+            pl.semaphore_signal(barrier, inc=1, device_id=(j, k), device_id_type=MESH)
         for where in (k1, k2, k3):
             pl.semaphore_signal(barrier, inc=1, device_id=(i, where), device_id_type=MESH)
 
@@ -653,8 +667,7 @@
         for copy in loads.values():
             copy.start()
         lane = lax.broadcasted_iota(jnp.int32, (in_local, LANES), 1)
-        for d in range(n_dp):
-            j = (i + d) % n_dp
+        for d, j in enumerate(peers + [home]):
             begin = 4 * qlanes[0] * j + qlanes[0] * k
             tile = begin // LANES
             part_a = xa[:, pl.ds(pl.multiple_of(tile * LANES, LANES), win[0])].astype(f32)
@@ -670,36 +683,41 @@
                 [part_a[:, :b_tile], seam, part_b[:, LANES : slab_lanes - b_tile]], axis=1
             ).astype(bf16)
         slot_x = [net.slot(n_dp) for _ in lane_parts]
-        w_taps = (slice(0, 3), slice(3, 6), slice(6, 9))
-        slot_w = [net.slot(4) for _ in range(len(w_taps) + 2)]
+        n_via = 2
+        via = [pl.ds((9 - n_via) * e, n_via) for e in (ix, 1 - ix)]
+        w_taps = [via[0], slice(n_via, 5), slice(5, 9 - n_via)]
+        slot_w = [net.slot(4) for _ in range(6)]
 
         def weight_refs(q):
-            return [w1g.at[q, taps] for taps in w_taps] + [wsg.at[q], vg.at[q]]
+            return [w1g.at[q, taps] for taps in w_taps] + [wsg.at[q], vg.at[q], w1g.at[q, via[1]]]
 
         ordered = regroup(xs[...], runs)
         for c, cols in enumerate(lane_parts):
             moved = ordered[:, cols]
             xt[:, :, cols] = moved.reshape(n_dp, in_local, moved.shape[1])
-            xr[i, :, cols] = moved[:in_local]
+            xr[i, :, cols] = moved[-in_local:]
             if c == 0:
                 pl.semaphore_wait(barrier, n_dp + 2)
-            for d in range(1, n_dp):
-                net.send(xt.at[d, :, cols], xr.at[i, :, cols], slot_x[c] + i, ((i + d) % n_dp, k))
+            for d, j in enumerate(peers):
+                net.send(xt.at[d, :, cols], xr.at[i, :, cols], slot_x[c] + i, (j, k))
             if c == 0:
                 need("w1", "ws", "g1", "b1")
-                for where in (k2, k1):
-                    for ref, slot in zip(weight_refs(k), slot_w):
-                        net.send(ref, ref, slot + k, (i, where))
+                for ref, slot in zip(weight_refs(k)[:5], slot_w):
+                    net.send(ref, ref, slot + k, (i, k2))
+                for ref, slot in zip(weight_refs(k), slot_w):
+                    net.send(ref, ref, slot + k, (i, k1))
 
         def weights_on(n):
             ref = weight_refs(k2)[n]
-            net.arrived(ref, slot_w[n] + k2, (i, k2))
+            net.arrived(ref, slot_w[n] + k2, mate if n == 5 else (i, k2))
             net.send(ref, ref, slot_w[n] + k2, (i, k1))
-
-        def weights_in():
+            if n == 0:
+                net.send(ref, ref, slot_w[5] + k2, mate)
+
+        def weights_in(parts):
             for q in (k1, k3):
-                for ref, slot in zip(weight_refs(q), slot_w):
-                    net.arrived(ref, slot + q, (i, k1))
+                for n in parts:
+                    net.arrived(weight_refs(q)[n], slot_w[n] + q, (i, k1))
 
         for buf in (zpa, zpb, a1a, a1b, dza, dzb, dzma, dzmb, d1a, d1b):
             side = buf.shape[1] if len(buf.shape) == 5 else buf.shape[0]
@@ -774,13 +792,12 @@
             mine = slots.at[rnd, i, : value.shape[0]]
             mine[...] = value
             first = net.slot(n_dp)
-            for d in range(1, n_dp):
-                net.send(mine, mine, first + i, ((i + d) % n_dp, k))
+            for j in peers:
+                net.send(mine, mine, first + i, (j, k))
             return first
 
         def total(rnd, first, count=8):
-            for d in range(1, n_dp):
-                j = (i + d) % n_dp
+            for j in peers:
                 net.arrived(slots.at[rnd, j, :count], first + j, (j, k))
             return jnp.sum(slots[rnd, :, :count], axis=0)
 
@@ -800,8 +817,7 @@
         pop_first = share(4, population)
 
         def quarter_in(c):
-            for d in range(1, n_dp):
-                j = (i + d) % n_dp
+            for j in peers:
                 net.arrived(xr.at[j, :, lane_parts[c]], slot_x[c] + j, (j, k))
 
         def patches(c):
@@ -810,70 +826,96 @@
             count = value.shape[0] // 9
             return [value[t * count : (t + 1) * count] for t in range(9)]
 
-        slot_z = [net.slot(4) for _ in row_parts]
         slot_s = net.slot(4)
+
+        z_cuts = (slice(0, top * 3 // 80 * 16), slice(top * 3 // 80 * 16, top), slice(top, q_rows))
+        slot_z = [net.slot(4) for _ in z_cuts]
+
+        def z_send(n):
+            for where in (k2, k1):
+                net.send(zb.at[k, z_cuts[n]], zb.at[k, z_cuts[n]], slot_z[n] + k, (i, where))
 
         def first_conv(c, taps, acc):
             part = row_parts[c]
             weights = lanes_cat([w1g[q].reshape(9 * chan_in, chan_part) for q in range(4)])
             value = mm(lanes_cat(taps), weights, 1, 0).astype(bf16)
             zb[k, part, :] = value
-            for where in (k2, k1):
-                net.send(zb.at[k, part], zb.at[k, part], slot_z[c] + k, (i, where))
-            side = mm(taps[4], lanes_cat([wsg[q] for q in range(4)]), 1, 0).astype(bf16)
-            ok = lanes_cat([vq[part, :]] * 4)
-            for n, z in enumerate((value, side)):
-                z = z.astype(f32)
-                u = z * ok
-                acc[2 * n] = acc[2 * n] + rowsum(u)
-                acc[2 * n + 1] = acc[2 * n + 1] + rowsum(u * z)
+            if c == 0:
+                z_send(0)
+            z = value.astype(f32)
+            u = z * lanes_cat([vq[part, :]] * 4)
+            return [acc[0] + rowsum(u), acc[1] + rowsum(u * z)]
+
+        def projection(c, patch):
+            side = mm(patch, lanes_cat([wsg[q] for q in range(4)]), 1, 0).astype(bf16)
             for q, z in enumerate(by_chan(side)):
-                zsq[q, part, :] = z
-            return acc
-
-        def act_on(c):
-            part = row_parts[c]
-            net.arrived(zb.at[k2, part], slot_z[c] + k2, (i, k2))
-            net.send(zb.at[k2, part], zb.at[k2, part], slot_z[c] + k2, (i, k1))
-
-        def act_in(c):
-            part = row_parts[c]
-            net.arrived(zb.at[k1, part], slot_z[c] + k1, (i, k1))
-            net.arrived(zb.at[k3, part], slot_z[c] + k3, (i, k1))
-
-        acc = [jnp.zeros((8, chan_full), f32)] * 4
+                zsq[q, row_parts[c], :] = z
+
+        def act_on(n):
+            part = zb.at[k2, z_cuts[n]]
+            net.arrived(part, slot_z[n] + k2, (i, k2))
+            net.send(part, part, slot_z[n] + k2, (i, k1))
+
+        def act_in(n):
+            net.arrived(zb.at[k1, z_cuts[n]], slot_z[n] + k1, (i, k1))
+            net.arrived(zb.at[k3, z_cuts[n]], slot_z[n] + k3, (i, k1))
+
+        acc = [jnp.zeros((8, chan_full), f32)] * 2
         need("pm0", "pm1")
-        weights_on(0)
-        weights_on(1)
+        for n in (0, 1, 5, 2):
+            weights_on(n)
         quarter_in(0)
         taps = patches(0)
-        for n in range(2, 5):
-            weights_on(n)
-        weights_in()
+        center = [taps[4]]
+        weights_on(3)
+        weights_on(4)
+        weights_in((0, 1, 2, 5))
         acc = first_conv(0, taps, acc)
         quarter_in(1)
-        acc = first_conv(1, patches(1), acc)
+        taps = patches(1)
+        center.append(taps[4])
+        acc = first_conv(1, taps, acc)
         acc = [jnp.sum(v, axis=0, keepdims=True) for v in acc]
-        first = share(0, message(sum((by_chan(v) for v in acc), [])))
-        act_on(0)
+        first = chan_share(0, message(sum((by_chan(v) for v in acc), [])))
+        z_send(1)
+        z_send(2)
+        weights_in((3, 4))
+        for c in range(2):
+            projection(c, center[c])
+        zsr[k] = zsq[k]
+
         need(*list(loads))
-        inv_pop = 1.0 / total(4, pop_first)[0:1]
-        first = chan_share(0, total(0, first, 16))
+        row_cuts = (slice(0, rows // 32 * 16), slice(rows // 32 * 16, rows))
+        slot_g0 = [net.slot(4) for _ in row_cuts]
+        whole = jnp.concatenate([xr[q] for q in range(n_dp)], axis=0)
+        for span in row_cuts:
+            zg[k, span, :] = mm(cells[span, :], whole, 1, 1).astype(bf16)
+        first = share(0, chan_total(0, first))
         for where in (k2, k3, k1):
             net.send(zsq.at[where], zsr.at[k], slot_s + k, (i, where))
-        zsr[k] = zsq[k]
+        act_on(0)
+        for span, slot in zip(row_cuts, slot_g0):
+            for where in (k2, k1):
+                net.send(zg.at[k, span], zg.at[k, span], slot + k, (i, where))
         act_on(1)
-        act_in(0)
-        tot = chan_total(0, first, 16)
-        stat[...] = tot
+        act_on(2)
+
+        def slab_on(n):
+            span, slot = row_cuts[n], slot_g0[n]
+            net.arrived(zg.at[k2, span], slot + k2, (i, k2))
+            net.send(zg.at[k2, span], zg.at[k2, span], slot + k2, (i, k1))
+
+        def slab_in(n):
+            span, slot = row_cuts[n], slot_g0[n]
+            net.arrived(zg.at[k1, span], slot + k1, (i, k1))
+            net.arrived(zg.at[k3, span], slot + k3, (i, k1))
+
+        inv_pop = 1.0 / total(4, pop_first)[0:1]
+        for n in range(3):
+            act_in(n)
+        tot = total(0, first)
+        stat[0:8, :] = tot
         tot_first = (stat[pl.ds(k, 1), :], stat[pl.ds(4 + k, 1), :])
-        if stop == 3:
-            act_in(1)
-            for where in (k2, k3, k1):
-                net.arrived(zsr.at[where], slot_s + where, (i, where))
-            valid[0:1, :] = inv_pop
-            return net.drain()
-
         def moments(total_, square):
             mean = total_ * inv_pop
             return mean, lax.rsqrt(square * inv_pop - mean * mean + epsilon)
@@ -953,13 +995,12 @@
                     apk[0, span, cols] = jnp.where(left, v[2 * p], t[2 * p + 1]).astype(bf16)
                     apk[1, span, cols] = jnp.where(left, t[2 * p], v[2 * p + 1]).astype(bf16)
 
-        early = starts[1] + sizes[1] * 3 // 64 * 16
-        third_cut = rs * widths[0] + (sizes[0] - rs * widths[0]) * 4 // 80 * 16
+        near = sizes[1] - sizes[1] // 6 // 16 * 16
+        far = sizes[0] * 17 // 32 // 16 * 16
         pack_spans = [
-            [slice(starts[1], early)],
-            [slice(early, rows), slice(0, rs * widths[0])],
-            [slice(rs * widths[0], third_cut)],
-            [slice(third_cut, sizes[0])],
+            [slice(starts[1], starts[1] + near)],
+            [slice(starts[1] + near, rows), slice(0, far)],
+            [slice(far, sizes[0])],
         ]
         slot_p = [[net.slot() for _ in spans_] for spans_ in pack_spans]
 
@@ -967,42 +1008,26 @@
             for span, slot in zip(pack_spans[n], slot_p[n]):
                 net.send(apk.at[1 - ix, span], arx.at[span], slot, mate)
 
-        act_in(1)
         activate(0)
         pack(1, 0, halves[1])
         pack(0, 0, rs)
+        pack_send(0)
+        for where in (k2, k3, k1):
+            net.arrived(zsr.at[where], slot_s + where, (i, where))
+        side_acc = zeros(2)
+        for c in range(2):
+            for g, r, s, z in whole_cells(lambda q, span: zsr[q, span, :], c):
+                begin = starts[g] + (r * halves[g] + s) * images[g]
+                span = slice(begin, begin + images[g])
+                zs[span, :] = z
+                u = z * valid[span, :]
+                side_acc = [side_acc[0] + rowsum(u), side_acc[1] + rowsum(u * z)]
         acc = second_conv([(1, 0, halves[1]), (0, 0, rs - 1)], zeros(2))
-        pack_send(0)
         activate(1)
         pack(0, rs, halves[0])
         acc = second_conv([(0, rs - 1, halves[0])], acc)
-        first = share(1, message(acc))
+        first = share(1, message(acc + side_acc))
         pack_send(1)
-
-        for where in (k2, k3, k1):
-            net.arrived(zsr.at[where], slot_s + where, (i, where))
-        means, scs = moments(stat[pl.ds(8 + k, 1), :], stat[pl.ds(12 + k, 1), :])
-        for c in range(2):
-            for g, r, s, z in whole_cells(lambda q, span: zsr[q, span, :], c):
-                begin = starts[g] + (r * halves[g] + s) * images[g]
-                zs[begin : begin + images[g], :] = (z - means) * scs
-        row_cuts = (slice(0, rows // 32 * 16), slice(rows // 32 * 16, rows))
-        slot_g0 = [net.slot(4) for _ in row_cuts]
-        whole = jnp.concatenate([xr[q] for q in range(n_dp)], axis=0)
-        for span, slot in zip(row_cuts, slot_g0):
-            zg[k, span, :] = mm(cells[span, :], whole, 1, 1).astype(bf16)
-            for where in (k2, k1):
-                net.send(zg.at[k, span], zg.at[k, span], slot + k, (i, where))
-
-        def slab_on(n):
-            span, slot = row_cuts[n], slot_g0[n]
-            net.arrived(zg.at[k2, span], slot + k2, (i, k2))
-            net.send(zg.at[k2, span], zg.at[k2, span], slot + k2, (i, k1))
-
-        def slab_in(n):
-            span, slot = row_cuts[n], slot_g0[n]
-            net.arrived(zg.at[k1, span], slot + k1, (i, k1))
-            net.arrived(zg.at[k3, span], slot + k3, (i, k1))
 
         def planes_of(quarters, g):
             count = quarter[g]
@@ -1035,13 +1060,7 @@
 
         tot = total(1, first)
         mean2, sc2 = moments(tot[0:1], tot[1:2])
-        if stop == 5:
-            valid[0:1, :] = sc2
-            for n in range(2):
-                slab_on(n)
-            for n in range(2):
-                slab_in(n)
-            return net.drain()
+        means, scs = moments(tot[2:3], tot[3:4])
         gain2, gains = g2[...], gs[...]
         shifts = b2[...] + bs[...]
         acc = zeros(3)
@@ -1049,13 +1068,14 @@
             span = slice(begin, begin + count)
             ok = valid[span, :]
             hat2 = (gv[span, :] - mean2) * sc2
-            hats = zs[span, :]
+            hats = (zs[span, :] - means) * scs
             v = hat2 * gain2 + hats * gains + shifts
             sig = sigma(v)
             outr[span, :] = v * sig * ok
             grad = up[span, :] * ok * (sig * (1.0 + v * (1.0 - sig)))
             up[span, :] = grad
             gv[span, :] = hat2
+            zs[span, :] = hats
             acc = [acc[0] + rowsum(grad), acc[1] + rowsum(grad * hat2), acc[2] + rowsum(grad * hats)]
         first = share(2, message(acc))
         pack_send(2)
@@ -1073,14 +1093,6 @@
             mask[span, :] = sig * (1.0 + v * (1.0 - sig)) * lanes_cat([valid[span, :]] * 4)
         tot = total(2, first)
         sum_tail, sum_gain2, sum_gains = tot[0:1], tot[1:2], tot[2:3]
-        if stop == 6:
-            valid[0:1, :] = sum_tail
-            for n in range(2):
-                slab_on(n)
-            for n in range(2):
-                slab_in(n)
-            return net.drain()
-
         k2g, ksg = gain2 * sc2, gains * scs
         db, dg2, dgs = sum_tail * inv_pop, sum_gain2 * inv_pop, sum_gains * inv_pop
         for g, r, begin, count in chunks:
@@ -1092,18 +1104,16 @@
         def dz_inner(buf, g):
             return buf[g].at[1 : 1 + halves[g], 1 : 1 + halves[g]]
 
-        pack_send(3)
         for g in range(2):
             net.send(dz_inner(dz, g), dz_inner(dzm, g), slot_d + g, mate)
 
-        def columns(buf):
-            for g in range(2):
+        def columns(buf, piece):
+            for g, r0, r1 in piece:
                 for t, (a, b) in enumerate(TAPS):
-                    dd[starts[g] : starts[g] + sizes[g], t * LANES : (t + 1) * LANES] = flat(
-                        buf[g][2 - a : 2 - a + halves[g], 2 - b : 2 - b + halves[g]]
-                    )
-
-        columns(dz)
+                    dd[
+                        starts[g] + r0 * widths[g] : starts[g] + r1 * widths[g],
+                        t * LANES : (t + 1) * LANES,
+                    ] = flat(buf[g][r0 + 2 - a : r1 + 2 - a, 2 - b : 2 - b + halves[g]])
 
         def back_second(first, span):
             begin = pl.multiple_of(first * chan_part, LANES)
@@ -1113,7 +1123,8 @@
             hp[first + 1, span, :] = value[:, chan_part:]
 
         slot_h = [net.slot(3) for _ in row_halves]
-        for span, slot in zip(row_halves, slot_h):
+        for span, slot, piece in zip(row_halves, slot_h, back_pieces):
+            columns(dz, piece)
             back_second(2 * (k2 // 2), span)
             net.send(hp.at[k3, span], hr1.at[1, span], slot + 1, (i, k1))
         for span, slot in zip(row_halves, slot_h):
@@ -1146,7 +1157,8 @@
                 net.arrived(arx.at[span], slot, mate)
         for g in range(2):
             net.arrived(dz_inner(dzm, g), slot_d + g, mate)
-        columns(dzm)
+        for piece in back_pieces:
+            columns(dzm, piece)
         for w, cols in enumerate(cols2):
             value = (gacc[:, cols] + mm(arx[...], dd[:, cols], 0, 0)).astype(bf16)
             (sum2.spread_of, sum2.second_of)[w](w, value)
@@ -1177,14 +1189,6 @@
             grad = grad * mask[part, own]
             value = k1g * (grad - valid[part, :] * (db + hat[part, own] * dg1))
             d1[g][r, s] = value.astype(bf16)
-        if stop == 8:
-            valid[0:1, :] = sum_head
-            sum2.third(1)
-            close_second()
-            for n in range(2):
-                slab_in(n)
-            return net.drain()
-
         def back_patch(pieces, p):
             parts = []
             for g, r0, r1 in pieces:
@@ -1241,8 +1245,7 @@
             a, b = out_win[c]
             value = mm(zt[a:b, :], cells[a:b, cols], 0, 0).astype(bf16)
             gt[:, :, cols] = value.reshape(n_dp, in_local, value.shape[1])
-            for d in range(1, n_dp):
-                j = (i + d) % n_dp
+            for j in peers:
                 net.send(gt.at[j, :, cols], gr.at[i, :, cols], slot_o[c] + i, (j, k))
 
         sum1 = Reduce(net, i, k, wg1, (p11, p12, p13, p14, p15), cols1)
@@ -1292,8 +1295,7 @@
         vecs[...] = message([sum_gain1, sum_head, sum_gain2, sum_tail, sum_gains])
         for c in range(n_parts):
             cols = out_lanes[c]
-            for d in range(1, n_dp):
-                j = (i + d) % n_dp
+            for j in peers:
                 net.arrived(gr.at[j, :, cols], slot_o[c] + j, (j, k))
         net.drain()
 

time: 92.2 us -> 90.4 us (0.980)
  Pallas kernels: 91.2 us -> 89.4 us
    pallas_call x1, Pallas kernels: 89.1 us -> 87.3 us  [fused_body(): main(input_a, input_b, boxes_a.T, boxes_b.T, weight_first, weight_second,...]
where the time goes in v5:
time: 90.4 us; the launch traced here: 90.2 us
  Pallas kernels  89.4 us (99%)
    pallas_call x1, Pallas kernels, fused_body(): main(input_a, input_b, boxes_a.T, boxes_b.T, weight_first, weight_second,...  87.3 us
    pallas_call x1, Pallas kernels, fused_body(): res = last(*mid)  2.12 us

profile of v5, /device:TPU:0, one launch (start us, length us, event | category | flops | bytes accessed | tf_op | source)
XLA Modules:
  0.0 90.2 jit_solution(9362406499690744175)
XLA Ops:
  0.7 87.3 %block.1 = (bf16[784,128]{1,0:T(8,128)(2,1)S(1)}, bf16[288,128]{1,0:T(8,128)(2,1)S(1)}, bf16[8,32,1152]{2,1,0:T(8,128)(2,1)S(1)}, f32[9,32,128]{2,1,0:T(8,128)S(...) custom-call(bf16[32,25088]{1,0:T(8,128)(2,1)} %refs_0_.1, ...), custom_call_target="tpu_custom_call" | custom-call | tf_op jit(solution)/shard_map/block/pallas_call | solution.py:1462
  88.0 2.1 %closing.1 = (bf16[784,128]{1,0:T(8,128)(2,1)}, bf16[288,128]{1,0:T(8,128)(2,1)}, bf16[32,8,784]{2,1,0:T(8,128)(2,1)}, bf16[32,8,288]{2,1,0:T(8,128)(2,1)}, f32[...) custom-call(bf16[784,128]{1,0:T(8,128)(2,1)S(1)} %get-tuple-element., ...), custom_call_target="tpu_custom_call" | custom-call | tf_op jit(solution)/shard_map/closing/pallas_call | solution.py:1466

commit v6 on v5

--- a/solution.py
+++ b/solution.py
@@ -581,24 +581,14 @@
         np.concatenate([m[rows_, lanes_] for m in patch_m], axis=0)
         for rows_, lanes_ in zip(row_parts, patch_win)
     ]
-    spans = [
-        (starts[g] + r0 * widths[g], starts[g] + r1 * widths[g])
-        for g, r0, r1 in (segments[0], segments[2], segments[1])
-    ]
-    pieces = [[segments[0]], [segments[2]], [segments[1]]]
-    part_chunks = [
-        [ch for ch in chunks if ch[0] == p[0][0] and p[0][1] <= ch[1] < p[0][2]] for p in pieces
-    ]
     low_lane = seg_lane[1] // LANES * LANES
-    out_lanes = [slice(0, low_lane), slice(cut_lane, slab_lanes), slice(low_lane, cut_lane)]
-    out_win = [spans[0], spans[1], (0, rows)]
-    n_parts = 3
+    out_lanes = [slice(cut_lane, slab_lanes), slice(0, low_lane), slice(low_lane, cut_lane)]
     back_pieces = (((0, 0, 2),), ((0, 2, halves[0] - 1),), ((0, halves[0] - 1, halves[0]), (1, 0, halves[1])))
     row_halves = [
         slice(starts[p[0][0]] + p[0][1] * widths[p[0][0]], starts[p[-1][0]] + p[-1][2] * widths[p[-1][0]])
         for p in back_pieces
     ]
-    cols2 = (slice(0, 6 * LANES), slice(6 * LANES, 9 * LANES))
+    cols2 = (slice(0, 4 * LANES), slice(4 * LANES, 9 * LANES))
     cols1 = (slice(6 * LANES, 10 * LANES), slice(0, 6 * LANES))
 
     def kernel(*refs):
@@ -611,7 +601,7 @@
          cslots, slots, stat, up, outr, gv, dza, dzb, dzma, dzmb, apk, arx, gacc, dzsr,
          dd, hp, hr1, hs, hr2, gu, d1a, d1b,
          p22, p23, p24, p25, p26, wg1, p11, p12, p13, p14, p15,
-         gp, gr1, gsum, gr2, zt, gt, lsem, ssem, rsem) = refs
+         sq, si, dq, di, gt, lsem, ssem, rsem) = refs
         i, k = lax.axis_index("dp"), lax.axis_index("chan")
         k1 = k + 1 - 2 * (k % 2)
         k2 = (k + 2) % 4
@@ -846,10 +836,13 @@
             u = z * lanes_cat([vq[part, :]] * 4)
             return [acc[0] + rowsum(u), acc[1] + rowsum(u * z)]
 
-        def projection(c, patch):
+        def projection(c, patch, acc):
             side = mm(patch, lanes_cat([wsg[q] for q in range(4)]), 1, 0).astype(bf16)
             for q, z in enumerate(by_chan(side)):
                 zsq[q, row_parts[c], :] = z
+            z = side.astype(f32)
+            u = z * lanes_cat([vq[row_parts[c], :]] * 4)
+            return [acc[0] + rowsum(u), acc[1] + rowsum(u * z)]
 
         def act_on(n):
             part = zb.at[k2, z_cuts[n]]
@@ -880,8 +873,11 @@
         z_send(1)
         z_send(2)
         weights_in((3, 4))
+        acc = [jnp.zeros((8, chan_full), f32)] * 2
         for c in range(2):
-            projection(c, center[c])
+            acc = projection(c, center[c], acc)
+        acc = [jnp.sum(v, axis=0, keepdims=True) for v in acc]
+        side_first = share(5, message(sum((by_chan(v) for v in acc), [])))
         zsr[k] = zsq[k]
 
         need(*list(loads))
@@ -894,11 +890,12 @@
         for where in (k2, k3, k1):
             net.send(zsq.at[where], zsr.at[k], slot_s + k, (i, where))
         act_on(0)
+        act_on(1)
+        act_on(2)
+        side_first = chan_share(2, total(5, side_first))
         for span, slot in zip(row_cuts, slot_g0):
             for where in (k2, k1):
                 net.send(zg.at[k, span], zg.at[k, span], slot + k, (i, where))
-        act_on(1)
-        act_on(2)
 
         def slab_on(n):
             span, slot = row_cuts[n], slot_g0[n]
@@ -911,19 +908,6 @@
             net.arrived(zg.at[k3, span], slot + k3, (i, k1))
 
         inv_pop = 1.0 / total(4, pop_first)[0:1]
-        for n in range(3):
-            act_in(n)
-        tot = total(0, first)
-        stat[0:8, :] = tot
-        tot_first = (stat[pl.ds(k, 1), :], stat[pl.ds(4 + k, 1), :])
-        def moments(total_, square):
-            mean = total_ * inv_pop
-            return mean, lax.rsqrt(square * inv_pop - mean * mean + epsilon)
-
-        mean1, sc1 = moments(tot[0:4], tot[4:8])
-        mean1, sc1 = (lanes_cat([v[q : q + 1] for q in range(4)]) for v in (mean1, sc1))
-        gain1, shift1 = (lanes_cat([vg[q, e] for q in range(4)]) for e in range(2))
-
         turn_low = lax.broadcasted_iota(jnp.int32, (8, 1), 0) < 4
 
         def whole_cells(read, c):
@@ -952,15 +936,39 @@
                             r, s = divmod(cell + e, halves[g])
                             yield g, r0 + r, s, value
 
-        def activate(c):
+        def gather_cells(c):
             for g, r, s, z in whole_cells(lambda q, span: zb[q, span, :], c):
                 begin = starts[g] + (r * halves[g] + s) * images[g]
-                span = slice(begin, begin + images[g])
-                h = (z - mean1) * sc1
-                hat[span, :] = h
-                v = h * gain1 + shift1
-                act = v * sigma(v) * lanes_cat([valid[span, :]] * 4)
-                a1[g][1 + r, 1 + s] = act.astype(bf16)
+                hat[begin : begin + images[g], :] = z
+
+        for n in range(2):
+            act_in(n)
+        gather_cells(0)
+        act_in(2)
+        gather_cells(1)
+        tot = total(0, first)
+        stat[0:8, :] = tot
+        tot_first = (stat[pl.ds(k, 1), :], stat[pl.ds(4 + k, 1), :])
+        def moments(total_, square):
+            mean = total_ * inv_pop
+            return mean, lax.rsqrt(square * inv_pop - mean * mean + epsilon)
+
+        mean1, sc1 = moments(tot[0:4], tot[4:8])
+        mean1, sc1 = (lanes_cat([v[q : q + 1] for q in range(4)]) for v in (mean1, sc1))
+        gain1, shift1 = (lanes_cat([vg[q, e] for q in range(4)]) for e in range(2))
+
+        scale1 = sc1 * gain1
+        offset1 = shift1 - mean1 * scale1
+
+        def activate(c):
+            for g, r0, r1 in (segments[:2], segments[2:])[c]:
+                for r in range(r0, r1):
+                    for s in range(halves[g]):
+                        begin = starts[g] + (r * halves[g] + s) * images[g]
+                        span = slice(begin, begin + images[g])
+                        v = hat[span, :] * scale1 + offset1
+                        act = v * sigma(v) * lanes_cat([valid[span, :]] * 4)
+                        a1[g][1 + r, 1 + s] = act.astype(bf16)
 
         def second_conv(parts, acc):
             value = None
@@ -1012,22 +1020,21 @@
         pack(1, 0, halves[1])
         pack(0, 0, rs)
         pack_send(0)
-        for where in (k2, k3, k1):
-            net.arrived(zsr.at[where], slot_s + where, (i, where))
-        side_acc = zeros(2)
-        for c in range(2):
-            for g, r, s, z in whole_cells(lambda q, span: zsr[q, span, :], c):
-                begin = starts[g] + (r * halves[g] + s) * images[g]
-                span = slice(begin, begin + images[g])
-                zs[span, :] = z
-                u = z * valid[span, :]
-                side_acc = [side_acc[0] + rowsum(u), side_acc[1] + rowsum(u * z)]
         acc = second_conv([(1, 0, halves[1]), (0, 0, rs - 1)], zeros(2))
         activate(1)
         pack(0, rs, halves[0])
         acc = second_conv([(0, rs - 1, halves[0])], acc)
-        first = share(1, message(acc + side_acc))
+        first = share(1, message(acc))
         pack_send(1)
+
+        stat[0:8, :] = chan_total(2, side_first)
+        means, scs = moments(stat[pl.ds(k, 1), :], stat[pl.ds(4 + k, 1), :])
+        for where in (k2, k3, k1):
+            net.arrived(zsr.at[where], slot_s + where, (i, where))
+        for c in range(2):
+            for g, r, s, z in whole_cells(lambda q, span: zsr[q, span, :], c):
+                begin = starts[g] + (r * halves[g] + s) * images[g]
+                zs[begin : begin + images[g], :] = (z - means) * scs
 
         def planes_of(quarters, g):
             count = quarter[g]
@@ -1060,7 +1067,6 @@
 
         tot = total(1, first)
         mean2, sc2 = moments(tot[0:1], tot[1:2])
-        means, scs = moments(tot[2:3], tot[3:4])
         gain2, gains = g2[...], gs[...]
         shifts = b2[...] + bs[...]
         acc = zeros(3)
@@ -1068,14 +1074,13 @@
             span = slice(begin, begin + count)
             ok = valid[span, :]
             hat2 = (gv[span, :] - mean2) * sc2
-            hats = (zs[span, :] - means) * scs
+            hats = zs[span, :]
             v = hat2 * gain2 + hats * gains + shifts
             sig = sigma(v)
             outr[span, :] = v * sig * ok
             grad = up[span, :] * ok * (sig * (1.0 + v * (1.0 - sig)))
             up[span, :] = grad
             gv[span, :] = hat2
-            zs[span, :] = hats
             acc = [acc[0] + rowsum(grad), acc[1] + rowsum(grad * hat2), acc[2] + rowsum(grad * hats)]
         first = share(2, message(acc))
         pack_send(2)
@@ -1088,7 +1093,9 @@
             target[...] = gu[starts[g] : starts[g] + sizes[g], :].astype(bf16)
         for begin in range(0, rows, 16):
             span = slice(begin, begin + 16)
-            v = hat[span, :] * gain1 + shift1
+            h = (hat[span, :] - mean1) * sc1
+            hat[span, :] = h
+            v = h * gain1 + shift1
             sig = sigma(v)
             mask[span, :] = sig * (1.0 + v * (1.0 - sig)) * lanes_cat([valid[span, :]] * 4)
         tot = total(2, first)
@@ -1107,9 +1114,10 @@
         for g in range(2):
             net.send(dz_inner(dz, g), dz_inner(dzm, g), slot_d + g, mate)
 
-        def columns(buf, piece):
+        def columns(buf, piece, taps=range(9)):
             for g, r0, r1 in piece:
-                for t, (a, b) in enumerate(TAPS):
+                for t in taps:
+                    a, b = TAPS[t]
                     dd[
                         starts[g] + r0 * widths[g] : starts[g] + r1 * widths[g],
                         t * LANES : (t + 1) * LANES,
@@ -1123,33 +1131,97 @@
             hp[first + 1, span, :] = value[:, chan_part:]
 
         slot_h = [net.slot(3) for _ in row_halves]
-        for span, slot, piece in zip(row_halves, slot_h, back_pieces):
-            columns(dz, piece)
-            back_second(2 * (k2 // 2), span)
-            net.send(hp.at[k3, span], hr1.at[1, span], slot + 1, (i, k1))
-        for span, slot in zip(row_halves, slot_h):
-            net.arrived(hr1.at[1, span], slot + 1, (i, k1))
+        def other_pair(n):
+            columns(dz, back_pieces[n])
+            back_second(2 * (k2 // 2), row_halves[n])
+            net.send(hp.at[k3, row_halves[n]], hr1.at[1, row_halves[n]], slot_h[n] + 1, (i, k1))
+
+        def cross_second(n):
+            span = row_halves[n]
+            net.arrived(hr1.at[1, span], slot_h[n] + 1, (i, k1))
             hs[span, :] = (hp[k2, span, :].astype(f32) + hr1[1, span, :].astype(f32)).astype(bf16)
-            net.send(hs.at[span], hr2.at[span], slot + 2, (i, k2))
+            net.send(hs.at[span], hr2.at[span], slot_h[n] + 2, (i, k2))
+
+        def pair_sums(first):
+            acc = [jnp.zeros((8, 2 * chan_part), f32)] * 2
+            cols = pl.ds(pl.multiple_of(first * chan_part, 2 * LANES), 2 * chan_part)
+            for begin in range(0, rows, 16):
+                span = slice(begin, begin + 16)
+                part = lanes_cat([hp[first + e, span, :] for e in range(2)]).astype(f32) * mask[span, cols]
+                acc = [acc[0] + rowsum(part), acc[1] + rowsum(part * hat[span, cols])]
+            acc = [jnp.sum(v, axis=0, keepdims=True) for v in acc]
+            for e in range(2):
+                for n in range(2):
+                    stat[pl.ds(4 * n + first + e, 1), :] = acc[n][:, e * LANES : (e + 1) * LANES]
+
+        other_pair(0)
+        other_pair(1)
+        cross_second(0)
+        other_pair(2)
+        cross_second(1)
         back_second(2 * (k // 2), slice(0, rows))
+        pair_sums(2 * (k2 // 2))
+        cross_second(2)
         for span, slot in zip(row_halves, slot_h):
             net.send(hp.at[k1, span], hr1.at[0, span], slot, (i, k1))
-
-        acc = [jnp.zeros((8, chan_full), f32)] * 2
-        for begin in range(0, rows, 16):
-            span = slice(begin, begin + 16)
-            part = lanes_cat([hp[q, span, :] for q in range(4)]).astype(f32) * mask[span, :]
-            acc = [acc[0] + rowsum(part), acc[1] + rowsum(part * hat[span, :])]
-        acc = [jnp.sum(v, axis=0, keepdims=True) for v in acc]
-        first = share(3, message(sum((by_chan(v) for v in acc), [])))
+        pair_sums(2 * (k // 2))
+        first = share(3, stat[0:8, :])
 
         sum2 = Reduce(net, i, k, None, (None, p22, p23, p24, p25), cols2, p26)
         gacc[...] = mm(apk[ix], dd[...], 0, 0)
         first = chan_share(1, total(3, first))
-        for g, r, begin, count in chunks:
-            span = slice(begin, begin + count)
+        def split_cells(read, target, c):
+            for begin in range(row_parts[c].start, row_parts[c].stop, 16):
+                tiles = []
+                for at in (begin, begin + 8):
+                    seg = max(e for e in range(3) if seg_row[e] <= at)
+                    g, r0, r1 = segments[seg]
+                    per = 8 // quarter[g]
+                    cell = (at - seg_row[seg]) // 8 * per
+                    blocks = []
+                    for e in range(per):
+                        if cell + e < seg_cells[seg]:
+                            r, s = divmod(cell + e, halves[g])
+                            blocks.append(read(g, r0 + r, s))
+                        else:
+                            blocks.append(jnp.zeros((images[g], chan_part), f32))
+                    if per == 1:
+                        tiles.append([blocks[0][8 * q : 8 * q + 8] for q in range(4)])
+                    else:
+                        found = []
+                        for h in range(2):
+                            v = [block[8 * h : 8 * h + 8] for block in blocks]
+                            t = [pltpu.roll(e, 4, 0) for e in v]
+                            found += [jnp.where(turn_low, v[0], t[1]), jnp.where(turn_low, t[0], v[1])]
+                        tiles.append(found)
+                for q in range(4):
+                    both = jnp.concatenate([tiles[0][q], tiles[1][q]], axis=0)
+                    target[q, begin : begin + 16, :] = both.astype(bf16)
+
+        def cell_span(g, r, s):
+            begin = starts[g] + (r * halves[g] + s) * images[g]
+            return slice(begin, begin + images[g])
+
+        def short_cell(g, r, s):
+            span = cell_span(g, r, s)
             value = ksg * (up[span, :] - valid[span, :] * (db + zs[span, :] * dgs))
             dzsr[span, :] = value.astype(bf16)
+            return value
+
+        slot_q = [net.slot(4) for _ in range(3)]
+
+        def quarters_out(source, target, span, slot):
+            for where in (k2, k3, k1):
+                net.send(source.at[where, span], target.at[k, span], slot + k, (i, where))
+            target[k, span, :] = source[k, span, :]
+
+        def quarters_in(target, span, slot):
+            for where in (k1, k2, k3):
+                net.arrived(target.at[where, span], slot + where, (i, where))
+
+        for c in range(2):
+            split_cells(short_cell, sq, c)
+        quarters_out(sq, si, slice(0, q_rows), slot_q[2])
         for n in range(2):
             slab_on(n)
         for spans_, slots_ in zip(pack_spans, slot_p):
@@ -1157,9 +1229,9 @@
                 net.arrived(arx.at[span], slot, mate)
         for g in range(2):
             net.arrived(dz_inner(dzm, g), slot_d + g, mate)
-        for piece in back_pieces:
-            columns(dzm, piece)
         for w, cols in enumerate(cols2):
+            for piece in back_pieces:
+                columns(dzm, piece, range(cols.start // LANES, cols.stop // LANES))
             value = (gacc[:, cols] + mm(arx[...], dd[:, cols], 0, 0)).astype(bf16)
             (sum2.spread_of, sum2.second_of)[w](w, value)
         tot = chan_total(1, first)
@@ -1176,19 +1248,22 @@
         mean1, sc1 = moments(tot_first[0], tot_first[1])
         k1g = vg[k, 0] * sc1
         db, dg1 = sum_head * inv_pop, sum_gain1 * inv_pop
-        per_cell = [(g, r, s) for g in range(2) for r in range(halves[g]) for s in range(halves[g])]
-        waiting = list(zip(row_halves, slot_h))
-        for g, r, s in per_cell:
-            begin = starts[g] + (r * halves[g] + s) * images[g]
-            part = slice(begin, begin + images[g])
-            while waiting and waiting[0][0].start < part.stop:
-                span, slot = waiting.pop(0)
-                net.arrived(hr1.at[0, span], slot, (i, k1))
-                net.arrived(hr2.at[span], slot + 2, (i, k2))
-            grad = hp[k, part, :].astype(f32) + hr1[0, part, :].astype(f32) + hr2[part, :].astype(f32)
-            grad = grad * mask[part, own]
-            value = k1g * (grad - valid[part, :] * (db + hat[part, own] * dg1))
+        for span, slot in zip(row_halves, slot_h):
+            net.arrived(hr1.at[0, span], slot, (i, k1))
+            net.arrived(hr2.at[span], slot + 2, (i, k2))
+
+        def first_cell(g, r, s):
+            span = cell_span(g, r, s)
+            grad = hp[k, span, :].astype(f32) + hr1[0, span, :].astype(f32) + hr2[span, :].astype(f32)
+            grad = grad * mask[span, own]
+            value = k1g * (grad - valid[span, :] * (db + hat[span, own] * dg1))
             d1[g][r, s] = value.astype(bf16)
+            return value
+
+        for c in (1, 0):
+            split_cells(first_cell, dq, c)
+            quarters_out(dq, di, row_parts[c], slot_q[c])
+
         def back_patch(pieces, p):
             parts = []
             for g, r0, r1 in pieces:
@@ -1202,51 +1277,24 @@
                 parts.append(lanes_cat(taps))
             return jnp.concatenate(parts, axis=0) if len(parts) > 1 else parts[0]
 
-        slot_g = [net.slot(3) for _ in range(n_parts)]
-
-        def back_first(c):
-            a, b = spans[c]
-            planes = []
-            for p in range(4):
-                weights = [w1g[k, 3 * ta + tb] for ta, tb in PLANE_TAPS[p]]
-                if p == 0:
-                    weights.append(wsg[k])
-                planes.append(mm(back_patch(pieces[c], p), lanes_cat(weights), 1, 1))
-            for g, r, begin, count in part_chunks[c]:
-                values = [
-                    v[begin - a : begin - a + count].reshape(halves[g], images[g], chan_in)
-                    for v in planes
-                ]
-                for q, value in enumerate(planes_of(values, g)):
-                    gp[q, begin : begin + count, :] = flat(value).astype(bf16)
-            net.send(gp.at[k3, a:b], gr1.at[1, a:b], slot_g[c] + 1, (i, k1))
-
-        def back_cross(c):
-            a, b = spans[c]
-            net.arrived(gr1.at[1, a:b], slot_g[c] + 1, (i, k1))
-            for begin in range(a, b, 16):
-                span = slice(begin, begin + 16)
-                value = gp[k2, span, :].astype(f32) + gr1[1, span, :].astype(f32)
-                gsum[span, :] = value.astype(bf16)
-            net.send(gsum.at[a:b], gr2.at[a:b], slot_g[c] + 2, (i, k2))
-            net.send(gp.at[k1, a:b], gr1.at[0, a:b], slot_g[c], (i, k1))
-
-        slot_o = [net.slot(n_dp) for _ in range(n_parts)]
-
-        def back_out(c):
-            a, b = spans[c]
-            net.arrived(gr1.at[0, a:b], slot_g[c], (i, k1))
-            net.arrived(gr2.at[a:b], slot_g[c] + 2, (i, k2))
-            for begin in range(a, b, 16):
-                span = slice(begin, begin + 16)
-                value = gp[k, span, :].astype(f32) + gr1[0, span, :].astype(f32)
-                zt[span, :] = (value + gr2[span, :].astype(f32)).astype(bf16)
-            cols = out_lanes[c]
-            a, b = out_win[c]
-            value = mm(zt[a:b, :], cells[a:b, cols], 0, 0).astype(bf16)
-            gt[:, :, cols] = value.reshape(n_dp, in_local, value.shape[1])
+        slot_o = [net.slot(n_dp) for _ in out_lanes]
+
+        def back_taps(c):
+            part = row_parts[c]
+            quarters_in(di, part, slot_q[c])
+            grads = lanes_cat([di[q, part, :] for q in range(4)])
+            weights = lanes_cat([w1g[q].reshape(9 * chan_in, chan_part) for q in range(4)])
+            value = mm(grads, weights, 1, 1)
+            taps = [value[:, t * chan_in : (t + 1) * chan_in] for t in range(9)]
+            side = lanes_cat([si[q, part, :] for q in range(4)])
+            taps[4] = taps[4] + mm(side, lanes_cat([wsg[q] for q in range(4)]), 1, 1)
+            return jnp.concatenate([tap.astype(bf16) for tap in taps], axis=0)
+
+        def out_send(n, value):
+            cols = out_lanes[n]
+            gt[:, :, cols] = value.astype(bf16).reshape(n_dp, in_local, value.shape[1])
             for j in peers:
-                net.send(gt.at[j, :, cols], gr.at[i, :, cols], slot_o[c] + i, (j, k))
+                net.send(gt.at[j, :, cols], gr.at[i, :, cols], slot_o[n] + i, (j, k))
 
         sum1 = Reduce(net, i, k, wg1, (p11, p12, p13, p14, p15), cols1)
 
@@ -1262,24 +1310,24 @@
             wg1[:, :, :, :, cols] = lanes_cat(blocks).reshape(2, 2, 2, in_local, cols.stop - cols.start)
             sum1.first(w)
 
-        back_first(0)
         for n in range(2):
             slab_in(n)
         make_planes()
         weight_first(0)
-        back_cross(0)
         weight_first(1)
-        back_first(1)
-        back_first(2)
-        back_cross(1)
-        back_cross(2)
-        back_out(0)
+        quarters_in(si, slice(0, q_rows), slot_q[2])
+        late = back_taps(1)
+        edge = cut_lane - patch_win[1].start
+        out_send(0, mm(late, pm1[:, edge:], 0, 0))
+        early_ = back_taps(0)
+        out_send(1, mm(early_, pm0[:, :low_lane], 0, 0))
+        rest = mm(early_, pm0[:, low_lane:], 0, 0)
+        shared = mm(late, pm1[:, low_lane - patch_win[1].start : edge], 0, 0)
         sum2.third(1)
         sum1.second(0)
         sum1.second(1)
-        back_out(1)
+        out_send(2, rest + shared)
         sum1.third(0)
-        back_out(2)
         sum1.third(1)
         gr[i] = gt[i]
         close_second()
@@ -1293,8 +1341,7 @@
             if cols.start <= LANES < cols.stop:
                 gws[...] = value[:, LANES - cols.start : 2 * LANES - cols.start]
         vecs[...] = message([sum_gain1, sum_head, sum_gain2, sum_tail, sum_gains])
-        for c in range(n_parts):
-            cols = out_lanes[c]
+        for c, cols in enumerate(out_lanes):
             for j in peers:
                 net.arrived(gr.at[j, :, cols], slot_o[c] + j, (j, k))
         net.drain()
@@ -1334,8 +1381,8 @@
         V((rows, chan_part), f32),
         V(pads[0][:3] + (chan_full,), bf16),
         V(pads[1][:3] + (chan_full,), bf16),
-        V((2, 4, 16, LANES), f32),
-        V((5, n_dp, 16, LANES), f32),
+        V((3, 4, 16, LANES), f32),
+        V((6, n_dp, 16, LANES), f32),
         V((16, LANES), f32),
         V((rows, chan_part), f32),
         V((rows, chan_part), f32),
@@ -1360,11 +1407,10 @@
     scratch += ladder(out_rows, 9 * LANES)[2:]
     scratch += [V((n_dp // 2, out_rows, cols2[0].stop), bf16)] + ladder(in_local, 10 * LANES)
     scratch += [
-        V((4, rows, chan_in), bf16),
-        V((2, rows, chan_in), bf16),
-        V((rows, chan_in), bf16),
-        V((rows, chan_in), bf16),
-        V((rows, chan_in), bf16),
+        V((4, q_rows, chan_part), bf16),
+        V((4, q_rows, chan_part), bf16),
+        V((4, q_rows, chan_part), bf16),
+        V((4, q_rows, chan_part), bf16),
         V((n_dp, in_local, slab_lanes), bf16),
         pltpu.SemaphoreType.DMA((20,)),
         pltpu.SemaphoreType.DMA((192,)),

time: 90.4 us -> 88.9 us (0.983)
  Pallas kernels: 89.4 us -> 87.9 us
    pallas_call x1, Pallas kernels: 87.3 us -> 85.8 us  [fused_body(): main(input_a, input_b, boxes_a.T, boxes_b.T, weight_first, weight_second,...]
where the time goes in v6:
time: 88.9 us; the launch traced here: 88.8 us
  Pallas kernels  87.9 us (99%)
    pallas_call x1, Pallas kernels, fused_body(): main(input_a, input_b, boxes_a.T, boxes_b.T, weight_first, weight_second,...  85.8 us
    pallas_call x1, Pallas kernels, fused_body(): res = last(*mid)  2.12 us

profile of v6, /device:TPU:0, one launch (start us, length us, event | category | flops | bytes accessed | tf_op | source)
XLA Modules:
  0.0 88.8 jit_solution(14848776755214529001)
XLA Ops:
  0.7 85.8 %block.1 = (bf16[784,128]{1,0:T(8,128)(2,1)S(1)}, bf16[288,128]{1,0:T(8,128)(2,1)S(1)}, bf16[8,32,1152]{2,1,0:T(8,128)(2,1)S(1)}, f32[9,32,128]{2,1,0:T(8,128)S(...) custom-call(bf16[32,25088]{1,0:T(8,128)(2,1)} %refs_0_.1, ...), custom_call_target="tpu_custom_call" | custom-call | tf_op jit(solution)/shard_map/block/pallas_call | solution.py:1508
  86.5 2.1 %closing.1 = (bf16[784,128]{1,0:T(8,128)(2,1)}, bf16[288,128]{1,0:T(8,128)(2,1)}, bf16[32,8,784]{2,1,0:T(8,128)(2,1)}, bf16[32,8,288]{2,1,0:T(8,128)(2,1)}, f32[...) custom-call(bf16[784,128]{1,0:T(8,128)(2,1)S(1)} %get-tuple-element., ...), custom_call_target="tpu_custom_call" | custom-call | tf_op jit(solution)/shard_map/closing/pallas_call | solution.py:1512

commit v7 on v6

--- a/solution.py
+++ b/solution.py
@@ -377,8 +377,8 @@
 class Links:
     def __init__(self, send_sems, recv_sems):
         self.send_sems, self.recv_sems = send_sems, recv_sems
-        self.sends = self.slots = 0
-        self.open = []
+        self.sends = self.slots = self.started = 0
+        self.open, self.free = [], []
 
     def slot(self, count=1):
         first = self.slots
@@ -386,13 +386,27 @@
         return first
 
     def send(self, source, target, slot, where):
+        if not self.free:
+            self.free.append(self.sends)
+            self.sends += 1
+        index = self.free.pop(0)
         copy = pltpu.make_async_remote_copy(
-            source, target, self.send_sems.at[self.sends], self.recv_sems.at[slot],
+            source, target, self.send_sems.at[index], self.recv_sems.at[slot],
             device_id=where, device_id_type=MESH,
         )
-        self.sends += 1
         copy.start()
-        self.open.append(copy)
+        self.open.append((copy, index))
+        self.started += 1
+
+    def mark(self):
+        return self.started
+
+    def settle(self, last):
+        count = last - self.started + len(self.open)
+        for copy, index in self.open[:count]:
+            copy.wait_send()
+            self.free.append(index)
+        self.open = self.open[count:]
 
     def arrived(self, target, slot, where):
         pltpu.make_async_remote_copy(
@@ -401,8 +415,7 @@
         ).wait_recv()
 
     def drain(self):
-        for copy in self.open:
-            copy.wait_send()
+        self.settle(self.mark())
 
 
 def mm(a, b, ca, cb):
@@ -446,6 +459,16 @@
     return jnp.concatenate([value[:, a:b] for a, b in runs], axis=1)
 
 
+def fold(value):
+    half = value.shape[1] // 2
+    left = lax.broadcasted_iota(jnp.int32, (1, 1, LANES), 2) < LANES // 2
+    return jnp.where(left, value[:, :half], pltpu.roll(value[:, half:], LANES // 2, 2))
+
+
+def unfold(value):
+    return jnp.concatenate([value, pltpu.roll(value, LANES // 2, 2)], axis=1)
+
+
 def sigma(v):
     return 0.5 * jnp.tanh(0.5 * v) + 0.5
 
@@ -531,7 +554,7 @@
         return self.s2[self.hz, :, cols].astype(jnp.float32) + self.b3[:, cols].astype(jnp.float32)
 
 
-def make_fused(n_dp, in_local, images, sides, chan_in, chan_part, stop):
+def make_fused(n_dp, in_local, images, sides, chan_in, chan_part):
     f32, bf16 = jnp.float32, jnp.bfloat16
     halves = tuple(side // 2 for side in sides)
     sizes = tuple(h * h * n for h, n in zip(halves, images))
@@ -546,6 +569,7 @@
     chunks = [(g, r, starts[g] + r * widths[g], widths[g]) for g in range(2) for r in range(halves[g])]
     win = [-(-q // LANES) * LANES for q in qlanes]
     b_tile = qlanes[0] // LANES * LANES
+    n_sends, n_slots = 68, 198
     b_skip = qlanes[0] - b_tile
     rs = halves[0] // 2
     segments = [(1, 0, halves[1]), (0, 0, rs), (0, rs, halves[0])]
@@ -582,7 +606,9 @@
         for rows_, lanes_ in zip(row_parts, patch_win)
     ]
     low_lane = seg_lane[1] // LANES * LANES
-    out_lanes = [slice(cut_lane, slab_lanes), slice(0, low_lane), slice(low_lane, cut_lane)]
+    last_lane = slab_lanes - LANES
+    assert sum(qlanes) - last_lane <= LANES // 2
+    out_lanes = [slice(cut_lane, last_lane), slice(0, low_lane), slice(low_lane, cut_lane)]
     back_pieces = (((0, 0, 2),), ((0, 2, halves[0] - 1),), ((0, halves[0] - 1, halves[0]), (1, 0, halves[1])))
     row_halves = [
         slice(starts[p[0][0]] + p[0][1] * widths[p[0][0]], starts[p[-1][0]] + p[-1][2] * widths[p[-1][0]])
@@ -595,13 +621,13 @@
         (xa_h, xb_h, bxa_h, bxb_h, w1_h, w2_h, ws_h, g1_h, b1_h, g2_h, b2_h, gs_h, bs_h, ua_h, ub_h,
          pm0_h, pm1_h, cells_h,
          turn_h,
-         oa, ob, gr, gw1, gws, gw2, vecs, turn,
+         oa, ob, gr, grf, gw1, gws, gw2, vecs, turn,
          xa, xb, bxa, bxb, w1g, w2, wsg, vg, g2, b2, gs, bs, ua, ub, pm0, pm1, cells,
          xs, xt, xr, zb, zsq, zsr, zg, zpa, zpb, valid, vq, hat, mask, zs, a1a, a1b,
          cslots, slots, stat, up, outr, gv, dza, dzb, dzma, dzmb, apk, arx, gacc, dzsr,
          dd, hp, hr1, hs, hr2, gu, d1a, d1b,
          p22, p23, p24, p25, p26, wg1, p11, p12, p13, p14, p15,
-         sq, si, dq, di, gt, lsem, ssem, rsem) = refs
+         sq, si, dq, di, gt, gtf, lsem, ssem, rsem) = refs
         i, k = lax.axis_index("dp"), lax.axis_index("chan")
         k1 = k + 1 - 2 * (k % 2)
         k2 = (k + 2) % 4
@@ -825,10 +851,13 @@
             for where in (k2, k1):
                 net.send(zb.at[k, z_cuts[n]], zb.at[k, z_cuts[n]], slot_z[n] + k, (i, where))
 
-        def first_conv(c, taps, acc):
+        def conv_taps(taps, some):
+            weights = lanes_cat([w1g[q, some].reshape(-1, chan_part) for q in range(4)])
+            return mm(lanes_cat(taps[some]), weights, 1, 0)
+
+        def first_conv(c, value, acc):
             part = row_parts[c]
-            weights = lanes_cat([w1g[q].reshape(9 * chan_in, chan_part) for q in range(4)])
-            value = mm(lanes_cat(taps), weights, 1, 0).astype(bf16)
+            value = value.astype(bf16)
             zb[k, part, :] = value
             if c == 0:
                 z_send(0)
@@ -862,14 +891,17 @@
         center = [taps[4]]
         weights_on(3)
         weights_on(4)
-        weights_in((0, 1, 2, 5))
-        acc = first_conv(0, taps, acc)
+        weights_in((0, 1, 5))
+        value = conv_taps(taps, slice(0, 5)) + conv_taps(taps, slice(9 - n_via, 9))
+        weights_in((2,))
+        acc = first_conv(0, value + conv_taps(taps, slice(5, 9 - n_via)), acc)
         quarter_in(1)
         taps = patches(1)
         center.append(taps[4])
-        acc = first_conv(1, taps, acc)
+        acc = first_conv(1, conv_taps(taps, slice(0, 9)), acc)
         acc = [jnp.sum(v, axis=0, keepdims=True) for v in acc]
         first = chan_share(0, message(sum((by_chan(v) for v in acc), [])))
+        gone = net.mark()
         z_send(1)
         z_send(2)
         weights_in((3, 4))
@@ -892,7 +924,9 @@
         act_on(0)
         act_on(1)
         act_on(2)
+        net.settle(gone)
         side_first = chan_share(2, total(5, side_first))
+        gone = net.mark()
         for span, slot in zip(row_cuts, slot_g0):
             for where in (k2, k1):
                 net.send(zg.at[k, span], zg.at[k, span], slot + k, (i, where))
@@ -1003,11 +1037,11 @@
                     apk[0, span, cols] = jnp.where(left, v[2 * p], t[2 * p + 1]).astype(bf16)
                     apk[1, span, cols] = jnp.where(left, t[2 * p], v[2 * p + 1]).astype(bf16)
 
-        near = sizes[1] - sizes[1] // 6 // 16 * 16
-        far = sizes[0] * 17 // 32 // 16 * 16
+        near = sizes[1]
+        far = sizes[0] * 9 // 16 // 16 * 16
         pack_spans = [
             [slice(starts[1], starts[1] + near)],
-            [slice(starts[1] + near, rows), slice(0, far)],
+            [slice(0, far)],
             [slice(far, sizes[0])],
         ]
         slot_p = [[net.slot() for _ in spans_] for spans_ in pack_spans]
@@ -1098,6 +1132,8 @@
             v = h * gain1 + shift1
             sig = sigma(v)
             mask[span, :] = sig * (1.0 + v * (1.0 - sig)) * lanes_cat([valid[span, :]] * 4)
+        net.settle(gone)
+        gone = net.mark()
         tot = total(2, first)
         sum_tail, sum_gain2, sum_gains = tot[0:1], tot[1:2], tot[2:3]
         k2g, ksg = gain2 * sc2, gains * scs
@@ -1169,6 +1205,7 @@
 
         sum2 = Reduce(net, i, k, None, (None, p22, p23, p24, p25), cols2, p26)
         gacc[...] = mm(apk[ix], dd[...], 0, 0)
+        net.settle(gone)
         first = chan_share(1, total(3, first))
         def split_cells(read, target, c):
             for begin in range(row_parts[c].start, row_parts[c].stop, 16):
@@ -1229,6 +1266,7 @@
                 net.arrived(arx.at[span], slot, mate)
         for g in range(2):
             net.arrived(dz_inner(dzm, g), slot_d + g, mate)
+        gone = net.mark()
         for w, cols in enumerate(cols2):
             for piece in back_pieces:
                 columns(dzm, piece, range(cols.start // LANES, cols.stop // LANES))
@@ -1290,8 +1328,17 @@
             taps[4] = taps[4] + mm(side, lanes_cat([wsg[q] for q in range(4)]), 1, 1)
             return jnp.concatenate([tap.astype(bf16) for tap in taps], axis=0)
 
+        slot_f = net.slot(n_dp)
+
         def out_send(n, value):
             cols = out_lanes[n]
+            if n == 0:
+                last_tile = value[:, value.shape[1] - LANES :].reshape(n_dp, in_local, LANES)
+                gtf[...] = fold(last_tile).astype(bf16)
+                grf[i] = gtf[i]
+                for j in peers:
+                    net.send(gtf.at[j], grf.at[i], slot_f + i, (j, k))
+                value = value[:, : value.shape[1] - LANES]
             gt[:, :, cols] = value.astype(bf16).reshape(n_dp, in_local, value.shape[1])
             for j in peers:
                 net.send(gt.at[j, :, cols], gr.at[i, :, cols], slot_o[n] + i, (j, k))
@@ -1315,6 +1362,7 @@
         make_planes()
         weight_first(0)
         weight_first(1)
+        net.settle(gone)
         quarters_in(si, slice(0, q_rows), slot_q[2])
         late = back_taps(1)
         edge = cut_lane - patch_win[1].start
@@ -1341,10 +1389,13 @@
             if cols.start <= LANES < cols.stop:
                 gws[...] = value[:, LANES - cols.start : 2 * LANES - cols.start]
         vecs[...] = message([sum_gain1, sum_head, sum_gain2, sum_tail, sum_gains])
+        for j in peers:
+            net.arrived(grf.at[j], slot_f + j, (j, k))
         for c, cols in enumerate(out_lanes):
             for j in peers:
                 net.arrived(gr.at[j, :, cols], slot_o[c] + j, (j, k))
         net.drain()
+        assert net.sends <= n_sends and net.slots <= n_slots
 
     V = pltpu.VMEM
     pads = [(h + 2, h + 2, n, chan_part) for h, n in zip(halves, images)]
@@ -1411,15 +1462,17 @@
         V((4, q_rows, chan_part), bf16),
         V((4, q_rows, chan_part), bf16),
         V((4, q_rows, chan_part), bf16),
-        V((n_dp, in_local, slab_lanes), bf16),
+        V((n_dp, in_local, last_lane), bf16),
+        V((n_dp, in_local // 2, LANES), bf16),
         pltpu.SemaphoreType.DMA((20,)),
-        pltpu.SemaphoreType.DMA((192,)),
-        pltpu.SemaphoreType.DMA((192,)),
+        pltpu.SemaphoreType.DMA((n_sends,)),
+        pltpu.SemaphoreType.DMA((n_slots,)),
     ]
     mid_outs = [
         V((sizes[0], chan_part), bf16),
         V((sizes[1], chan_part), bf16),
-        V((n_dp, in_local, slab_lanes), bf16),
+        V((n_dp, in_local, last_lane), bf16),
+        V((n_dp, in_local // 2, LANES), bf16),
         V((9, in_local, LANES), f32),
         V((in_local, LANES), f32),
         V((9, out_rows, LANES), f32),
@@ -1440,8 +1493,8 @@
         name="block",
     )
 
-    def closing(oa, ob, gr, gw1, gws, gw2, vecs, turn,
-                fa, fb, ia, ib, f1, f2, fs, c1, h1, c2, h2, cs, hs, sems):
+    def closing(oa, ob, gr, grf, gw1, gws, gw2, vecs, turn,
+                fa, fb, ia, ib, f1, f2, fs, c1, h1, c2, h2, cs, hs, iav, ibv, sems):
         outs = [
             pltpu.make_async_copy(source, target, sems.at[index])
             for index, (source, target) in enumerate(
@@ -1450,11 +1503,19 @@
         ]
         for out in outs:
             out.start()
-        moved = mm(turn[...], gr[...].reshape(n_dp * in_local, slab_lanes), 1, 0)
-        natural = regroup(moved, back_runs)
-        ia[...] = natural[:, : qlanes[0]].reshape(in_local, n_dp, qlanes[0]).astype(bf16)
-        tail = natural[:, qlanes[0] : qlanes[0] + qlanes[1]]
-        ib[...] = tail.reshape(in_local, n_dp, qlanes[1]).astype(bf16)
+        tail = unfold(grf[...].astype(f32)).astype(bf16).reshape(n_dp * in_local, LANES)
+        moved = jnp.concatenate([gr[...].reshape(n_dp * in_local, last_lane), tail], axis=1)
+        n_half = in_local // 2
+        for h in range(2):
+            part = slice(h * n_half, (h + 1) * n_half)
+            natural = regroup(mm(turn[h * n_half * n_dp : (h + 1) * n_half * n_dp, :], moved, 1, 0), back_runs)
+            iav[part] = natural[:, : qlanes[0]].reshape(n_half, n_dp, qlanes[0]).astype(bf16)
+            tail = natural[:, qlanes[0] : qlanes[0] + qlanes[1]]
+            ibv[part] = tail.reshape(n_half, n_dp, qlanes[1]).astype(bf16)
+            for e, (source, target) in enumerate(((iav, ia), (ibv, ib))):
+                out = pltpu.make_async_copy(source.at[part], target.at[part], sems.at[5 + 2 * h + e])
+                out.start()
+                outs.append(out)
         for ref, row in ((c1, 0), (h1, 1), (c2, 2), (h2, 3), (cs, 4), (hs, 3)):
             ref[...] = vecs[row : row + 1, :]
         for out in outs:
@@ -1472,9 +1533,13 @@
             jax.ShapeDtypeStruct((in_local, LANES), f32),
         ]
         + [jax.ShapeDtypeStruct((1, LANES), f32)] * 6,
-        in_specs=[vmem] * 8,
-        out_specs=[hbm, hbm, vmem, vmem, hbm, hbm, hbm] + [vmem] * 6,
-        scratch_shapes=[pltpu.SemaphoreType.DMA((5,))],
+        in_specs=[vmem] * 9,
+        out_specs=[hbm] * 7 + [vmem] * 6,
+        scratch_shapes=[
+            V((in_local, n_dp, qlanes[0]), bf16),
+            V((in_local, n_dp, qlanes[1]), bf16),
+            pltpu.SemaphoreType.DMA((9,)),
+        ],
         compiler_params=pltpu.CompilerParams(vmem_limit_bytes=32 * 2**20),
         name="closing",
     )
@@ -1484,9 +1549,6 @@
         for j in range(n_dp):
             turn[c * n_dp + j, j * in_local + c] = 1.0
     return (main, last) + tuple(m.astype(jnp.bfloat16) for m in (*patch_ms, cells_m, turn))
-
-
-STOP = 99
 
 
 def fused_body(
@@ -1499,7 +1561,7 @@
     in_local = input_a.shape[0]
     main, last, *matrices = make_fused(
         n_dp, in_local, (boxes_a.shape[0], boxes_b.shape[0]), (SA, SB),
-        weight_first.shape[1], chan_part, STOP,
+        weight_first.shape[1], chan_part,
     )
     vectors = [
         v.reshape(1, chan_part)

time: 88.9 us -> 86.8 us (0.976)
  Pallas kernels: 87.9 us -> 85.8 us
    pallas_call x1, Pallas kernels: 85.8 us -> 83.8 us  [fused_body(): main(input_a, input_b, boxes_a.T, boxes_b.T, weight_first, weight_second,...]
where the time goes in v7:
time: 86.8 us; the launch traced here: 86.6 us
  Pallas kernels  85.8 us (99%)
    pallas_call x1, Pallas kernels, fused_body(): main(input_a, input_b, boxes_a.T, boxes_b.T, weight_first, weight_second,...  83.8 us
    pallas_call x1, Pallas kernels, fused_body(): res = last(*mid)  1.94 us

profile of v7, /device:TPU:0, one launch (start us, length us, event | category | flops | bytes accessed | tf_op | source)
XLA Modules:
  0.0 86.6 jit_solution(15464964996686466803)
XLA Ops:
  0.7 83.8 %block.1 = (bf16[784,128]{1,0:T(8,128)(2,1)S(1)}, bf16[288,128]{1,0:T(8,128)(2,1)S(1)}, bf16[8,32,1024]{2,1,0:T(8,128)(2,1)S(1)}, bf16[8,16,128]{2,1,0:T(8,128)(...) custom-call(bf16[32,25088]{1,0:T(8,128)(2,1)} %refs_0_.1, ...), custom_call_target="tpu_custom_call" | custom-call | tf_op jit(solution)/shard_map/block/pallas_call | solution.py:1570
  84.5 1.9 %closing.1 = (bf16[784,128]{1,0:T(8,128)(2,1)}, bf16[288,128]{1,0:T(8,128)(2,1)}, bf16[32,8,784]{2,1,0:T(8,128)(2,1)}, bf16[32,8,288]{2,1,0:T(8,128)(2,1)}, f32[...) custom-call(bf16[784,128]{1,0:T(8,128)(2,1)S(1)} %get-tuple-element., ...), custom_call_target="tpu_custom_call" | custom-call | tf_op jit(solution)/shard_map/closing/pallas_call | solution.py:1574

commit v8 on v7

--- a/solution.py
+++ b/solution.py
@@ -379,8 +379,15 @@
         self.send_sems, self.recv_sems = send_sems, recv_sems
         self.sends = self.slots = self.started = 0
         self.open, self.free = [], []
-
-    def slot(self, count=1):
+        self.spare, self.spare_dp = set(), set()
+
+    def slot(self, count=1, dp_only=False):
+        for spare in (self.spare_dp, self.spare) if dp_only else (self.spare,):
+            for first in sorted(spare):
+                run = set(range(first, first + count))
+                if run <= spare:
+                    spare -= run
+                    return first
         first = self.slots
         self.slots += count
         return first
@@ -484,7 +491,7 @@
             (i + 2 - 4 * self.pz, k),
             (i + 4 - 8 * self.hz, k),
         )
-        self.slots = [net.slot(3) for _ in windows]
+        self.slots = [net.slot(3, True) for _ in windows]
 
     def first(self, w):
         cols = self.windows[w]
@@ -518,7 +525,7 @@
         cols = self.windows[w]
         self.s1[:, :, :, cols] = value.reshape(2, 2, -1, value.shape[1])
         z = 2 * self.hz + self.pz
-        self.direct = self.net.slot(4)
+        self.direct = self.net.slot(4, True)
         for d in range(1, 4):
             to = (z + d) % 4
             self.net.send(
@@ -569,7 +576,7 @@
     chunks = [(g, r, starts[g] + r * widths[g], widths[g]) for g in range(2) for r in range(halves[g])]
     win = [-(-q // LANES) * LANES for q in qlanes]
     b_tile = qlanes[0] // LANES * LANES
-    n_sends, n_slots = 68, 198
+    n_sends, n_slots = 68, 107
     b_skip = qlanes[0] - b_tile
     rs = halves[0] // 2
     segments = [(1, 0, halves[1]), (0, 0, rs), (0, rs, halves[0])]
@@ -804,10 +811,13 @@
         def by_chan(value):
             return [value[:, q * LANES : (q + 1) * LANES] for q in range(4)]
 
+        used = []
+
         def share(rnd, value):
             mine = slots.at[rnd, i, : value.shape[0]]
             mine[...] = value
-            first = net.slot(n_dp)
+            first = net.slot(n_dp, True)
+            used.append((first, n_dp))
             for j in peers:
                 net.send(mine, mine, first + i, (j, k))
             return first
@@ -821,6 +831,7 @@
             mine = cslots.at[rnd, k, : value.shape[0]]
             mine[...] = value
             first = net.slot(4)
+            used.append((first, 4))
             for where in (k2, k3, k1):
                 net.send(mine, mine, first + k, (i, where))
             return first
@@ -1100,6 +1111,7 @@
                     zp[g][p, 1 + r, 1 : 1 + halves[g]] = value.astype(bf16)
 
         tot = total(1, first)
+        net.spare |= set(range(slot_x[0], slot_x[-1] + n_dp)) | set(range(slot_w[0], slot_w[-1] + 4))
         mean2, sc2 = moments(tot[0:1], tot[1:2])
         gain2, gains = g2[...], gs[...]
         shifts = b2[...] + bs[...]
@@ -1135,6 +1147,8 @@
         net.settle(gone)
         gone = net.mark()
         tot = total(2, first)
+        done = used[:-1] + [(begin, 4) for begin in slot_z] + [(slot_s, 4)]
+        net.spare_dp |= {begin + e for begin, count in done for e in range(count)}
         sum_tail, sum_gain2, sum_gains = tot[0:1], tot[1:2], tot[2:3]
         k2g, ksg = gain2 * sc2, gains * scs
         db, dg2, dgs = sum_tail * inv_pop, sum_gain2 * inv_pop, sum_gains * inv_pop
@@ -1315,7 +1329,7 @@
                 parts.append(lanes_cat(taps))
             return jnp.concatenate(parts, axis=0) if len(parts) > 1 else parts[0]
 
-        slot_o = [net.slot(n_dp) for _ in out_lanes]
+        slot_o = [net.slot(n_dp, True) for _ in out_lanes]
 
         def back_taps(c):
             part = row_parts[c]
@@ -1328,7 +1342,7 @@
             taps[4] = taps[4] + mm(side, lanes_cat([wsg[q] for q in range(4)]), 1, 1)
             return jnp.concatenate([tap.astype(bf16) for tap in taps], axis=0)
 
-        slot_f = net.slot(n_dp)
+        slot_f = net.slot(n_dp, True)
 
         def out_send(n, value):
             cols = out_lanes[n]

time: 86.8 us -> 86 us (level)
  no operation moved by 1% of the time
where the time goes in v8:
time: 86 us; the launch traced here: 85.8 us
  Pallas kernels  85 us (99%)
    pallas_call x1, Pallas kernels, fused_body(): main(input_a, input_b, boxes_a.T, boxes_b.T, weight_first, weight_second,...  83 us
    pallas_call x1, Pallas kernels, fused_body(): res = last(*mid)  1.95 us

profile of v8, /device:TPU:0, one launch (start us, length us, event | category | flops | bytes accessed | tf_op | source)
XLA Modules:
  0.0 85.8 jit_solution(7512250915102159198)
XLA Ops:
  0.7 83.0 %block.1 = (bf16[784,128]{1,0:T(8,128)(2,1)S(1)}, bf16[288,128]{1,0:T(8,128)(2,1)S(1)}, bf16[8,32,1024]{2,1,0:T(8,128)(2,1)S(1)}, bf16[8,16,128]{2,1,0:T(8,128)(...) custom-call(bf16[32,25088]{1,0:T(8,128)(2,1)} %refs_0_.1, ...), custom_call_target="tpu_custom_call" | custom-call | tf_op jit(solution)/shard_map/block/pallas_call | solution.py:1584
  83.7 1.9 %closing.1 = (bf16[784,128]{1,0:T(8,128)(2,1)}, bf16[288,128]{1,0:T(8,128)(2,1)}, bf16[32,8,784]{2,1,0:T(8,128)(2,1)}, bf16[32,8,288]{2,1,0:T(8,128)(2,1)}, f32[...) custom-call(bf16[784,128]{1,0:T(8,128)(2,1)S(1)} %get-tuple-element., ...), custom_call_target="tpu_custom_call" | custom-call | tf_op jit(solution)/shard_map/closing/pallas_call | solution.py:1588

commit v9 on v8

--- a/solution.py
+++ b/solution.py
@@ -576,7 +576,7 @@
     chunks = [(g, r, starts[g] + r * widths[g], widths[g]) for g in range(2) for r in range(halves[g])]
     win = [-(-q // LANES) * LANES for q in qlanes]
     b_tile = qlanes[0] // LANES * LANES
-    n_sends, n_slots = 68, 107
+    n_sends, n_slots = 55, 107
     b_skip = qlanes[0] - b_tile
     rs = halves[0] // 2
     segments = [(1, 0, halves[1]), (0, 0, rs), (0, rs, halves[0])]
@@ -929,13 +929,13 @@
         whole = jnp.concatenate([xr[q] for q in range(n_dp)], axis=0)
         for span in row_cuts:
             zg[k, span, :] = mm(cells[span, :], whole, 1, 1).astype(bf16)
+        net.settle(gone)
         first = share(0, chan_total(0, first))
         for where in (k2, k3, k1):
             net.send(zsq.at[where], zsr.at[k], slot_s + k, (i, where))
         act_on(0)
         act_on(1)
         act_on(2)
-        net.settle(gone)
         side_first = chan_share(2, total(5, side_first))
         gone = net.mark()
         for span, slot in zip(row_cuts, slot_g0):
@@ -1110,6 +1110,7 @@
                 for p, value in enumerate(planes_of(quarters, g)):
                     zp[g][p, 1 + r, 1 : 1 + halves[g]] = value.astype(bf16)
 
+        net.settle(gone)
         tot = total(1, first)
         net.spare |= set(range(slot_x[0], slot_x[-1] + n_dp)) | set(range(slot_w[0], slot_w[-1] + 4))
         mean2, sc2 = moments(tot[0:1], tot[1:2])

time: 86 us -> 85.8 us (level)
  no operation moved by 1% of the time
where the time goes in v9:
time: 85.8 us; the launch traced here: 85.6 us
  Pallas kernels  84.8 us (99%)
    pallas_call x1, Pallas kernels, fused_body(): main(input_a, input_b, boxes_a.T, boxes_b.T, weight_first, weight_second,...  82.9 us
    pallas_call x1, Pallas kernels, fused_body(): res = last(*mid)  1.95 us

profile of v9, /device:TPU:0, one launch (start us, length us, event | category | flops | bytes accessed | tf_op | source)
XLA Modules:
  0.0 85.6 jit_solution(2345057588678746969)
XLA Ops:
  0.7 82.9 %block.1 = (bf16[784,128]{1,0:T(8,128)(2,1)S(1)}, bf16[288,128]{1,0:T(8,128)(2,1)S(1)}, bf16[8,32,1024]{2,1,0:T(8,128)(2,1)S(1)}, bf16[8,16,128]{2,1,0:T(8,128)(...) custom-call(bf16[32,25088]{1,0:T(8,128)(2,1)} %refs_0_.1, ...), custom_call_target="tpu_custom_call" | custom-call | tf_op jit(solution)/shard_map/block/pallas_call | solution.py:1585
  83.5 1.9 %closing.1 = (bf16[784,128]{1,0:T(8,128)(2,1)}, bf16[288,128]{1,0:T(8,128)(2,1)}, bf16[32,8,784]{2,1,0:T(8,128)(2,1)}, bf16[32,8,288]{2,1,0:T(8,128)(2,1)}, f32[...) custom-call(bf16[784,128]{1,0:T(8,128)(2,1)S(1)} %get-tuple-element., ...), custom_call_target="tpu_custom_call" | custom-call | tf_op jit(solution)/shard_map/closing/pallas_call | solution.py:1589
